TPU v7x, 256 devices: a whole 4x4x8 slice. The times are simulated.
256 devices in a mesh: qrow: 16 (over x, y_hi, core), kcol: 16 (over y_lo, z).
Axes of the slice: x: 4, y: 4 (y_hi: 2, y_lo: 2; y = y_hi * 2 + y_lo), z: 8, core: 2. Of those that a mesh axis runs over, the one named last changes fastest.
Arguments:
- single: bfloat16 [2, 2048, 768], P(None, ('qrow', 'kcol'))
- restype: int32 [2048], P(('qrow', 'kcol')), may hold values from 0 to 31
- restype_table: bfloat16 [32, 768], replicated, may hold values from -6 to 6
- chain: int32 [2048], replicated, may hold values from 0 to 7, never falling along the last dimension, each value on 1 to 512 neighbouring positions
- live: int32 [2048], P('kcol'), may hold values from 0 to 1, as said below
- pair: bfloat16 [2048, 2048, 128], P('qrow', 'kcol')
- pair_gain: float32 [128], replicated, may hold values from 0.1 to 1.9
- pair_weight: float32 [128, 16], replicated
- chain_bias: float32 [16], replicated, may hold values from -4 to 4
- single_gain: float32 [768], replicated, may hold values from 0.1 to 1.9
- w_qkvg: bfloat16 [768, 3072], replicated
- w_out: bfloat16 [768, 768], replicated, may hold values from -0.875 to 0.875
Outputs:
- update: bfloat16 [2, 2048, 768], P(None, ('qrow', 'kcol'))
Inputs may be any that keep to these rules, and one draw needn't show every extreme that they name: Token 0 is always live and the last token is always padding; padding tokens may stand anywhere else. `chain`: chain numbers never fall along the tokens.
All inputs are finite; a program needn't handle non-finite values.
Results may differ from a plain program's by a relative error of at most 0.018.
Values may be sent and summed in bfloat16 or wider, within the bound.
No kernel may reach another device: no remote copies, remote signals or barrier semaphores. Data moves between devices by JAX's collectives and lax.ppermute only.
A program may use at most 64 MiB of HBM per device.

v0:
```python
import math

import jax
import jax.numpy as jnp
from jax import lax
from jax.sharding import PartitionSpec as P


def from_root(value, axis, source):
    kept = jnp.where(lax.axis_index(axis) == source, value, 0).astype(value.dtype)
    return lax.psum(kept, axis)


def joined(shard, axis, combine):
    everything = jax.tree.map(lambda part: lax.all_gather(part, axis), shard)
    first = jax.tree.map(lambda part: part[0], everything)

    def lap(k, so_far):
        return combine(so_far, jax.tree.map(lambda part: part[k], everything))

    return lax.fori_loop(1, lax.axis_size(axis), lap, first)


def layer_norm(inputs, scales):
    average = jnp.mean(inputs, -1, keepdims=True)
    centred = inputs - average
    variance = jnp.mean(centred * centred, -1, keepdims=True)
    return centred * lax.rsqrt(variance + 1e-05) * scales


def shards(
    single,
    restype,
    restype_table,
    chain,
    live,
    pair,
    pair_gain,
    pair_weight,
    chain_bias,
    single_gain,
    w_qkvg,
    w_out,
):
    samples, tok_rows, model_width = single.shape
    row_len, col_len, channels = pair.shape
    head_count = chain_bias.shape[0]
    head_width = model_width // head_count
    row_ratio = lax.axis_size("qrow") // lax.axis_size("kcol")
    row_index = lax.axis_index("qrow")
    col_index = lax.axis_index("kcol")
    one_hot = (
        restype[:, None] == jnp.arange(restype_table.shape[0], dtype=jnp.int32)[None, :]
    ).astype(jnp.bfloat16)
    embedded = (
        single.astype(jnp.float32)
        + jnp.dot(one_hot, restype_table, preferred_element_type=jnp.float32)[None]
    )
    normed = layer_norm(embedded, single_gain).astype(jnp.bfloat16)
    own_flat = normed.reshape(samples * tok_rows, model_width)
    gating = jax.nn.sigmoid(
        jnp.dot(own_flat, w_qkvg[:, 3 * model_width :], preferred_element_type=jnp.float32)
    )
    gating = gating.reshape(samples, tok_rows, model_width)
    own_proj = jnp.dot(own_flat, w_qkvg[:, : 3 * model_width], preferred_element_type=jnp.float32)
    own_proj = own_proj.astype(jnp.bfloat16).reshape(samples, tok_rows, 3 * model_width)
    row_proj = lax.all_gather(own_proj, "kcol", axis=1, tiled=True)
    queries = row_proj[..., :model_width]
    row_keyval = row_proj[..., model_width:]
    col_parts = from_root(row_keyval, "qrow", col_index * row_ratio + 0)
    pair_normed = layer_norm(pair.astype(jnp.float32), pair_gain)
    pair_bias = jnp.einsum("qkc,ch->hqk", pair_normed, pair_weight, precision=lax.Precision.HIGHEST)
    row_chain = lax.dynamic_slice_in_dim(chain, row_index * row_len, row_len, 0)
    col_chain = lax.dynamic_slice_in_dim(chain, col_index * col_len, col_len, 0)
    same_chain = (row_chain[:, None] == col_chain[None, :]).astype(jnp.float32)
    pair_bias = pair_bias + chain_bias[:, None, None] * same_chain[None]
    query_heads = queries.reshape(samples, row_len, head_count, head_width)
    key_rows = col_parts[..., :model_width].reshape(samples, col_len, head_count, head_width)
    value_rows = col_parts[..., model_width:].reshape(samples, col_len, head_count, head_width)
    scores = jnp.einsum(
        "sqhd,skhd->shqk", query_heads, key_rows, preferred_element_type=jnp.float32
    )
    scores = scores / math.sqrt(head_width) + pair_bias[None]
    live_mask = (live == 1)[None, None, None, :]
    scores = jnp.where(live_mask, scores, -1e30)
    local_top = jnp.max(scores, -1)
    weights = jnp.where(live_mask, jnp.exp(scores - local_top[..., None]), 0.0)
    denominator = jnp.transpose(jnp.sum(weights, -1), (0, 2, 1))
    numerator = jnp.einsum(
        "shqk,skhd->sqhd",
        weights.astype(jnp.bfloat16),
        value_rows,
        preferred_element_type=jnp.float32,
    )
    numerator = numerator.reshape(samples, row_len, model_width)
    top_rows = jnp.transpose(local_top, (0, 2, 1))

    def combine_partials(first, second):
        first_top, first_denom, first_numer = first
        second_top, second_denom, second_numer = second
        joint_top = jnp.maximum(first_top, second_top)
        first_factor = jnp.exp(first_top - joint_top)
        second_factor = jnp.exp(second_top - joint_top)
        shape_heads = first_numer.shape[:-1] + (first_factor.shape[-1], -1)
        joint_numer = (
            first_numer.reshape(shape_heads) * first_factor[..., None]
            + second_numer.reshape(shape_heads) * second_factor[..., None]
        )
        return (
            joint_top,
            first_denom * first_factor + second_denom * second_factor,
            joint_numer.reshape(first_numer.shape),
        )

    merged = joined((top_rows, denominator, numerator), "kcol", combine_partials)
    offset = col_index * tok_rows
    denom_own = lax.dynamic_slice_in_dim(merged[1], offset, tok_rows, 1)
    numer_own = lax.dynamic_slice_in_dim(merged[2], offset, tok_rows, 1)
    attended = numer_own.reshape(samples, tok_rows, head_count, head_width) / denom_own[..., None]
    attended = attended.reshape(samples, tok_rows, model_width)
    gated = (gating * attended).astype(jnp.bfloat16)
    update = jnp.dot(
        gated.reshape(samples * tok_rows, model_width), w_out, preferred_element_type=jnp.float32
    )
    return update.astype(jnp.bfloat16).reshape(samples, tok_rows, model_width)


def solution(mesh):
    return jax.shard_map(
        shards,
        mesh=mesh,
        in_specs=(
            P(None, ("qrow", "kcol"), None),
            P(("qrow", "kcol")),
            P(),
            P(),
            P("kcol"),
            P("qrow", "kcol", None),
            P(),
            P(),
            P(),
            P(),
            P(),
            P(),
        ),
        out_specs=P(None, ("qrow", "kcol"), None),
        check_vma=False,
    )
```

profile of v0, /device:TPU:40, one launch (start us, length us, event | category | flops | bytes accessed | tf_op | source)
XLA Modules:
  0.0 451.9 jit_solution(14128760981830205378)
XLA Ops:
  9.9 3.3 fusion.17
  14.1 3.5 convert_reduce_fusion
  17.6 4.8 %fusion.5 = f32[128,128]{1,0:T(8,128)S(1)} fusion(bf16[128,128,128]{2,1,0:T(8,128)(2,1)S(1)} %copy-done.1, f32[128,128]{1,0:T(8,128)S(1)} %broadcast_multiply_fusion), kind=kLoop, calls=%fused_computation.14 | loop fusion | flops 8372224 | bytes 4325376 | tf_op jit(solution)/shard_map/reduce_sum | solution.py:27
  22.5 61.4 %all-gather.5.cloned.1.call-done = bf16[2,128,2304]{2,1,0:T(8,128)(2,1)} async-done(((bf16[2,8,2304]{2,1,0:T(8,128)(2,1)}), bf16[2,128,2304]{2,1,0:T(8,128)(2,1)}) %all-gather.5.cloned.1.call-update) | async-done | bytes 1179664 | tf_op jit(solution)/shard_map/all_gather | solution.py:67
  83.8 2.1 slice_select_fusion
  86.1 12.5 %fusion.26 = f32[16,128,128]{2,0,1:T(8,128)} fusion(bf16[128,128,128]{2,1,0:T(8,128)(2,1)} %param.19, f32[128]{0:T(128)S(1)} %copy-done.8, f32[128,128]{1,0:T(8,128)S(1)} %add_rsqrt_fusion, f32[128,128]{1,0:T(8,128)S(1)} %broadcast_multiply_fusion, f32[128,128]{1,0:T(8,128)S(1)} %compare_convert_fusion, f32[16]{0:T(128)S(1)} %copy-done.9, ...), kind=kOutput, calls=%fused_computation.30 | convolution fusion | flops 411566080 | bytes 5448256 | tf_op jit(solution)/shard_map/qkc,ch->hqk/dot_general | solution.py:72
  98.6 1.6 copy.37
  100.5 129.6 %all-reduce.2.cloned.1.call-done = bf16[2,128,1536]{2,1,0:T(8,128)(2,1)} async-done(((bf16[2,128,1536]{2,1,0:T(8,128)(2,1)}), bf16[2,128,1536]{2,1,0:T(8,128)(2,1)}) %all-reduce.2.cloned.1.call-update) | async-done | bytes 786448 | tf_op jit(solution)/shard_map/psum | solution.py:11
  235.6 2.2 fusion.25
  237.8 36.7 %all-gather.1 = f32[32,128,16]{1,2,0:T(8,128)} all-gather(f32[2,128,16]{1,2,0:T(8,128)S(1)} %bitcast.83), channel_id=3, replica_groups=mesh['qrow'=16,'kcol'=16] {'kcol'}, dimensions={0}, use_global_device_ids=true | all-gather | bytes 278528 | tf_op jit(solution)/shard_map/all_gather | solution.py:15
  275.8 38.8 %all-gather = f32[32,128,16]{1,2,0:T(8,128)} all-gather(f32[2,128,16]{1,2,0:T(8,128)S(1)} %bitcast.82), channel_id=2, replica_groups=mesh['qrow'=16,'kcol'=16] {'kcol'}, dimensions={0}, use_global_device_ids=true | all-gather | bytes 278528 | tf_op jit(solution)/shard_map/all_gather | solution.py:15
  315.9 65.8 %all-gather.7.cloned.1.call-done = f32[16,2,128,768]{3,2,1,0:T(8,128)} async-done(((f32[1,2,128,768]{3,2,1,0:T(8,128)}), f32[16,2,128,768]{3,2,1,0:T(8,128)}) %all-gather.7.cloned.1.call-update) | async-done | bytes 12582928 | tf_op jit(solution)/shard_map/all_gather | solution.py:15
  383.2 58.2 %while.19 = (s32[]{:T(128)}, f32[2,128,16]{1,2,0:T(8,128)}, f32[2,128,16]{1,2,0:T(8,128)}, f32[2,128,768]{1,2,0:T(8,128)S(1)}, f32[16,2,128,16]{2,3,1,0:T(8,128)...) while((s32[]{:T(128)}, f32[2,128,16]{1,2,0:T(8,128)}, ...), condition=%wide.region_8.9_spmd, body=%wide.region_7.8_spmd.sunk | while | flops 614405 | bytes 5669007 | solution.py:21
  383.2 1.4 fusion.88
  387.1 1.4 fusion.88
  391.0 1.4 fusion.88
  394.9 1.4 fusion.88
  398.8 1.4 fusion.88
  402.7 1.4 fusion.88
  406.5 1.4 fusion.88
  410.4 1.4 fusion.88
  414.3 1.4 fusion.88
  422.1 1.4 fusion.88
  442.8 2.5 fusion.52
  (106 shorter events, 59.4 us)
Async XLA Ops:
  6.5 436.3 %copy-start = (bf16[768,768]{1,0:T(8,128)(2,1)S(1)}, bf16[768,768]{1,0:T(8,128)(2,1)}, u32[]{:S(2)}) copy-start(bf16[768,768]{1,0:T(8,128)(2,1)} %param.25) | copy-start | bytes 3538948
  6.5 77.3 %all-gather.5.cloned.1.call-start = ((), (), s32[]{:S(2)}) async-start(), calls=%async_computation | async-start | bytes 1253376 | tf_op jit(solution)/shard_map/all_gather | solution.py:67
  7.6 1.8 copy-start.3
  8.5 0.9 copy-start.5
  9.4 0.5 copy-start.6
  13.2 216.8 %all-reduce.2.cloned.1.call-start = ((), (), s32[]{:S(2)}) async-start(), calls=%async_computation.1 | async-start | bytes 1572864 | tf_op jit(solution)/shard_map/psum | solution.py:11
  14.1 3.5 copy-start.1
  22.4 63.7 %copy-start.7 = (f32[128,16]{0,1:T(8,128)S(1)}, f32[128,16]{0,1:T(8,128)}, u32[]{:S(2)}) copy-start(f32[128,16]{0,1:T(8,128)} %param.21) | copy-start | bytes 24580
  22.4 63.7 %copy-start.8 = (f32[128]{0:T(128)S(1)}, f32[128]{0:T(128)}, u32[]{:S(2)}) copy-start(f32[128]{0:T(128)} %param.20) | copy-start | bytes 1540
  22.4 63.7 %copy-start.9 = (f32[16]{0:T(128)S(1)}, f32[16]{0:T(128)}, u32[]{:S(2)}) copy-start(f32[16]{0:T(128)} %param.22) | copy-start | bytes 196
  85.9 295.8 %all-gather.7.cloned.1.call-start = ((), (), s32[]{:S(2)}) async-start(), calls=%async_computation.2 | async-start | bytes 13369344 | tf_op jit(solution)/shard_map/all_gather | solution.py:15
  98.6 1.6 copy-start.10
  98.6 1.7 slice-start
  232.4 1.0 copy-start.4
  233.1 1.3 copy-start.2
Sparse Core Ops, SparseCore 0:
  13.4 70.4 all-gather.4
  86.5 143.5 all-reduce.1
  235.7 145.9 all-gather.6
where the time goes:
time: 461 us; the launch traced here: 452 us
  waiting for transfers between devices  257 us (56%)
  blocking collectives  75.5 us (16%)
  other arithmetic  50.6 us (11%)
  local copies, waits for them, and re-layouts  34.2 us (7%)
  matrix products  20.9 us (5%)
  between operations  13.3 us (3%)
    psum x1, waiting for transfers between devices, from_root(): return lax.psum(kept, axis)  130 us
    all_gather x2, blocking collectives, joined(): everything = jax.tree.map(lambda part: lax.all_gather(part, axis), shard)  75.5 us
    all_gather x1, waiting for transfers between devices, joined(): everything = jax.tree.map(lambda part: lax.all_gather(part, axis), shard)  65.8 us
    all_gather x1, waiting for transfers between devices, shards(): row_proj = lax.all_gather(own_proj, 'kcol', axis=1, tiled=True)  61.4 us
    dynamic_slice x30, local copies, waits for them, and re-layouts, lap(): return combine(so_far, jax.tree.map(lambda part: part[k], everything))  21.6 us
    add x15, other arithmetic, combine_partials(): first_denom * first_factor + second_denom * second_factor  20.9 us
    add x15, other arithmetic, combine_partials(): first_numer.reshape(shape_heads) * first_factor[..., None]  15.2 us
    dot_general x1, matrix products, shards(): jnp.einsum('qkc,ch->hqk', pair_normed, pair_weight, precision=lax.Precisi...  12.5 us
  transfers between devices with their start and end apart: 3, of which 3 were waited for; matrix products, arithmetic and copies ran while one was open for 6% of the time, Pallas kernels for 0%

commit v1 on v0

v1 whole, which is shorter than its diff:
```python
import math

import jax
import jax.numpy as jnp
from jax import lax
from jax.experimental import pallas as pl
from jax.experimental.pallas import tpu as pltpu
from jax.sharding import PartitionSpec as P

BF = jnp.bfloat16
F32 = jnp.float32
EPS = 1e-05
STATS = 128


def vmem():
    return pl.BlockSpec(memory_space=pltpu.VMEM)


def smem():
    return pl.BlockSpec(memory_space=pltpu.SMEM)


def dot_nt(a, b):
    return lax.dot_general(a, b, (((1,), (1,)), ((), ())), preferred_element_type=F32)


def layer_norm(x):
    centred = x - jnp.mean(x, -1, keepdims=True)
    variance = jnp.mean(centred * centred, -1, keepdims=True)
    return centred * lax.rsqrt(variance + EPS)


def split3(x):
    hi = x.astype(BF)
    rest = x - hi.astype(F32)
    mid = rest.astype(BF)
    low = (rest - mid.astype(F32)).astype(BF)
    return hi, mid, low


def norm_kernel(restype_ref, single_ref, table_ref, gain_ref, normed_ref, copies_ref):
    samples, tok, width = single_ref.shape
    kinds = table_ref.shape[0]
    row = lax.broadcasted_iota(jnp.int32, (tok, kinds), 0)
    col = lax.broadcasted_iota(jnp.int32, (tok, kinds), 1)
    kind = jnp.zeros((tok, kinds), jnp.int32)
    for t in range(tok):
        kind = jnp.where(row == t, restype_ref[t], kind)
    one_hot = jnp.where(kind == col, 1.0, 0.0).astype(BF)
    emb = jnp.dot(one_hot, table_ref[...], preferred_element_type=F32)
    x = single_ref[...].astype(F32) + emb[None]
    normed = (layer_norm(x) * gain_ref[...][None]).reshape(samples * tok, width).astype(BF)
    normed_ref[...] = normed
    for j in range(copies_ref.shape[0]):
        copies_ref[j] = normed


def bias_kernel(
    where_ref, chain_ref, cbias_ref, chain_rows_ref, live_ref, gain_ref, weight_ref, pair_ref, out_ref, lhs_ref, cb_ref
):
    heads, channels = weight_ref.shape
    block, keys, _ = pair_ref.shape
    step = pl.program_id(0)

    @pl.when(step == 0)
    def _():
        hi, mid, low = split3(weight_ref[...] * gain_ref[...])
        lhs_ref[...] = jnp.concatenate(
            [
                jnp.concatenate([hi, hi], 1),
                jnp.concatenate([mid, mid], 1),
                jnp.concatenate([low, jnp.zeros_like(low)], 1),
            ],
            0,
        )
        row = lax.broadcasted_iota(jnp.int32, (heads, keys), 0)
        column = jnp.zeros((heads, keys), F32)
        for h in range(heads):
            column = jnp.where(row == h, cbias_ref[h], column)
        cb_ref[...] = column

    first = where_ref[0] * (block * pl.num_programs(0)) + step * block
    col_chain = chain_rows_ref[pl.ds(where_ref[1], 1), :]
    alive = live_ref[...] == 1
    lhs = lhs_ref[...]
    column = cb_ref[...]
    for q in range(0, block, 2):
        x = pair_ref[q : q + 2].astype(F32).reshape(2 * keys, channels)
        z = layer_norm(x)
        hi = z.astype(BF)
        low = (z - hi.astype(F32)).astype(BF)
        res = dot_nt(lhs, jnp.concatenate([hi, low], 1))
        res = res[:heads] + res[heads : 2 * heads] + res[2 * heads :]
        for i in range(2):
            part = res[:, i * keys : (i + 1) * keys]
            same = col_chain == chain_ref[first + q + i]
            part = part + jnp.where(same, column, 0.0)
            out_ref[:, q + i, :] = jnp.where(alive, part, -1e30)


def query_kernel(rows_ref, own_ref, wq_ref, wg_ref, q_ref, gate_ref):
    parts, per, width = rows_ref.shape
    half = per // 2
    x = rows_ref[...].reshape(parts * per, width)
    proj = jnp.dot(x, wq_ref[...], preferred_element_type=F32)
    proj = proj.reshape(parts, 2, half, width)
    for s in range(2):
        q_ref[s] = proj[:, s].reshape(parts * half, width).astype(BF)
    pre = jnp.dot(own_ref[...], wg_ref[...], preferred_element_type=F32)
    gate_ref[...] = jax.nn.sigmoid(pre)


def attend_kernel(rows_ref, wk_ref, wv_ref, q_ref, bias_ref, out_ref, acc_ref):
    parts, per, width = rows_ref.shape
    half = per // 2
    heads, queries, keys = bias_ref.shape
    size = width // heads
    scale = 1.0 / math.sqrt(size)
    x = rows_ref[...].reshape(parts * per, width)
    kf = jnp.dot(x, wk_ref[...], preferred_element_type=F32).reshape(parts, 2, half, width)
    vf = jnp.dot(x, wv_ref[...], preferred_element_type=F32).reshape(parts, 2, half, width)
    lane = lax.broadcasted_iota(jnp.int32, (queries, STATS), 1)
    for s in range(2):
        k = kf[:, s].reshape(keys, width).astype(BF)
        v = vf[:, s].reshape(keys, width).astype(BF)
        q = q_ref[s]
        sums = [jnp.zeros((queries, 128), F32) for _ in range(width // 128)]
        tops = jnp.zeros((queries, STATS), F32)
        tots = jnp.zeros((queries, STATS), F32)
        for h in range(heads):
            a, b = h * size // 128, -(-(h + 1) * size // 128)
            spot = lax.broadcasted_iota(jnp.int32, (1, (b - a) * 128), 1) + a * 128
            mask = jnp.where((spot >= h * size) & (spot < (h + 1) * size), 1.0, 0.0).astype(BF)
            cut = slice(a * 128, b * 128)
            sc = dot_nt(q[:, cut] * mask, k[:, cut]) * scale + bias_ref[h]
            top = jnp.max(sc, -1, keepdims=True)
            w = jnp.exp(sc - top)
            tot = jnp.sum(w, -1, keepdims=True)
            o = jnp.dot(w.astype(BF), v[:, cut] * mask, preferred_element_type=F32)
            for i in range(b - a):
                sums[a + i] = sums[a + i] + o[:, i * 128 : (i + 1) * 128]
            tops = jnp.where(lane == h, top, tops)
            tots = jnp.where(lane == h, tot, tots)
        hi, mid, low = split3(tops)
        thi, tmid, _ = split3(tots)
        stats = hi.astype(F32)
        for i, p in enumerate((mid, low, thi, tmid)):
            stats = stats + pltpu.roll(p.astype(F32), heads * (i + 1), 1)
        for i, p in enumerate(sums + [stats]):
            acc_ref[:, s * half : (s + 1) * half, i * 128 : (i + 1) * 128] = p.reshape(parts, half, 128)
    out_ref[...] = acc_ref[...].astype(BF)


def merge_kernel(parts_ref, gate_ref, wout_ref, out_ref):
    parts, per, wide = parts_ref.shape
    width = wide - STATS
    heads = 16
    size = width // heads
    st = parts_ref[:, :, width:].astype(F32).reshape(parts * per, STATS)
    top = st + pltpu.roll(st, STATS - heads, 1) + pltpu.roll(st, STATS - 2 * heads, 1)
    tot = pltpu.roll(st, STATS - 3 * heads, 1) + pltpu.roll(st, STATS - 4 * heads, 1)
    lane = lax.broadcasted_iota(jnp.int32, (parts * per, STATS), 1)
    top = jnp.where(lane < heads, top, 0.0).reshape(parts, per, STATS)
    tot = jnp.where(lane < heads, tot, 1.0).reshape(parts, per, STATS)
    e = jnp.exp(top - jnp.max(top, 0, keepdims=True))
    f = e / jnp.sum(e * tot, 0, keepdims=True)
    f = jnp.where(lane < heads, f.reshape(parts * per, STATS), 0.0)
    hrow = lax.broadcasted_iota(jnp.int32, (STATS, width), 0) * size
    col = lax.broadcasted_iota(jnp.int32, (STATS, width), 1)
    spread = jnp.where((col >= hrow) & (col < hrow + size), 1.0, 0.0).astype(BF)
    hi = f.astype(BF)
    low = (f - hi.astype(F32)).astype(BF)
    factor = jnp.dot(jnp.concatenate([hi, low], 1), jnp.concatenate([spread, spread], 0), preferred_element_type=F32)
    num = parts_ref[:, :, :width].astype(F32)
    attended = jnp.sum(num * factor.reshape(parts, per, width), 0)
    gated = (gate_ref[...] * attended).astype(BF)
    update = jnp.dot(gated, wout_ref[...], preferred_element_type=F32)
    out_ref[...] = update.reshape(out_ref.shape).astype(BF)


def params(mib):
    return pltpu.CompilerParams(vmem_limit_bytes=mib << 20)


def shards(
    single,
    restype,
    restype_table,
    chain,
    live,
    pair,
    pair_gain,
    pair_weight,
    chain_bias,
    single_gain,
    w_qkvg,
    w_out,
):
    samples, tok, width = single.shape
    row_len, col_len, channels = pair.shape
    heads = chain_bias.shape[0]
    n_row, n_col = lax.axis_size("qrow"), lax.axis_size("kcol")
    shape = jax.ShapeDtypeStruct
    own = samples * tok

    normed, copies = pl.pallas_call(
        norm_kernel,
        name="norm",
        out_shape=(shape((own, width), BF), shape((n_col, own, width), BF)),
        in_specs=[smem(), vmem(), vmem(), vmem()],
        out_specs=(vmem(), vmem()),
        compiler_params=params(16),
    )(restype, single, restype_table, single_gain.reshape(1, width))

    swap = [(r * n_col + c, c * n_col + r) for r in range(n_row) for c in range(n_col)]
    turned = lax.ppermute(normed, ("qrow", "kcol"), swap)
    row_tokens = lax.all_to_all(copies, "kcol", 0, 0)
    col_tokens = lax.all_to_all(jnp.broadcast_to(turned[None], (n_row, own, width)), "qrow", 0, 0)

    block = 16
    where = jnp.stack([lax.axis_index("qrow"), lax.axis_index("kcol")]).astype(jnp.int32)
    whole = lambda *dims: pl.BlockSpec(dims, lambda i: (0,) * len(dims))
    bias = pl.pallas_call(
        bias_kernel,
        name="bias",
        grid=(row_len // block,),
        out_shape=shape((heads, row_len, col_len), F32),
        in_specs=[
            smem(),
            smem(),
            smem(),
            whole(chain.shape[0] // col_len, col_len),
            whole(1, col_len),
            whole(1, channels),
            whole(heads, channels),
            pl.BlockSpec((block, col_len, channels), lambda i: (i, 0, 0)),
        ],
        out_specs=pl.BlockSpec((heads, block, col_len), lambda i: (0, i, 0)),
        scratch_shapes=[pltpu.VMEM((3 * heads, 2 * channels), BF), pltpu.VMEM((heads, col_len), F32)],
        compiler_params=params(16),
        cost_estimate=pl.CostEstimate(flops=10**9, bytes_accessed=40 * 10**6, transcendentals=0),
    )(
        where,
        chain,
        chain_bias,
        chain.reshape(-1, col_len),
        live.reshape(1, col_len),
        pair_gain.reshape(1, channels),
        pair_weight.T,
        pair,
    )

    cols = lambda i: pl.BlockSpec((width, width), lambda step: (0, i))
    queries, gate = pl.pallas_call(
        query_kernel,
        name="query",
        grid=(1,),
        out_shape=(shape((samples, row_len, width), BF), shape((own, width), F32)),
        in_specs=[vmem(), vmem(), cols(0), cols(3)],
        out_specs=(vmem(), vmem()),
        compiler_params=params(24),
    )(row_tokens, normed, w_qkvg, w_qkvg)

    partial = pl.pallas_call(
        attend_kernel,
        name="attend",
        grid=(1,),
        out_shape=shape((n_col, own, width + STATS), BF),
        in_specs=[vmem(), cols(1), cols(2), vmem(), vmem()],
        out_specs=vmem(),
        scratch_shapes=[pltpu.VMEM((n_col, own, width + STATS), F32)],
        compiler_params=params(32),
    )(col_tokens, w_qkvg, w_qkvg, queries, bias)

    gathered = lax.all_to_all(partial, "kcol", 0, 0)
    return pl.pallas_call(
        merge_kernel,
        name="merge",
        out_shape=shape((samples, tok, width), BF),
        in_specs=[vmem(), vmem(), vmem()],
        out_specs=vmem(),
        compiler_params=params(24),
    )(gathered, gate, w_out)


def solution(mesh):
    return jax.shard_map(
        shards,
        mesh=mesh,
        in_specs=(
            P(None, ("qrow", "kcol"), None),
            P(("qrow", "kcol")),
            P(),
            P(),
            P("kcol"),
            P("qrow", "kcol", None),
            P(),
            P(),
            P(),
            P(),
            P(),
            P(),
        ),
        out_specs=P(None, ("qrow", "kcol"), None),
        check_vma=False,
    )
```

time: 461 us -> 79.7 us (0.17); the launches traced: 452 us -> 78.2 us
  waiting for transfers between devices: 257 us -> 9.86 us
  blocking collectives: 75.5 us -> 20.3 us
  other arithmetic: 50.6 us -> 0.08 us
  local copies, waits for them, and re-layouts: 34.2 us -> 12 us
  matrix products: 20.9 us -> 0 us
  starting transfers between devices: 0.09 us -> 19.8 us
  Pallas kernels: 0 us -> 16.2 us
  between operations: 13.3 us -> 0.08 us
    psum x1 -> x0, waiting for transfers between devices: 130 us -> none  [from_root(): return lax.psum(kept, axis)]
    all_gather x2 -> x0, waiting for transfers between devices: 127 us -> none  [the longest x1 65.8 us: joined(): everything = jax.tree.map(lambda part: lax.all_gather(part, axis), shard)]
    all_gather x2 -> x0, blocking collectives: 75.5 us -> none  [joined(): everything = jax.tree.map(lambda part: lax.all_gather(part, axis), shard)]
    add x30 -> x0, other arithmetic: 36.1 us -> none  [the longest x15 20.9 us: combine_partials(): first_denom * first_factor + second_denom * second_factor]
    dynamic_slice x33 -> x0, local copies, waits for them, and re-layouts: 23.3 us -> none  [the longest x30 21.6 us: lap(): return combine(so_far, jax.tree.map(lambda part: part[k], everything))]
    dot_general x6 -> x0, matrix products: 20.9 us -> none  [the longest x1 12.5 us: shards(): jnp.einsum('qkc,ch->hqk', pair_normed, pair_weight, precision=lax.Precisi...]
    all_to_all x0 -> x1, blocking collectives: none -> 20.3 us  [shards(): gathered = lax.all_to_all(partial, 'kcol', 0, 0)]
    pallas_call x0 -> x5, Pallas kernels: none -> 16.2 us  [the longest x1 8.22 us: shards(): pl.pallas_call(bias_kernel, name='bias', grid=(row_len // block,), out_sh...]
  transfers between devices with their start and end apart: 3 -> 3, of which waited for: 3 -> 2; matrix products, arithmetic and copies ran while one was open for 6% -> 0% of each run, Pallas kernels for 0% -> 11%
where the time goes in v1:
time: 79.7 us; the launch traced here: 78.2 us
  blocking collectives  20.3 us (25%)
  starting transfers between devices  19.8 us (25%)
  Pallas kernels  16.2 us (20%)
  local copies, waits for them, and re-layouts  12 us (15%)
  waiting for transfers between devices  9.86 us (12%)
    all_to_all x1, blocking collectives, shards(): gathered = lax.all_to_all(partial, 'kcol', 0, 0)  20.3 us
    unnamed x24, local copies, waits for them, and re-layouts  10.5 us
    all_to_all x1, starting transfers between devices, shards(): row_tokens = lax.all_to_all(copies, 'kcol', 0, 0)  9.49 us
    pallas_call x1, Pallas kernels, shards(): pl.pallas_call(bias_kernel, name='bias', grid=(row_len // block,), out_sh...  8.22 us
    all_to_all x1, starting transfers between devices, shards(): lax.all_to_all(jnp.broadcast_to(turned[None], (n_row, own, width)), 'qrow...  6.66 us
    ppermute x1, waiting for transfers between devices, shards(): turned = lax.ppermute(normed, ('qrow', 'kcol'), swap)  5.66 us
    pallas_call x1, Pallas kernels, shards(): pl.pallas_call(attend_kernel, name='attend', grid=(1,), out_shape=shape((...  4.41 us
    all_to_all x1, waiting for transfers between devices, shards(): row_tokens = lax.all_to_all(copies, 'kcol', 0, 0)  4.19 us
  transfers between devices with their start and end apart: 3, of which 2 were waited for; matrix products, arithmetic and copies ran while one was open for 0% of the time, Pallas kernels for 11%

profile of v1, /device:TPU:40, one launch (start us, length us, event | category | flops | bytes accessed | tf_op | source)
XLA Modules:
  0.0 78.2 jit_solution(12530618192739656148)
XLA Ops:
  0.0 0.7 reshape.13.gain_ref
  0.7 0.8 %copy-done.4 = bf16[32,768]{1,0:T(8,128)(2,1)S(1)} copy-done((bf16[32,768]{1,0:T(8,128)(2,1)S(1)}, bf16[32,768]{1,0:T(8,128)(2,1)}, u32[]{:S(2)}) %copy-start.4) | copy-done | bytes 49176
  1.5 0.7 copy-done.6
  2.2 0.7 copy-done.8
  2.9 1.6 %norm.1 = (bf16[16,768]{1,0:T(8,128)(2,1)S(1)}, bf16[16,16,768]{2,1,0:T(8,128)(2,1)}) custom-call(s32[8]{0:T(128)S(1)} %copy-done.8, bf16[2,8,768]{2,1,0:T(8,128)(2,1)S(1)} %copy-done.6, bf16[32,768]{1,0:T(8,128)(2,1)S(1)} %copy-done.4, f32[1,768]{1,0:T(1,128)S(1)} %reshape.13.gain_ref), custom_call_target="tpu_custom_call" | custom-call | tf_op jit(solution)/shard_map/norm/pallas_call | solution.py:207
  4.5 9.5 %all-to-all-start.1 = ((bf16[16,16,768]{2,1,0:T(8,128)(2,1)}), bf16[16,16,768]{2,1,0:T(8,128)(2,1)S(1)}, u32[]{:S(2)}, u32[]{:S(2)}) async-start(bf16[16,16,768]{2,1,0:T(8,128)(2,1)} %get-tuple-element.10), calls=%async_computation.1 | async-start | bytes 786432 | tf_op jit(solution)/shard_map/all_to_all | solution.py:218
  14.0 3.6 %collective-permute-start = (bf16[16,768]{1,0:T(8,128)(2,1)S(1)}, bf16[16,768]{1,0:T(8,128)(2,1)S(1)}, u32[]{:S(2)}, u32[]{:S(2)}) collective-permute-start(bf16[16,768]{1,0:T(8,128)(2,1)S(1)} %get-tuple-element.9.own_ref), channel_id=1, source_target_pairs={{0,0},{1,16},{2,32},{3,48},{4,64},{5,80},{6,96},{7,112},{8,128},{9... | collective-permute-start | bytes 73736 | tf_op jit(solution)/shard_map/ppermute | solution.py:217
  17.6 5.7 %collective-permute-done = bf16[16,768]{1,0:T(8,128)(2,1)S(1)} collective-permute-done((bf16[16,768]{1,0:T(8,128)(2,1)S(1)}, bf16[16,768]{1,0:T(8,128)(2,1)S(1)}, u32[]{:S(2)}, u32[]{:S(2)}) %collective-permute-start) | collective-permute-done | bytes 24608 | tf_op jit(solution)/shard_map/ppermute | solution.py:217
  23.3 4.2 %all-to-all-done.1.rows_ref = bf16[16,16,768]{2,1,0:T(8,128)(2,1)S(1)} async-done(((bf16[16,16,768]{2,1,0:T(8,128)(2,1)}), bf16[16,16,768]{2,1,0:T(8,128)(2,1)S(1)}, u32[]{:S(2)}, u32[]{:S(2)}) %all-to-all-start.1) | async-done | bytes 393248 | tf_op jit(solution)/shard_map/all_to_all | solution.py:218
  27.5 0.8 broadcast_in_dim.2
  28.3 6.7 %all-to-all-start = ((bf16[16,16,768]{2,1,0:T(8,128)(2,1)}), bf16[16,16,768]{2,1,0:T(8,128)(2,1)S(1)}, u32[]{:S(2)}, u32[]{:S(2)}) async-start(bf16[16,16,768]{2,1,0:T(8,128)(2,1)} %broadcast_in_dim.2), calls=%async_computation | async-start | bytes 786432 | tf_op jit(solution)/shard_map/all_to_all | solution.py:219
  34.9 0.1 pad_add_fusion.where_ref
  35.0 2.3 %copy-done.2 = bf16[128,128,128]{2,1,0:T(8,128)(2,1)S(1)} copy-done((bf16[128,128,128]{2,1,0:T(8,128)(2,1)S(1)}, bf16[128,128,128]{2,1,0:T(8,128)(2,1)}, u32[]{:S(2)}) %copy-start.2) | copy-done | bytes 4194328
  37.4 1.0 %copy-done.5 = s32[2048]{0:T(1024)S(1)} copy-done((s32[2048]{0:T(1024)S(1)}, s32[2048]{0:T(1024)}, u32[]{:S(2)}) %copy-start.5) | copy-done | bytes 8216
  38.3 0.7 copy-done.7
  39.0 0.7 copy-done.9
  39.7 0.7 copy-done.10
  40.3 0.7 copy-done.11
  41.0 8.2 %bias.1.bias_ref = f32[16,128,128]{2,1,0:T(8,128)S(1)} custom-call(s32[2]{0:T(128)S(1)} %pad_add_fusion.where_ref, s32[2048]{0:T(1024)S(1)} %copy-done.5, f32[16]{0:T(128)S(1)} %copy-done.9, s32[16,128]{1,0:T(8,128)S(1)} %bitcast.6, s32[1,128]{1,0:T(1,128)S(1)} %bitcast.8, f32[1,128]{1,0:T(1,128)S(1)} %bitcast.9, f32[16,128]{1,0:T(8,128)S(1)} %bitcast.7, ...), custom_call_target="tpu_custom_call" | custom-call | flops 1000000000 | bytes 40000000 | tf_op jit(solution)/shard_map/bias/pallas_call | solution.py:224
  49.2 0.6 query.1
  49.9 2.3 %copy-done.1 = bf16[768,3072]{1,0:T(8,128)(2,1)S(1)} copy-done((bf16[768,3072]{1,0:T(8,128)(2,1)S(1)}, bf16[768,3072]{1,0:T(8,128)(2,1)}, u32[]{:S(2)}) %copy-start.1) | copy-done | bytes 4718616
  52.2 4.4 %attend.1 = bf16[16,16,896]{2,1,0:T(8,128)(2,1)S(1)} custom-call(bf16[16,16,768]{2,1,0:T(8,128)(2,1)S(1)} %all-to-all-done.rows_ref, bf16[768,3072]{1,0:T(8,128)(2,1)S(1)} %copy-done.1, bf16[768,3072]{1,0:T(8,128)(2,1)S(1)} %copy-done.1, bf16[2,128,768]{2,1,0:T(8,128)(2,1)S(1)} %get-tuple-element.11.q_ref, f32[16,128,128]{2,1,0:T(8,128)S(1)} %bias.1.bias_ref), custom_call_target="tpu_custom_call" | custom-call | tf_op jit(solution)/shard_map/attend/pallas_call | solution.py:265
  56.6 20.3 %all_to_all.15.parts_ref = bf16[16,16,896]{2,1,0:T(8,128)(2,1)S(1)} all-to-all(bf16[16,16,896]{2,1,0:T(8,128)(2,1)S(1)} %attend.1), channel_id=1, replica_groups=mesh['qrow'=16,'kcol'=16] {'kcol'}, dimensions={0} | all-to-all | bytes 917504 | tf_op jit(solution)/shard_map/all_to_all | solution.py:276
  76.9 1.3 %merge.1 = bf16[2,8,768]{2,1,0:T(8,128)(2,1)} custom-call(bf16[16,16,896]{2,1,0:T(8,128)(2,1)S(1)} %all_to_all.15.parts_ref, f32[16,768]{1,0:T(8,128)S(1)} %get-tuple-element.12.gate_ref, bf16[768,768]{1,0:T(8,128)(2,1)S(1)} %copy-done.3), custom_call_target="tpu_custom_call" | custom-call | tf_op jit(solution)/shard_map/merge/pallas_call | solution.py:277
  (15 shorter events, 0.0 us)
Async XLA Ops:
  0.7 0.8 %copy-start.4 = (bf16[32,768]{1,0:T(8,128)(2,1)S(1)}, bf16[32,768]{1,0:T(8,128)(2,1)}, u32[]{:S(2)}) copy-start(bf16[32,768]{1,0:T(8,128)(2,1)} %table_ref.1) | copy-start | bytes 147460
  1.5 0.7 copy-start.6
  2.2 0.7 copy-start.8
  4.5 23.0 %all-to-all-start.1 = ((bf16[16,16,768]{2,1,0:T(8,128)(2,1)}), bf16[16,16,768]{2,1,0:T(8,128)(2,1)S(1)}, u32[]{:S(2)}, u32[]{:S(2)}) async-start(bf16[16,16,768]{2,1,0:T(8,128)(2,1)} %get-tuple-element.10), calls=%async_computation.1 | async-start | bytes 786432 | tf_op jit(solution)/shard_map/all_to_all | solution.py:218
  14.0 9.3 %collective-permute-start = (bf16[16,768]{1,0:T(8,128)(2,1)S(1)}, bf16[16,768]{1,0:T(8,128)(2,1)S(1)}, u32[]{:S(2)}, u32[]{:S(2)}) collective-permute-start(bf16[16,768]{1,0:T(8,128)(2,1)S(1)} %get-tuple-element.9.own_ref), channel_id=1, source_target_pairs={{0,0},{1,16},{2,32},{3,48},{4,64},{5,80},{6,96},{7,112},{8,128},{9... | collective-permute-start | bytes 73736 | tf_op jit(solution)/shard_map/ppermute | solution.py:217
  28.3 21.6 %all-to-all-start = ((bf16[16,16,768]{2,1,0:T(8,128)(2,1)}), bf16[16,16,768]{2,1,0:T(8,128)(2,1)S(1)}, u32[]{:S(2)}, u32[]{:S(2)}) async-start(bf16[16,16,768]{2,1,0:T(8,128)(2,1)} %broadcast_in_dim.2), calls=%async_computation | async-start | bytes 786432 | tf_op jit(solution)/shard_map/all_to_all | solution.py:219
  34.9 14.3 %copy-start = (bf16[768,3072]{1,0:T(8,128)(2,1)S(1)}, bf16[768,3072]{1,0:T(8,128)(2,1)}, u32[]{:S(2)}) copy-start(bf16[768,3072]{1,0:T(8,128)(2,1)} %wv_ref.1) | copy-start | bytes 14155780
  35.0 2.3 %copy-start.2 = (bf16[128,128,128]{2,1,0:T(8,128)(2,1)S(1)}, bf16[128,128,128]{2,1,0:T(8,128)(2,1)}, u32[]{:S(2)}) copy-start(bf16[128,128,128]{2,1,0:T(8,128)(2,1)} %pair_ref.1) | copy-start | bytes 12582916
  37.4 1.0 %copy-start.5 = (s32[2048]{0:T(1024)S(1)}, s32[2048]{0:T(1024)}, u32[]{:S(2)}) copy-start(s32[2048]{0:T(1024)} %chain_ref.1) | copy-start | bytes 24580
  38.3 0.7 copy-start.7
  39.0 0.7 copy-start.9
  39.7 0.7 copy-start.10
  40.3 0.7 copy-start.11
  49.9 2.3 %copy-start.1 = (bf16[768,3072]{1,0:T(8,128)(2,1)S(1)}, bf16[768,3072]{1,0:T(8,128)(2,1)}, u32[]{:S(2)}) copy-start(bf16[768,3072]{1,0:T(8,128)(2,1)} %wv_ref.1) | copy-start | bytes 14155780
  52.2 24.7 %copy-start.3 = (bf16[768,768]{1,0:T(8,128)(2,1)S(1)}, bf16[768,768]{1,0:T(8,128)(2,1)}, u32[]{:S(2)}) copy-start(bf16[768,768]{1,0:T(8,128)(2,1)} %wout_ref.1) | copy-start | bytes 3538948

commit v2 on v1

v2 whole, which is shorter than its diff:
```python
import functools
import math

import jax
import jax.numpy as jnp
from jax import lax
from jax.experimental import pallas as pl
from jax.experimental.pallas import tpu as pltpu
from jax.sharding import PartitionSpec as P

BF = jnp.bfloat16
F32 = jnp.float32
EPS = 1e-05


def vmem():
    return pl.BlockSpec(memory_space=pltpu.VMEM)


def smem():
    return pl.BlockSpec(memory_space=pltpu.SMEM)


def dot_nt(a, b):
    return lax.dot_general(a, b, (((1,), (1,)), ((), ())), preferred_element_type=F32)


def layer_norm(x):
    centred = x - jnp.mean(x, -1, keepdims=True)
    variance = jnp.mean(centred * centred, -1, keepdims=True)
    return centred * lax.rsqrt(variance + EPS)


def split3(x):
    hi = x.astype(BF)
    rest = x - hi.astype(F32)
    mid = rest.astype(BF)
    low = (rest - mid.astype(F32)).astype(BF)
    return hi, mid, low


def fetch(copies, sems):
    started = [pltpu.make_async_copy(src, dst, sems.at[i]) for i, (src, dst) in enumerate(copies)]
    for copy in started:
        copy.start()
    for copy in started:
        copy.wait()


def norm_kernel(
    restype_hbm, single_hbm, table_hbm, gain_hbm, normed_ref, copies_ref, restype_ref, single_ref, table_ref, gain_ref, sems
):
    fetch(
        [
            (restype_hbm, restype_ref),
            (single_hbm, single_ref),
            (table_hbm, table_ref),
            (gain_hbm, gain_ref),
        ],
        sems,
    )
    samples, tok, width = single_ref.shape
    kinds = table_ref.shape[0]
    row = lax.broadcasted_iota(jnp.int32, (tok, kinds), 0)
    col = lax.broadcasted_iota(jnp.int32, (tok, kinds), 1)
    kind = jnp.zeros((tok, kinds), jnp.int32)
    for t in range(tok):
        kind = jnp.where(row == t, restype_ref[t], kind)
    one_hot = jnp.where(kind == col, 1.0, 0.0).astype(BF)
    emb = jnp.dot(one_hot, table_ref[...], preferred_element_type=F32)
    x = single_ref[...].astype(F32) + emb[None]
    normed = layer_norm(x) * gain_ref[...].reshape(1, 1, width)
    normed = normed.reshape(samples * tok, width).astype(BF)
    normed_ref[...] = normed
    for j in range(copies_ref.shape[0]):
        copies_ref[j] = normed


def copies_kernel(one_ref, after_ref, copies_ref):
    for j in range(copies_ref.shape[0]):
        copies_ref[j] = one_ref[...]


def bias_kernel(
    start,
    where_ref,
    normed_ref,
    chain_hbm,
    cbias_hbm,
    chain_rows_hbm,
    live_hbm,
    gain_hbm,
    weight_hbm,
    pair_hbm,
    out_ref,
    chain_ref,
    cbias_ref,
    chain_rows_ref,
    live_ref,
    gain_ref,
    weight_ref,
    pair_ref,
    sems,
    pair_sems,
):
    chunks, block, keys, channels = pair_ref.shape
    heads = weight_ref.shape[0]
    loads = [
        pltpu.make_async_copy(pair_hbm.at[pl.ds(start + i * block, block)], pair_ref.at[i], pair_sems.at[i])
        for i in range(chunks)
    ]
    loads[0].start()
    fetch(
        [
            (chain_hbm, chain_ref),
            (cbias_hbm, cbias_ref),
            (chain_rows_hbm, chain_rows_ref),
            (live_hbm, live_ref),
            (gain_hbm, gain_ref),
            (weight_hbm, weight_ref),
        ],
        sems,
    )
    for load in loads[1:]:
        load.start()
    hi, mid, low = split3(weight_ref[...] * gain_ref[...])
    lhs = jnp.concatenate(
        [
            jnp.concatenate([hi, hi], 1),
            jnp.concatenate([mid, mid], 1),
            jnp.concatenate([low, jnp.zeros_like(low)], 1),
        ],
        0,
    )
    row = lax.broadcasted_iota(jnp.int32, (heads, keys), 0)
    column = jnp.zeros((heads, keys), F32)
    for h in range(heads):
        column = jnp.where(row == h, cbias_ref[h], column)
    base = where_ref[0] * pair_hbm.shape[0] + start
    col_chain = chain_rows_ref[pl.ds(where_ref[1], 1), :]
    alive = live_ref[...] == 1
    for i in range(chunks):
        loads[i].wait()
        for q in range(0, block, 2):
            x = pair_ref[i, q : q + 2].astype(F32).reshape(2 * keys, channels)
            z = layer_norm(x)
            hi = z.astype(BF)
            low = (z - hi.astype(F32)).astype(BF)
            res = dot_nt(lhs, jnp.concatenate([hi, low], 1))
            res = res[:heads] + res[heads : 2 * heads] + res[2 * heads :]
            for k in range(2):
                at = i * block + q + k
                part = res[:, k * keys : (k + 1) * keys]
                same = col_chain == chain_ref[base + at]
                part = part + jnp.where(same, column, 0.0)
                out_ref[:, at, :] = jnp.where(alive, part, -1e30)


def query_kernel(rows_ref, own_ref, w_hbm, q_ref, gate_ref, wkv_ref, wqg_ref, sems):
    parts, per, width = rows_ref.shape
    half = per // 2
    cut = lambda i, n: w_hbm.at[:, pl.ds(i * width, n * width)]
    ahead = pltpu.make_async_copy(cut(1, 2), wkv_ref, sems.at[2])
    load_q = pltpu.make_async_copy(cut(0, 1), wqg_ref.at[0], sems.at[0])
    load_g = pltpu.make_async_copy(cut(3, 1), wqg_ref.at[1], sems.at[1])
    load_q.start()
    load_g.start()
    ahead.start()
    load_q.wait()
    x = rows_ref[...].reshape(parts * per, width)
    proj = jnp.dot(x, wqg_ref[0], preferred_element_type=F32)
    proj = proj.reshape(parts, 2, half, width)
    for s in range(2):
        q_ref[s] = proj[:, s].reshape(parts * half, width).astype(BF)
    load_g.wait()
    pre = jnp.dot(own_ref[...], wqg_ref[1], preferred_element_type=F32)
    gate_ref[...] = jax.nn.sigmoid(pre)
    ahead.wait()


def attend_kernel(order_ref, rows_ref, wkv_ref, q_ref, bias_a_ref, bias_b_ref, out_ref, x_ref):
    parts, per, width = rows_ref.shape
    half = per // 2
    heads, few, keys = bias_a_ref.shape
    queries = 2 * few
    size = width // heads
    tiles = width // 128
    scale = 1.0 / math.sqrt(size)
    for i in range(parts):
        x_ref[pl.ds(order_ref[i], 1)] = rows_ref[pl.ds(i, 1)]
    x = x_ref[...].reshape(parts * per, width)
    kf = jnp.dot(x, wkv_ref[:, :width], preferred_element_type=F32).reshape(parts, 2, half, width)
    vf = jnp.dot(x, wkv_ref[:, width:], preferred_element_type=F32).reshape(parts, 2, half, width)
    lane = lax.broadcasted_iota(jnp.int32, (queries, 128), 1)
    both = []
    for s in range(2):
        k = kf[:, s].reshape(keys, width).astype(BF)
        v = vf[:, s].reshape(keys, width).astype(BF)
        q = q_ref[s]
        sums = [jnp.zeros((queries, 128), F32) for _ in range(tiles)]
        tops = jnp.zeros((queries, 128), F32)
        tots = jnp.zeros((queries, 128), F32)
        for h in range(heads):
            a, b = h * size // 128, -(-(h + 1) * size // 128)
            spot = lax.broadcasted_iota(jnp.int32, (1, (b - a) * 128), 1) + a * 128
            mask = jnp.where((spot >= h * size) & (spot < (h + 1) * size), 1.0, 0.0).astype(BF)
            cut = slice(a * 128, b * 128)
            sc = dot_nt(q[:, cut] * mask, k[:, cut]) * scale + jnp.concatenate([bias_a_ref[h], bias_b_ref[h]], 0)
            top = jnp.max(sc, -1, keepdims=True)
            w = jnp.exp(sc - top)
            tot = jnp.sum(w, -1, keepdims=True)
            o = jnp.dot(w.astype(BF), v[:, cut] * mask, preferred_element_type=F32)
            for i in range(b - a):
                sums[a + i] = sums[a + i] + o[:, i * 128 : (i + 1) * 128]
            tops = jnp.where(lane == h, top, tops)
            tots = jnp.where(lane == h, tot, tots)
        hi, mid, low = split3(tops)
        stats = hi.astype(F32)
        for i, p in enumerate((mid.astype(F32), low.astype(F32), tots)):
            stats = stats + pltpu.roll(p, heads * (i + 1), 1)
        both.append([p.reshape(parts, 1, half, 128) for p in sums + [stats]])
    for i in range(tiles):
        pair = jnp.concatenate([both[0][i], both[1][i]], 1)
        out_ref[:, i * per : (i + 1) * per, :] = pair.reshape(parts, per, 128).astype(BF)
    first, second = [p[tiles].reshape(queries, 128) for p in both]
    stats = first + pltpu.roll(second, 64, 1)
    out_ref[:, tiles * per :, :] = stats.reshape(parts, half, 128).astype(BF)


def merge_kernel(parts_ref, gate_ref, wout_ref, out_ref):
    parts, rows, _ = parts_ref.shape
    per, width = gate_ref.shape
    half = per // 2
    tiles = width // 128
    heads = 16
    size = width // heads
    both = parts_ref[:, tiles * per :, :].astype(F32).reshape(parts, 1, half, 128)
    other = pltpu.roll(both.reshape(parts * half, 128), 64, 1).reshape(parts, 1, half, 128)
    st = jnp.concatenate([both, other], 1).reshape(parts * per, 128)
    top = st + pltpu.roll(st, 128 - heads, 1) + pltpu.roll(st, 128 - 2 * heads, 1)
    tot = pltpu.roll(st, 128 - 3 * heads, 1)
    lane = lax.broadcasted_iota(jnp.int32, (parts * per, 128), 1)
    top = jnp.where(lane < heads, top, 0.0).reshape(parts, per, 128)
    tot = jnp.where(lane < heads, tot, 1.0).reshape(parts, per, 128)
    e = jnp.exp(top - jnp.max(top, 0, keepdims=True))
    f = e / jnp.sum(e * tot, 0, keepdims=True)
    f = jnp.where(lane < heads, f.reshape(parts * per, 128), 0.0)
    hrow = lax.broadcasted_iota(jnp.int32, (128, width), 0) * size
    col = lax.broadcasted_iota(jnp.int32, (128, width), 1)
    spread = jnp.where((col >= hrow) & (col < hrow + size), 1.0, 0.0).astype(BF)
    hi = f.astype(BF)
    low = (f - hi.astype(F32)).astype(BF)
    factor = jnp.dot(jnp.concatenate([hi, low], 1), jnp.concatenate([spread, spread], 0), preferred_element_type=F32)
    attended = []
    for i in range(tiles):
        num = parts_ref[:, i * per : (i + 1) * per, :].astype(F32)
        attended.append(jnp.sum(num * factor[:, i * 128 : (i + 1) * 128].reshape(parts, per, 128), 0))
    gated = (gate_ref[...] * jnp.concatenate(attended, 1)).astype(BF)
    update = jnp.dot(gated, wout_ref[...], preferred_element_type=F32)
    out_ref[...] = update.reshape(out_ref.shape).astype(BF)


def near_swap(n):
    ring = lambda a, b, size: min((a - b) % size, (b - a) % size)
    table = []
    for c in range(n):
        cx, cyh, cco = c // 4, c // 2 % 2, c % 2
        cyl, cz = c // 8, c % 8

        def cost(j, i):
            hops = ring(cx, i // 4, 4) + ring(j % 8, cz, 8)
            hops += ring(cyh * 2 + j // 8, (i // 2 % 2) * 2 + cyl, 4)
            return 2 * hops + (cco != i % 2)

        for most in range(100):
            taken = {}

            def place(j, seen):
                for i in range(n):
                    if cost(j, i) <= most and i not in seen:
                        seen.add(i)
                        if i not in taken or place(taken[i], seen):
                            taken[i] = j
                            return True
                return False

            if all(place(j, set()) for j in range(n)):
                break
        table.append([taken[i] for i in range(n)])
    return table


def params(mib):
    return pltpu.CompilerParams(vmem_limit_bytes=mib << 20)


def shards(
    single,
    restype,
    restype_table,
    chain,
    live,
    pair,
    pair_gain,
    pair_weight,
    chain_bias,
    single_gain,
    w_qkvg,
    w_out,
):
    samples, tok, width = single.shape
    row_len, col_len, channels = pair.shape
    heads = chain_bias.shape[0]
    n_row, n_col = lax.axis_size("qrow"), lax.axis_size("kcol")
    shape = jax.ShapeDtypeStruct
    own = samples * tok

    stay = lambda *arrays: [pltpu.with_memory_space_constraint(x, pltpu.HBM) for x in arrays]
    hbm = lambda count: [pl.BlockSpec(memory_space=pltpu.HBM)] * count
    dma = pltpu.SemaphoreType.DMA
    normed, copies = pl.pallas_call(
        norm_kernel,
        name="norm",
        out_shape=(shape((own, width), BF), shape((n_col, own, width), BF)),
        in_specs=hbm(4),
        out_specs=(vmem(), vmem()),
        scratch_shapes=[
            pltpu.SMEM((tok,), jnp.int32),
            pltpu.VMEM((samples, tok, width), BF),
            pltpu.VMEM(restype_table.shape, BF),
            pltpu.VMEM((width,), F32),
            dma((4,)),
        ],
        compiler_params=params(4),
    )(*stay(restype, single, restype_table, single_gain))

    table = near_swap(n_row)
    swap = [(c * n_col + j, i * n_col + c) for c in range(n_row) for i, j in enumerate(table[c])]
    turned = lax.ppermute(normed, ("qrow", "kcol"), swap)
    row_tokens = lax.all_to_all(copies, "kcol", 0, 0)

    row_at, col_at = lax.axis_index("qrow"), lax.axis_index("kcol")
    where = jnp.stack([row_at, col_at]).astype(jnp.int32)
    order = jnp.asarray(table, jnp.int32)[col_at]
    chunks = 4
    half = row_len // 2

    def bias_of(part):
        return pl.pallas_call(
            functools.partial(bias_kernel, part * half),
            name="bias_" + str(part),
            out_shape=shape((heads, half, col_len), F32),
            in_specs=[smem()] + hbm(8),
            out_specs=vmem(),
            scratch_shapes=[
                pltpu.SMEM(chain.shape, jnp.int32),
                pltpu.SMEM((heads,), F32),
                pltpu.VMEM((chain.shape[0] // col_len, col_len), jnp.int32),
                pltpu.VMEM((1, col_len), jnp.int32),
                pltpu.VMEM((1, channels), F32),
                pltpu.VMEM((heads, channels), F32),
                pltpu.VMEM((chunks, half // chunks, col_len, channels), BF),
                dma((6,)),
                dma((chunks,)),
            ],
            compiler_params=params(6),
            cost_estimate=pl.CostEstimate(flops=5 * 10**8, bytes_accessed=10 * 10**6, transcendentals=0),
        )(
            where,
            normed,
            *stay(
                chain,
                chain_bias,
                chain.reshape(-1, col_len),
                live.reshape(1, col_len),
                pair_gain.reshape(1, channels),
                pair_weight.T,
                pair,
            ),
        )

    bias = [bias_of(part) for part in range(2)]
    turned_copies = pl.pallas_call(
        copies_kernel,
        name="copies",
        out_shape=shape((n_row, own, width), BF),
        in_specs=[vmem(), pl.BlockSpec(memory_space=pl.ANY)],
        out_specs=vmem(),
        compiler_params=params(4),
    )(turned, bias[0])
    col_tokens = lax.all_to_all(turned_copies, "qrow", 0, 0)

    queries, gate, w_kv = pl.pallas_call(
        query_kernel,
        name="query",
        out_shape=(
            shape((samples, row_len, width), BF),
            shape((own, width), F32),
            shape((width, 2 * width), BF),
        ),
        in_specs=[vmem(), vmem()] + hbm(1),
        out_specs=(vmem(), vmem(), vmem()),
        scratch_shapes=[pltpu.VMEM((2, width, width), BF), dma((3,))],
        compiler_params=params(10),
    )(row_tokens, normed, *stay(w_qkvg))

    rows = own * width // 128 + tok
    partial = pl.pallas_call(
        attend_kernel,
        name="attend",
        out_shape=shape((n_col, rows, 128), BF),
        in_specs=[smem()] + [vmem()] * 5,
        out_specs=vmem(),
        scratch_shapes=[pltpu.VMEM(col_tokens.shape, BF)],
        compiler_params=params(12),
    )(order, col_tokens, w_kv, queries, *bias)

    gathered = lax.all_to_all(partial, "kcol", 0, 0)
    return pl.pallas_call(
        merge_kernel,
        name="merge",
        out_shape=shape((samples, tok, width), BF),
        in_specs=[vmem(), vmem(), vmem()],
        out_specs=vmem(),
        compiler_params=params(8),
    )(gathered, gate, w_out)


def solution(mesh):
    return jax.shard_map(
        shards,
        mesh=mesh,
        in_specs=(
            P(None, ("qrow", "kcol"), None),
            P(("qrow", "kcol")),
            P(),
            P(),
            P("kcol"),
            P("qrow", "kcol", None),
            P(),
            P(),
            P(),
            P(),
            P(),
            P(),
        ),
        out_specs=P(None, ("qrow", "kcol"), None),
        check_vma=False,
    )
```

time: 79.7 us -> 70.5 us (0.88)
  the two profiles are of different devices: /device:TPU:40 before, /device:TPU:16 now
where the time goes in v2:
time: 70.5 us; the launch traced here: 70 us
  Pallas kernels  22.6 us (32%)
  starting transfers between devices  19.8 us (28%)
  blocking collectives  19.4 us (28%)
  waiting for transfers between devices  4.4 us (6%)
  local copies, waits for them, and re-layouts  3.54 us (5%)
    all_to_all x1, blocking collectives, shards(): gathered = lax.all_to_all(partial, 'kcol', 0, 0)  19.4 us
    pallas_call x2, Pallas kernels, bias_of(): pl.pallas_call(functools.partial(bias_kernel, part * half), name='bias_'...  10.7 us
    all_to_all x1, starting transfers between devices, shards(): row_tokens = lax.all_to_all(copies, 'kcol', 0, 0)  9.3 us
    pallas_call x1, Pallas kernels, shards(): pl.pallas_call(attend_kernel, name='attend', out_shape=shape((n_col, rows...  5.43 us
    all_to_all x1, starting transfers between devices, shards(): col_tokens = lax.all_to_all(turned_copies, 'qrow', 0, 0)  5.42 us
    ppermute x1, starting transfers between devices, shards(): turned = lax.ppermute(normed, ('qrow', 'kcol'), swap)  5.09 us
    ppermute x1, waiting for transfers between devices, shards(): turned = lax.ppermute(normed, ('qrow', 'kcol'), swap)  4.4 us
    unnamed x10, local copies, waits for them, and re-layouts  2.84 us
  transfers between devices with their start and end apart: 3, of which 1 were waited for; matrix products, arithmetic and copies ran while one was open for 1% of the time, Pallas kernels for 20%

profile of v2, /device:TPU:16, one launch (start us, length us, event | category | flops | bytes accessed | tf_op | source)
XLA Modules:
  0.0 70.0 jit_solution(12203739040406806249)
XLA Ops:
  0.0 1.9 %norm.1 = (bf16[16,768]{1,0:T(8,128)(2,1)S(1)}, bf16[16,16,768]{2,1,0:T(8,128)(2,1)}) custom-call(s32[8]{0:T(128)} %restype_hbm.1, bf16[2,8,768]{2,1,0:T(8,128)(2,1)} %single_hbm.1, bf16[32,768]{1,0:T(8,128)(2,1)} %table_hbm.1, f32[768]{0:T(1024)} %gain_hbm.1), custom_call_target="tpu_custom_call" | custom-call | tf_op jit(solution)/shard_map/norm/pallas_call | solution.py:321
  1.9 9.3 %all-to-all-start.1 = ((bf16[16,16,768]{2,1,0:T(8,128)(2,1)}), bf16[16,16,768]{2,1,0:T(8,128)(2,1)S(1)}, u32[]{:S(2)}, u32[]{:S(2)}) async-start(bf16[16,16,768]{2,1,0:T(8,128)(2,1)} %get-tuple-element.11), calls=%async_computation.1 | async-start | bytes 786432 | tf_op jit(solution)/shard_map/all_to_all | solution.py:340
  11.2 5.1 %collective-permute-start = (bf16[16,768]{1,0:T(8,128)(2,1)S(1)}, bf16[16,768]{1,0:T(8,128)(2,1)S(1)}, u32[]{:S(2)}, u32[]{:S(2)}) collective-permute-start(bf16[16,768]{1,0:T(8,128)(2,1)S(1)} %get-tuple-element.10.normed_ref.own_ref), channel_id=1, source_target_pairs={{15,0},{14,16},{12,32},{13,48},{10,64},{8,80},{11,96},{9,112},{5,1... | collective-permute-start | bytes 73736 | tf_op jit(solution)/shard_map/ppermute | solution.py:339
  16.3 0.1 pad_add_fusion.where_ref
  16.4 5.4 %bias_0.1.after_ref.bias_a_ref = f32[16,64,128]{2,1,0:T(8,128)S(1)} custom-call(s32[2]{0:T(128)S(1)} %pad_add_fusion.where_ref, bf16[16,768]{1,0:T(8,128)(2,1)S(1)} %get-tuple-element.10.normed_ref.own_ref, s32[2048]{0:T(1024)} %chain_hbm.3, f32[16]{0:T(128)} %cbias_hbm.3, s32[16,128]{1,0:T(8,128)} %bitcast.8, s32[1,128]{1,0:T(1,128)} %bitcast.12, ...), custom_call_target="tpu_custom_call" | custom-call | flops 500000000 | bytes 10000000 | tf_op jit(solution)/shard_map/bias_0/pallas_call | solution.py:349
  21.8 4.4 %collective-permute-done.one_ref = bf16[16,768]{1,0:T(8,128)(2,1)S(1)} collective-permute-done((bf16[16,768]{1,0:T(8,128)(2,1)S(1)}, bf16[16,768]{1,0:T(8,128)(2,1)S(1)}, u32[]{:S(2)}, u32[]{:S(2)}) %collective-permute-start) | collective-permute-done | bytes 24608 | tf_op jit(solution)/shard_map/ppermute | solution.py:339
  26.2 0.8 %copies.1 = bf16[16,16,768]{2,1,0:T(8,128)(2,1)} custom-call(bf16[16,768]{1,0:T(8,128)(2,1)S(1)} %collective-permute-done.one_ref, f32[16,64,128]{2,1,0:T(8,128)S(1)} %bias_0.1.after_ref.bias_a_ref), custom_call_target="tpu_custom_call" | custom-call | tf_op jit(solution)/shard_map/copies/pallas_call | solution.py:383
  26.9 0.0 all-to-all-done.1.rows_ref
  26.9 0.0 copy-start
  26.9 5.4 %all-to-all-start = ((bf16[16,16,768]{2,1,0:T(8,128)(2,1)}), bf16[16,16,768]{2,1,0:T(8,128)(2,1)}, u32[]{:S(2)}, u32[]{:S(2)}) async-start(bf16[16,16,768]{2,1,0:T(8,128)(2,1)} %copies.1), calls=%async_computation | async-start | bytes 786432 | tf_op jit(solution)/shard_map/all_to_all | solution.py:391
  32.4 5.4 %bias_1.1.bias_b_ref = f32[16,64,128]{2,1,0:T(8,128)S(1)} custom-call(s32[2]{0:T(128)S(1)} %pad_add_fusion.where_ref, bf16[16,768]{1,0:T(8,128)(2,1)S(1)} %get-tuple-element.10.normed_ref.own_ref, s32[2048]{0:T(1024)} %chain_hbm.3, f32[16]{0:T(128)} %cbias_hbm.3, s32[16,128]{1,0:T(8,128)} %bitcast.9, s32[1,128]{1,0:T(1,128)} %bitcast.13, f32[1,128]{1,0:T(1,128)} %bitcast.15, ...), custom_call_target="tpu_custom_call" | custom-call | flops 500000000 | bytes 10000000 | tf_op jit(solution)/shard_map/bias_1/pallas_call | solution.py:349
  37.7 0.0 copy-done
  37.7 0.7 %dynamic-slice_bitcast_fusion.order_ref = s32[16]{0:T(128)S(1)} fusion(s32[16,16]{1,0:T(8,128)} %constant.13.clone, s32[]{:T(128)S(6)} %select_n.3), kind=kLoop, calls=%fused_computation.1 | loop fusion | bytes 132 | tf_op jit(solution)/shard_map/squeeze | solution.py:344
  38.4 0.0 copy-start.1
  38.4 1.0 %copy-done.1 = bf16[16,16,768]{2,1,0:T(8,128)(2,1)S(1)} copy-done((bf16[16,16,768]{2,1,0:T(8,128)(2,1)S(1)}, bf16[16,16,768]{2,1,0:T(8,128)(2,1)}, u32[]{:S(2)}) %copy-start.1) | copy-done | bytes 393240
  39.4 2.4 %query.1 = (bf16[2,128,768]{2,1,0:T(8,128)(2,1)S(1)}, f32[16,768]{1,0:T(8,128)S(1)}, bf16[768,1536]{1,0:T(8,128)(2,1)S(1)}) custom-call(bf16[16,16,768]{2,1,0:T(8,128)(2,1)S(1)} %copy-done.1, bf16[16,768]{1,0:T(8,128)(2,1)S(1)} %get-tuple-element.10.normed_ref.own_ref, bf16[768,3072]{1,0:T(8,128)(2,1)} %w_hbm.1), custom_call_target="tpu_custom_call" | custom-call | tf_op jit(solution)/shard_map/query/pallas_call | solution.py:393
  41.9 0.0 copy-start.3
  41.9 0.7 %copy-done.3 = bf16[2,128,768]{2,1,0:T(8,128)(2,1)} copy-done((bf16[2,128,768]{2,1,0:T(8,128)(2,1)}, bf16[2,128,768]{2,1,0:T(8,128)(2,1)S(1)}, u32[]{:S(2)}) %copy-start.3) | copy-done | bytes 393240
  42.6 0.0 all-to-all-done.rows_ref
  42.6 1.1 %copy-done.4 = bf16[2,128,768]{2,1,0:T(8,128)(2,1)S(1)} copy-done((bf16[2,128,768]{2,1,0:T(8,128)(2,1)S(1)}, bf16[2,128,768]{2,1,0:T(8,128)(2,1)}, u32[]{:S(2)}) %copy-start.4) | copy-done | bytes 393240
  43.7 5.4 %attend.1 = bf16[16,104,128]{2,1,0:T(8,128)(2,1)S(1)} custom-call(s32[16]{0:T(128)S(1)} %dynamic-slice_bitcast_fusion.order_ref, bf16[16,16,768]{2,1,0:T(8,128)(2,1)} %all-to-all-done.rows_ref, bf16[768,1536]{1,0:T(8,128)(2,1)S(1)} %get-tuple-element.12.wkv_ref, bf16[2,128,768]{2,1,0:T(8,128)(2,1)S(1)} %copy-done.4, ...), custom_call_target="tpu_custom_call" | custom-call | tf_op jit(solution)/shard_map/attend/pallas_call | solution.py:408
  49.1 19.4 %all_to_all.15.parts_ref = bf16[16,104,128]{2,1,0:T(8,128)(2,1)S(1)} all-to-all(bf16[16,104,128]{2,1,0:T(8,128)(2,1)S(1)} %attend.1), channel_id=1, replica_groups=mesh['qrow'=16,'kcol'=16] {'kcol'}, dimensions={0} | all-to-all | bytes 851968 | tf_op jit(solution)/shard_map/all_to_all | solution.py:418
  68.6 0.0 copy-done.2
  68.6 1.4 %merge.1 = bf16[2,8,768]{2,1,0:T(8,128)(2,1)} custom-call(bf16[16,104,128]{2,1,0:T(8,128)(2,1)S(1)} %all_to_all.15.parts_ref, f32[16,768]{1,0:T(8,128)S(1)} %get-tuple-element.14.gate_ref, bf16[768,768]{1,0:T(8,128)(2,1)S(1)} %copy-done.2), custom_call_target="tpu_custom_call" | custom-call | tf_op jit(solution)/shard_map/merge/pallas_call | solution.py:419
  (2 shorter events, 0.0 us)
Async XLA Ops:
  1.9 25.0 %all-to-all-start.1 = ((bf16[16,16,768]{2,1,0:T(8,128)(2,1)}), bf16[16,16,768]{2,1,0:T(8,128)(2,1)S(1)}, u32[]{:S(2)}, u32[]{:S(2)}) async-start(bf16[16,16,768]{2,1,0:T(8,128)(2,1)} %get-tuple-element.11), calls=%async_computation.1 | async-start | bytes 786432 | tf_op jit(solution)/shard_map/all_to_all | solution.py:340
  11.2 14.9 %collective-permute-start = (bf16[16,768]{1,0:T(8,128)(2,1)S(1)}, bf16[16,768]{1,0:T(8,128)(2,1)S(1)}, u32[]{:S(2)}, u32[]{:S(2)}) collective-permute-start(bf16[16,768]{1,0:T(8,128)(2,1)S(1)} %get-tuple-element.10.normed_ref.own_ref), channel_id=1, source_target_pairs={{15,0},{14,16},{12,32},{13,48},{10,64},{8,80},{11,96},{9,112},{5,1... | collective-permute-start | bytes 73736 | tf_op jit(solution)/shard_map/ppermute | solution.py:339
  26.9 10.8 %copy-start = (bf16[16,16,768]{2,1,0:T(8,128)(2,1)}, bf16[16,16,768]{2,1,0:T(8,128)(2,1)S(1)}, u32[]{:S(2)}) copy-start(bf16[16,16,768]{2,1,0:T(8,128)(2,1)S(1)} %all-to-all-done.1.rows_ref) | copy-start | bytes 1179652
  26.9 15.7 %all-to-all-start = ((bf16[16,16,768]{2,1,0:T(8,128)(2,1)}), bf16[16,16,768]{2,1,0:T(8,128)(2,1)}, u32[]{:S(2)}, u32[]{:S(2)}) async-start(bf16[16,16,768]{2,1,0:T(8,128)(2,1)} %copies.1), calls=%async_computation | async-start | bytes 786432 | tf_op jit(solution)/shard_map/all_to_all | solution.py:391
  38.4 1.0 %copy-start.1 = (bf16[16,16,768]{2,1,0:T(8,128)(2,1)S(1)}, bf16[16,16,768]{2,1,0:T(8,128)(2,1)}, u32[]{:S(2)}) copy-start(bf16[16,16,768]{2,1,0:T(8,128)(2,1)} %copy-done) | copy-start | bytes 1179652
  41.9 0.8 %copy-start.3 = (bf16[2,128,768]{2,1,0:T(8,128)(2,1)}, bf16[2,128,768]{2,1,0:T(8,128)(2,1)S(1)}, u32[]{:S(2)}) copy-start(bf16[2,128,768]{2,1,0:T(8,128)(2,1)S(1)} %get-tuple-element.13.q_ref) | copy-start | bytes 1179652
  42.6 26.0 %copy-start.2 = (bf16[768,768]{1,0:T(8,128)(2,1)S(1)}, bf16[768,768]{1,0:T(8,128)(2,1)}, u32[]{:S(2)}) copy-start(bf16[768,768]{1,0:T(8,128)(2,1)} %wout_ref.1) | copy-start | bytes 3538948
  42.6 1.1 %copy-start.4 = (bf16[2,128,768]{2,1,0:T(8,128)(2,1)S(1)}, bf16[2,128,768]{2,1,0:T(8,128)(2,1)}, u32[]{:S(2)}) copy-start(bf16[2,128,768]{2,1,0:T(8,128)(2,1)} %copy-done.3) | copy-start | bytes 1179652

commit v3 on v2

--- a/solution.py
+++ b/solution.py
@@ -81,150 +81,162 @@
         copies_ref[j] = one_ref[...]
 
 
-def bias_kernel(
-    start,
-    where_ref,
-    normed_ref,
-    chain_hbm,
-    cbias_hbm,
-    chain_rows_hbm,
-    live_hbm,
-    gain_hbm,
-    weight_hbm,
-    pair_hbm,
-    out_ref,
-    chain_ref,
-    cbias_ref,
-    chain_rows_ref,
-    live_ref,
-    gain_ref,
-    weight_ref,
-    pair_ref,
-    sems,
-    pair_sems,
-):
+def bias_kernel(start, ahead, where_ref, normed_ref, *refs):
+    ins, refs = refs[: 7 + ahead], refs[7 + ahead :]
+    pair_hbm = ins[6]
+    out_ref, refs = refs[0], refs[1:]
+    if ahead:
+        (gate_ref, w_ref), refs = refs[:2], refs[2:]
+    chain_ref, cbias_ref, chain_rows_ref, live_ref, gain_ref, weight_ref, pair_ref, sems, pair_sems = refs[:9]
     chunks, block, keys, channels = pair_ref.shape
     heads = weight_ref.shape[0]
     loads = [
         pltpu.make_async_copy(pair_hbm.at[pl.ds(start + i * block, block)], pair_ref.at[i], pair_sems.at[i])
         for i in range(chunks)
     ]
-    loads[0].start()
-    fetch(
-        [
-            (chain_hbm, chain_ref),
-            (cbias_hbm, cbias_ref),
-            (chain_rows_hbm, chain_rows_ref),
-            (live_hbm, live_ref),
-            (gain_hbm, gain_ref),
-            (weight_hbm, weight_ref),
-        ],
-        sems,
-    )
-    for load in loads[1:]:
+    for load in loads[:2]:
         load.start()
-    hi, mid, low = split3(weight_ref[...] * gain_ref[...])
-    lhs = jnp.concatenate(
-        [
-            jnp.concatenate([hi, hi], 1),
-            jnp.concatenate([mid, mid], 1),
-            jnp.concatenate([low, jnp.zeros_like(low)], 1),
-        ],
-        0,
-    )
+    small = list(zip(ins[:6], (chain_ref, cbias_ref, chain_rows_ref, live_ref, gain_ref, weight_ref)))
+    small = [pltpu.make_async_copy(src, dst, sems.at[i]) for i, (src, dst) in enumerate(small)]
+    for load in small + loads[2:]:
+        load.start()
+    if ahead:
+        width = normed_ref.shape[1]
+        wg_ref, w_sems = refs[9:]
+        w_hbm = ins[7]
+        load_g = pltpu.make_async_copy(w_hbm.at[:, pl.ds(3 * width, width)], wg_ref, w_sems.at[0])
+        load_w = pltpu.make_async_copy(w_hbm.at[:, pl.ds(width, 2 * width)], w_ref, w_sems.at[1])
+        load_g.start()
+        load_w.start()
+    for load in small:
+        load.wait()
+    weight = weight_ref[...] * gain_ref[...]
+    lhs = jnp.concatenate(split3(weight), 0)
+    total = jnp.sum(weight, -1, keepdims=True)
     row = lax.broadcasted_iota(jnp.int32, (heads, keys), 0)
     column = jnp.zeros((heads, keys), F32)
     for h in range(heads):
         column = jnp.where(row == h, cbias_ref[h], column)
     base = where_ref[0] * pair_hbm.shape[0] + start
     col_chain = chain_rows_ref[pl.ds(where_ref[1], 1), :]
-    alive = live_ref[...] == 1
+    alive = jnp.broadcast_to(live_ref[...] == 1, (heads, keys))
     for i in range(chunks):
         loads[i].wait()
         for q in range(0, block, 2):
-            x = pair_ref[i, q : q + 2].astype(F32).reshape(2 * keys, channels)
-            z = layer_norm(x)
-            hi = z.astype(BF)
-            low = (z - hi.astype(F32)).astype(BF)
-            res = dot_nt(lhs, jnp.concatenate([hi, low], 1))
+            turned = pair_ref[i, q : q + 2].reshape(2 * keys, channels).T
+            x = turned.astype(F32)
+            mean = jnp.sum(x, 0, keepdims=True) * (1.0 / channels)
+            centred = x - mean
+            variance = jnp.sum(centred * centred, 0, keepdims=True) * (1.0 / channels)
+            res = jnp.dot(lhs, turned, preferred_element_type=F32)
             res = res[:heads] + res[heads : 2 * heads] + res[2 * heads :]
+            res = (res - total * mean) * lax.rsqrt(variance + EPS)
             for k in range(2):
                 at = i * block + q + k
                 part = res[:, k * keys : (k + 1) * keys]
                 same = col_chain == chain_ref[base + at]
                 part = part + jnp.where(same, column, 0.0)
                 out_ref[:, at, :] = jnp.where(alive, part, -1e30)
-
-
-def query_kernel(rows_ref, own_ref, w_hbm, q_ref, gate_ref, wkv_ref, wqg_ref, sems):
+    if ahead:
+        load_g.wait()
+        pre = jnp.dot(normed_ref[...], wg_ref[...], preferred_element_type=F32)
+        gate_ref[...] = jax.nn.sigmoid(pre)
+        load_w.wait()
+
+
+def attend_kernel(
+    where_ref,
+    order_ref,
+    rows_ref,
+    cols_hbm,
+    wkv_ref,
+    w_hbm,
+    bias_a_hbm,
+    bias_b_hbm,
+    out_ref,
+    x_ref,
+    wq_ref,
+    bias_ref,
+    sems,
+):
     parts, per, width = rows_ref.shape
     half = per // 2
-    cut = lambda i, n: w_hbm.at[:, pl.ds(i * width, n * width)]
-    ahead = pltpu.make_async_copy(cut(1, 2), wkv_ref, sems.at[2])
-    load_q = pltpu.make_async_copy(cut(0, 1), wqg_ref.at[0], sems.at[0])
-    load_g = pltpu.make_async_copy(cut(3, 1), wqg_ref.at[1], sems.at[1])
-    load_q.start()
-    load_g.start()
-    ahead.start()
-    load_q.wait()
-    x = rows_ref[...].reshape(parts * per, width)
-    proj = jnp.dot(x, wqg_ref[0], preferred_element_type=F32)
-    proj = proj.reshape(parts, 2, half, width)
+    heads, queries, keys = bias_ref.shape
+    few = queries // 2
+    size = width // heads
+    scale = 1.0 / math.sqrt(size)
+    loads = [
+        pltpu.make_async_copy(w_hbm.at[:, pl.ds(0, width)], wq_ref, sems.at[0]),
+        pltpu.make_async_copy(bias_a_hbm, bias_ref.at[:, pl.ds(0, few)], sems.at[1]),
+        pltpu.make_async_copy(bias_b_hbm, bias_ref.at[:, pl.ds(few, few)], sems.at[2]),
+    ]
+    tokens = [
+        pltpu.make_async_copy(cols_hbm.at[i], x_ref.at[order_ref[where_ref[1] * parts + i]], sems.at[3 + i])
+        for i in range(parts)
+    ]
+    for load in tokens + loads:
+        load.start()
+    for load in tokens:
+        load.wait()
+
+    def project(tokens, w):
+        x = tokens[...].reshape(parts * per, width)
+        return jnp.dot(x, w, preferred_element_type=F32).reshape(parts, 2, half, width)
+
+    kf, vf = project(x_ref, wkv_ref[:, :width]), project(x_ref, wkv_ref[:, width:])
+    for load in loads:
+        load.wait()
+    qf = project(rows_ref, wq_ref[...])
+    span = 256
+    wins = width // span
+
+    def members(t):
+        return [h for h in range(heads) if h * size < (t + 1) * span and (h + 1) * size > t * span]
+
+    def mask_of(h, t):
+        spot = lax.broadcasted_iota(jnp.int32, (1, span), 1) + t * span
+        return jnp.where((spot >= h * size) & (spot < (h + 1) * size), 1.0, 0.0).astype(BF)
+
+    lane = lax.broadcasted_iota(jnp.int32, (queries, 128), 1)
+    stats = jnp.zeros((queries, 128), F32)
     for s in range(2):
-        q_ref[s] = proj[:, s].reshape(parts * half, width).astype(BF)
-    load_g.wait()
-    pre = jnp.dot(own_ref[...], wqg_ref[1], preferred_element_type=F32)
-    gate_ref[...] = jax.nn.sigmoid(pre)
-    ahead.wait()
-
-
-def attend_kernel(order_ref, rows_ref, wkv_ref, q_ref, bias_a_ref, bias_b_ref, out_ref, x_ref):
-    parts, per, width = rows_ref.shape
-    half = per // 2
-    heads, few, keys = bias_a_ref.shape
-    queries = 2 * few
-    size = width // heads
-    tiles = width // 128
-    scale = 1.0 / math.sqrt(size)
-    for i in range(parts):
-        x_ref[pl.ds(order_ref[i], 1)] = rows_ref[pl.ds(i, 1)]
-    x = x_ref[...].reshape(parts * per, width)
-    kf = jnp.dot(x, wkv_ref[:, :width], preferred_element_type=F32).reshape(parts, 2, half, width)
-    vf = jnp.dot(x, wkv_ref[:, width:], preferred_element_type=F32).reshape(parts, 2, half, width)
-    lane = lax.broadcasted_iota(jnp.int32, (queries, 128), 1)
-    both = []
-    for s in range(2):
+        q = qf[:, s].reshape(queries, width).astype(BF)
         k = kf[:, s].reshape(keys, width).astype(BF)
         v = vf[:, s].reshape(keys, width).astype(BF)
-        q = q_ref[s]
-        sums = [jnp.zeros((queries, 128), F32) for _ in range(tiles)]
+        raw = {}
+        for t in range(wins):
+            cut = slice(t * span, (t + 1) * span)
+            lhs = jnp.concatenate([q[:, cut] * mask_of(h, t) for h in members(t)], 0)
+            res = dot_nt(lhs, k[:, cut])
+            for i, h in enumerate(members(t)):
+                piece = res[i * queries : (i + 1) * queries]
+                raw[h] = raw[h] + piece if h in raw else piece
         tops = jnp.zeros((queries, 128), F32)
         tots = jnp.zeros((queries, 128), F32)
+        rounded = []
         for h in range(heads):
-            a, b = h * size // 128, -(-(h + 1) * size // 128)
-            spot = lax.broadcasted_iota(jnp.int32, (1, (b - a) * 128), 1) + a * 128
-            mask = jnp.where((spot >= h * size) & (spot < (h + 1) * size), 1.0, 0.0).astype(BF)
-            cut = slice(a * 128, b * 128)
-            sc = dot_nt(q[:, cut] * mask, k[:, cut]) * scale + jnp.concatenate([bias_a_ref[h], bias_b_ref[h]], 0)
+            sc = raw[h] * scale + bias_ref[h]
             top = jnp.max(sc, -1, keepdims=True)
             w = jnp.exp(sc - top)
-            tot = jnp.sum(w, -1, keepdims=True)
-            o = jnp.dot(w.astype(BF), v[:, cut] * mask, preferred_element_type=F32)
-            for i in range(b - a):
-                sums[a + i] = sums[a + i] + o[:, i * 128 : (i + 1) * 128]
+            rounded.append(w.astype(BF))
+            tots = jnp.where(lane == h, jnp.sum(w, -1, keepdims=True), tots)
             tops = jnp.where(lane == h, top, tops)
-            tots = jnp.where(lane == h, tot, tots)
+        for t in range(wins):
+            cut = slice(t * span, (t + 1) * span)
+            o = jnp.dot(
+                jnp.concatenate([rounded[h] for h in members(t)], 1),
+                jnp.concatenate([v[:, cut] * mask_of(h, t) for h in members(t)], 0),
+                preferred_element_type=F32,
+            )
+            at = (s * wins + t) * per
+            tiles = [o[:, i * 128 : (i + 1) * 128].reshape(parts, half, 128) for i in range(2)]
+            out_ref[:, at : at + per, :] = jnp.concatenate(tiles, 1).astype(BF)
         hi, mid, low = split3(tops)
-        stats = hi.astype(F32)
+        mine = hi.astype(F32)
         for i, p in enumerate((mid.astype(F32), low.astype(F32), tots)):
-            stats = stats + pltpu.roll(p, heads * (i + 1), 1)
-        both.append([p.reshape(parts, 1, half, 128) for p in sums + [stats]])
-    for i in range(tiles):
-        pair = jnp.concatenate([both[0][i], both[1][i]], 1)
-        out_ref[:, i * per : (i + 1) * per, :] = pair.reshape(parts, per, 128).astype(BF)
-    first, second = [p[tiles].reshape(queries, 128) for p in both]
-    stats = first + pltpu.roll(second, 64, 1)
-    out_ref[:, tiles * per :, :] = stats.reshape(parts, half, 128).astype(BF)
+            mine = mine + pltpu.roll(p, heads * (i + 1), 1)
+        stats = stats + (pltpu.roll(mine, 64, 1) if s else mine)
+    out_ref[:, 2 * wins * per :, :] = stats.reshape(parts, half, 128).astype(BF)
 
 
 def merge_kernel(parts_ref, gate_ref, wout_ref, out_ref):
@@ -253,7 +265,9 @@
     factor = jnp.dot(jnp.concatenate([hi, low], 1), jnp.concatenate([spread, spread], 0), preferred_element_type=F32)
     attended = []
     for i in range(tiles):
-        num = parts_ref[:, i * per : (i + 1) * per, :].astype(F32)
+        at = [(s * (tiles // 2) + i // 2) * per for s in range(2)]
+        num = [parts_ref[:, a : a + per, :].astype(F32)[:, i % 2 * half : i % 2 * half + half] for a in at]
+        num = jnp.concatenate(num, 1)
         attended.append(jnp.sum(num * factor[:, i * 128 : (i + 1) * 128].reshape(parts, per, 128), 0))
     gated = (gate_ref[...] * jnp.concatenate(attended, 1)).astype(BF)
     update = jnp.dot(gated, wout_ref[...], preferred_element_type=F32)
@@ -339,31 +353,34 @@
     turned = lax.ppermute(normed, ("qrow", "kcol"), swap)
     row_tokens = lax.all_to_all(copies, "kcol", 0, 0)
 
-    row_at, col_at = lax.axis_index("qrow"), lax.axis_index("kcol")
-    where = jnp.stack([row_at, col_at]).astype(jnp.int32)
-    order = jnp.asarray(table, jnp.int32)[col_at]
+    where = jnp.stack([lax.axis_index("qrow"), lax.axis_index("kcol")]).astype(jnp.int32)
     chunks = 4
     half = row_len // 2
 
     def bias_of(part):
+        out = [shape((heads, half, col_len), F32)]
+        scratch = [
+            pltpu.SMEM(chain.shape, jnp.int32),
+            pltpu.SMEM((heads,), F32),
+            pltpu.VMEM((chain.shape[0] // col_len, col_len), jnp.int32),
+            pltpu.VMEM((1, col_len), jnp.int32),
+            pltpu.VMEM((1, channels), F32),
+            pltpu.VMEM((heads, channels), F32),
+            pltpu.VMEM((chunks, half // chunks, col_len, channels), BF),
+            dma((6,)),
+            dma((chunks,)),
+        ]
+        if part:
+            out += [shape((own, width), F32), shape((width, 2 * width), BF)]
+            scratch += [pltpu.VMEM((width, width), BF), dma((2,))]
         return pl.pallas_call(
-            functools.partial(bias_kernel, part * half),
+            functools.partial(bias_kernel, part * half, part),
             name="bias_" + str(part),
-            out_shape=shape((heads, half, col_len), F32),
-            in_specs=[smem()] + hbm(8),
-            out_specs=vmem(),
-            scratch_shapes=[
-                pltpu.SMEM(chain.shape, jnp.int32),
-                pltpu.SMEM((heads,), F32),
-                pltpu.VMEM((chain.shape[0] // col_len, col_len), jnp.int32),
-                pltpu.VMEM((1, col_len), jnp.int32),
-                pltpu.VMEM((1, channels), F32),
-                pltpu.VMEM((heads, channels), F32),
-                pltpu.VMEM((chunks, half // chunks, col_len, channels), BF),
-                dma((6,)),
-                dma((chunks,)),
-            ],
-            compiler_params=params(6),
+            out_shape=out,
+            in_specs=[smem(), vmem()] + hbm(7 + part),
+            out_specs=[vmem()] * len(out),
+            scratch_shapes=scratch,
+            compiler_params=params(12 if part else 6),
             cost_estimate=pl.CostEstimate(flops=5 * 10**8, bytes_accessed=10 * 10**6, transcendentals=0),
         )(
             where,
@@ -376,10 +393,12 @@
                 pair_gain.reshape(1, channels),
                 pair_weight.T,
                 pair,
+                *[w_qkvg][:part],
             ),
         )
 
-    bias = [bias_of(part) for part in range(2)]
+    (bias_a,) = bias_of(0)
+    bias_b, gate, w_kv = bias_of(1)
     turned_copies = pl.pallas_call(
         copies_kernel,
         name="copies",
@@ -387,33 +406,26 @@
         in_specs=[vmem(), pl.BlockSpec(memory_space=pl.ANY)],
         out_specs=vmem(),
         compiler_params=params(4),
-    )(turned, bias[0])
+    )(turned, bias_a)
+    turned_copies, row_tokens = lax.optimization_barrier((turned_copies, row_tokens))
     col_tokens = lax.all_to_all(turned_copies, "qrow", 0, 0)
 
-    queries, gate, w_kv = pl.pallas_call(
-        query_kernel,
-        name="query",
-        out_shape=(
-            shape((samples, row_len, width), BF),
-            shape((own, width), F32),
-            shape((width, 2 * width), BF),
-        ),
-        in_specs=[vmem(), vmem()] + hbm(1),
-        out_specs=(vmem(), vmem(), vmem()),
-        scratch_shapes=[pltpu.VMEM((2, width, width), BF), dma((3,))],
-        compiler_params=params(10),
-    )(row_tokens, normed, *stay(w_qkvg))
-
+    order = jnp.asarray(table, jnp.int32).reshape(-1)
     rows = own * width // 128 + tok
     partial = pl.pallas_call(
         attend_kernel,
         name="attend",
         out_shape=shape((n_col, rows, 128), BF),
-        in_specs=[smem()] + [vmem()] * 5,
+        in_specs=[smem()] * 2 + [vmem()] + hbm(1) + [vmem()] + hbm(3),
         out_specs=vmem(),
-        scratch_shapes=[pltpu.VMEM(col_tokens.shape, BF)],
-        compiler_params=params(12),
-    )(order, col_tokens, w_kv, queries, *bias)
+        scratch_shapes=[
+            pltpu.VMEM(col_tokens.shape, BF),
+            pltpu.VMEM((width, width), BF),
+            pltpu.VMEM((heads, row_len, col_len), F32),
+            dma((3 + n_row,)),
+        ],
+        compiler_params=params(16),
+    )(where, order, row_tokens, *stay(col_tokens), w_kv, *stay(w_qkvg, bias_a, bias_b))
 
     gathered = lax.all_to_all(partial, "kcol", 0, 0)
     return pl.pallas_call(

time: 70.5 us -> 67.9 us (0.963)
  the two profiles are of different devices: /device:TPU:16 before, /device:TPU:40 now
where the time goes in v3:
time: 67.9 us; the launch traced here: 67.5 us
  blocking collectives  18.6 us (27%)
  Pallas kernels  17.3 us (25%)
  starting transfers between devices  17.3 us (25%)
  waiting for transfers between devices  13.4 us (20%)
  local copies, waits for them, and re-layouts  0.79 us (1%)
    all_to_all x1, blocking collectives, shards(): gathered = lax.all_to_all(partial, 'kcol', 0, 0)  18.6 us
    all_to_all x1, starting transfers between devices, shards(): row_tokens = lax.all_to_all(copies, 'kcol', 0, 0)  9.5 us
    pallas_call x2, Pallas kernels, bias_of(): pl.pallas_call(functools.partial(bias_kernel, part * half, part), name='b...  8.09 us
    ppermute x1, waiting for transfers between devices, shards(): turned = lax.ppermute(normed, ('qrow', 'kcol'), swap)  7.04 us
    all_to_all x1, starting transfers between devices, shards(): col_tokens = lax.all_to_all(turned_copies, 'qrow', 0, 0)  6.71 us
    all_to_all x1, waiting for transfers between devices, shards(): col_tokens = lax.all_to_all(turned_copies, 'qrow', 0, 0)  5.6 us
    pallas_call x1, Pallas kernels, shards(): pl.pallas_call(attend_kernel, name='attend', out_shape=shape((n_col, rows...  5.08 us
    pallas_call x1, Pallas kernels, shards(): pl.pallas_call(norm_kernel, name='norm', out_shape=(shape((own, width), B...  1.92 us
  transfers between devices with their start and end apart: 3, of which 3 were waited for; matrix products, arithmetic and copies ran while one was open for 0% of the time, Pallas kernels for 13%

profile of v3, /device:TPU:40, one launch (start us, length us, event | category | flops | bytes accessed | tf_op | source)
XLA Modules:
  0.0 67.5 jit_solution(7759318149845092716)
XLA Ops:
  0.0 1.9 %norm.1 = (bf16[16,768]{1,0:T(8,128)(2,1)S(1)}, bf16[16,16,768]{2,1,0:T(8,128)(2,1)}) custom-call(s32[8]{0:T(128)} %restype_hbm.1, bf16[2,8,768]{2,1,0:T(8,128)(2,1)} %single_hbm.1, bf16[32,768]{1,0:T(8,128)(2,1)} %table_hbm.1, f32[768]{0:T(1024)} %gain_hbm.1), custom_call_target="tpu_custom_call" | custom-call | tf_op jit(solution)/shard_map/norm/pallas_call | solution.py:335
  1.9 9.5 %all-to-all-start = ((bf16[16,16,768]{2,1,0:T(8,128)(2,1)}), bf16[16,16,768]{2,1,0:T(8,128)(2,1)S(1)}, u32[]{:S(2)}, u32[]{:S(2)}) async-start(bf16[16,16,768]{2,1,0:T(8,128)(2,1)} %get-tuple-element.13), calls=%async_computation | async-start | bytes 786432 | tf_op jit(solution)/shard_map/all_to_all | solution.py:354
  11.4 1.1 %collective-permute-start = (bf16[16,768]{1,0:T(8,128)(2,1)S(1)}, bf16[16,768]{1,0:T(8,128)(2,1)S(1)}, u32[]{:S(2)}, u32[]{:S(2)}) collective-permute-start(bf16[16,768]{1,0:T(8,128)(2,1)S(1)} %get-tuple-element.12.normed_ref), channel_id=1, source_target_pairs={{15,0},{14,16},{12,32},{13,48},{10,64},{8,80},{11,96},{9,112},{5,1... | collective-permute-start | bytes 73736 | tf_op jit(solution)/shard_map/ppermute | solution.py:353
  12.5 0.1 pad_add_fusion.where_ref
  12.6 3.7 %bias_0.1.after_ref.bias_a_hbm = f32[16,64,128]{2,1,0:T(8,128)S(1)} custom-call(s32[2]{0:T(128)S(1)} %pad_add_fusion.where_ref, bf16[16,768]{1,0:T(8,128)(2,1)S(1)} %get-tuple-element.12.normed_ref, s32[2048]{0:T(1024)} %refs_0_.3, f32[16]{0:T(128)} %refs_1_.3, s32[16,128]{1,0:T(8,128)} %bitcast.6, s32[1,128]{1,0:T(1,128)} %bitcast.10, f32[1,128]{1,0:T(1,128)} %bitcast.12, ...), custom_call_target="tpu_custom_call" | custom-call | flops 500000000 | bytes 10000000 | tf_op jit(solution)/shard_map/bias_0/pallas_call | solution.py:376
  16.3 0.0 copy-start
  16.4 7.0 %collective-permute-done.one_ref = bf16[16,768]{1,0:T(8,128)(2,1)S(1)} collective-permute-done((bf16[16,768]{1,0:T(8,128)(2,1)S(1)}, bf16[16,768]{1,0:T(8,128)(2,1)S(1)}, u32[]{:S(2)}, u32[]{:S(2)}) %collective-permute-start) | collective-permute-done | bytes 24608 | tf_op jit(solution)/shard_map/ppermute | solution.py:353
  23.4 0.8 %copies.1 = bf16[16,16,768]{2,1,0:T(8,128)(2,1)} custom-call(bf16[16,768]{1,0:T(8,128)(2,1)S(1)} %collective-permute-done.one_ref, f32[16,64,128]{2,1,0:T(8,128)S(1)} %bias_0.1.after_ref.bias_a_hbm), custom_call_target="tpu_custom_call" | custom-call | tf_op jit(solution)/shard_map/copies/pallas_call | solution.py:402
  24.2 0.7 %all-to-all-done.rows_ref = bf16[16,16,768]{2,1,0:T(8,128)(2,1)S(1)} async-done(((bf16[16,16,768]{2,1,0:T(8,128)(2,1)}), bf16[16,16,768]{2,1,0:T(8,128)(2,1)S(1)}, u32[]{:S(2)}, u32[]{:S(2)}) %all-to-all-start) | async-done | bytes 393248 | tf_op jit(solution)/shard_map/all_to_all | solution.py:354
  24.9 6.7 %all-to-all-start.1 = ((bf16[16,16,768]{2,1,0:T(8,128)(2,1)}), bf16[16,16,768]{2,1,0:T(8,128)(2,1)}, u32[]{:S(2)}, u32[]{:S(2)}) async-start(bf16[16,16,768]{2,1,0:T(8,128)(2,1)} %copies.1), calls=%async_computation.1 | async-start | bytes 786432 | tf_op jit(solution)/shard_map/all_to_all | solution.py:411
  31.6 0.0 copy-start.3
  31.6 4.4 %bias_1.1 = (f32[16,64,128]{2,1,0:T(8,128)S(1)}, f32[16,768]{1,0:T(8,128)S(1)}, bf16[768,1536]{1,0:T(8,128)(2,1)S(1)}) custom-call(s32[2]{0:T(128)S(1)} %pad_add_fusion.where_ref, bf16[16,768]{1,0:T(8,128)(2,1)S(1)} %get-tuple-element.12.normed_ref, s32[2048]{0:T(1024)} %refs_0_.3, f32[16]{0:T(128)} %refs_1_.3, s32[16,128]{1,0:T(8,128)} %bitcast.7, ...), custom_call_target="tpu_custom_call" | custom-call | flops 500000000 | bytes 10000000 | tf_op jit(solution)/shard_map/bias_1/pallas_call | solution.py:376
  36.0 0.0 copy-done
  36.0 0.0 copy-start.2
  36.0 0.8 %copy-done.2 = f32[16,64,128]{2,1,0:T(8,128)} copy-done((f32[16,64,128]{2,1,0:T(8,128)}, f32[16,64,128]{2,1,0:T(8,128)S(1)}, u32[]{:S(2)}) %copy-start.2) | copy-done | bytes 524312
  36.8 5.6 %all-to-all-done.1.cols_hbm = bf16[16,16,768]{2,1,0:T(8,128)(2,1)} async-done(((bf16[16,16,768]{2,1,0:T(8,128)(2,1)}), bf16[16,16,768]{2,1,0:T(8,128)(2,1)}, u32[]{:S(2)}, u32[]{:S(2)}) %all-to-all-start.1) | async-done | bytes 393248 | tf_op jit(solution)/shard_map/all_to_all | solution.py:411
  42.4 0.0 copy-done.3
  42.4 0.0 copy-start.1
  42.4 5.1 %attend.1 = bf16[16,104,128]{2,1,0:T(8,128)(2,1)S(1)} custom-call(s32[2]{0:T(128)S(1)} %pad_add_fusion.where_ref, s32[256]{0:T(256)S(1)} %copy-done.3, bf16[16,16,768]{2,1,0:T(8,128)(2,1)S(1)} %all-to-all-done.rows_ref, bf16[16,16,768]{2,1,0:T(8,128)(2,1)} %all-to-all-done.1.cols_hbm, bf16[768,1536]{1,0:T(8,128)(2,1)S(1)} %get-tuple-element.16.wkv_ref, ...), custom_call_target="tpu_custom_call" | custom-call | tf_op jit(solution)/shard_map/attend/pallas_call | solution.py:415
  47.5 18.6 %all_to_all.15.parts_ref = bf16[16,104,128]{2,1,0:T(8,128)(2,1)S(1)} all-to-all(bf16[16,104,128]{2,1,0:T(8,128)(2,1)S(1)} %attend.1), channel_id=1, replica_groups=mesh['qrow'=16,'kcol'=16] {'kcol'}, dimensions={0} | all-to-all | bytes 851968 | tf_op jit(solution)/shard_map/all_to_all | solution.py:430
  66.1 0.0 copy-done.1
  66.1 1.4 %merge.1 = bf16[2,8,768]{2,1,0:T(8,128)(2,1)} custom-call(bf16[16,104,128]{2,1,0:T(8,128)(2,1)S(1)} %all_to_all.15.parts_ref, f32[16,768]{1,0:T(8,128)S(1)} %get-tuple-element.18.gate_ref, bf16[768,768]{1,0:T(8,128)(2,1)S(1)} %copy-done.1), custom_call_target="tpu_custom_call" | custom-call | tf_op jit(solution)/shard_map/merge/pallas_call | solution.py:431
Async XLA Ops:
  1.9 23.0 %all-to-all-start = ((bf16[16,16,768]{2,1,0:T(8,128)(2,1)}), bf16[16,16,768]{2,1,0:T(8,128)(2,1)S(1)}, u32[]{:S(2)}, u32[]{:S(2)}) async-start(bf16[16,16,768]{2,1,0:T(8,128)(2,1)} %get-tuple-element.13), calls=%async_computation | async-start | bytes 786432 | tf_op jit(solution)/shard_map/all_to_all | solution.py:354
  11.4 12.0 %collective-permute-start = (bf16[16,768]{1,0:T(8,128)(2,1)S(1)}, bf16[16,768]{1,0:T(8,128)(2,1)S(1)}, u32[]{:S(2)}, u32[]{:S(2)}) collective-permute-start(bf16[16,768]{1,0:T(8,128)(2,1)S(1)} %get-tuple-element.12.normed_ref), channel_id=1, source_target_pairs={{15,0},{14,16},{12,32},{13,48},{10,64},{8,80},{11,96},{9,112},{5,1... | collective-permute-start | bytes 73736 | tf_op jit(solution)/shard_map/ppermute | solution.py:353
  16.3 19.7 %copy-start = (f32[16,64,128]{2,1,0:T(8,128)}, f32[16,64,128]{2,1,0:T(8,128)S(1)}, u32[]{:S(2)}) copy-start(f32[16,64,128]{2,1,0:T(8,128)S(1)} %bias_0.1.after_ref.bias_a_hbm) | copy-start | bytes 1572868
  24.9 17.5 %all-to-all-start.1 = ((bf16[16,16,768]{2,1,0:T(8,128)(2,1)}), bf16[16,16,768]{2,1,0:T(8,128)(2,1)}, u32[]{:S(2)}, u32[]{:S(2)}) async-start(bf16[16,16,768]{2,1,0:T(8,128)(2,1)} %copies.1), calls=%async_computation.1 | async-start | bytes 786432 | tf_op jit(solution)/shard_map/all_to_all | solution.py:411
  31.6 10.8 %copy-start.3 = (s32[256]{0:T(256)S(1)}, s32[256]{0:T(256)}, u32[]{:S(2)}) copy-start(s32[256]{0:T(256)} %constant.12.order_ref) | copy-start | bytes 3076
  36.0 0.8 %copy-start.2 = (f32[16,64,128]{2,1,0:T(8,128)}, f32[16,64,128]{2,1,0:T(8,128)S(1)}, u32[]{:S(2)}) copy-start(f32[16,64,128]{2,1,0:T(8,128)S(1)} %get-tuple-element.17.bias_b_hbm) | copy-start | bytes 1572868
  42.4 23.7 %copy-start.1 = (bf16[768,768]{1,0:T(8,128)(2,1)S(1)}, bf16[768,768]{1,0:T(8,128)(2,1)}, u32[]{:S(2)}) copy-start(bf16[768,768]{1,0:T(8,128)(2,1)} %wout_ref.1) | copy-start | bytes 3538948

commit v4 on v3

--- a/solution.py
+++ b/solution.py
@@ -358,7 +358,7 @@
     half = row_len // 2
 
     def bias_of(part):
-        out = [shape((heads, half, col_len), F32)]
+        out = [pltpu.HBM((heads, half, col_len), F32)]
         scratch = [
             pltpu.SMEM(chain.shape, jnp.int32),
             pltpu.SMEM((heads,), F32),
@@ -403,10 +403,10 @@
         copies_kernel,
         name="copies",
         out_shape=shape((n_row, own, width), BF),
-        in_specs=[vmem(), pl.BlockSpec(memory_space=pl.ANY)],
+        in_specs=[vmem()] + hbm(1),
         out_specs=vmem(),
         compiler_params=params(4),
-    )(turned, bias_a)
+    )(turned, *stay(bias_a))
     turned_copies, row_tokens = lax.optimization_barrier((turned_copies, row_tokens))
     col_tokens = lax.all_to_all(turned_copies, "qrow", 0, 0)
 
@@ -425,7 +425,7 @@
             dma((3 + n_row,)),
         ],
         compiler_params=params(16),
-    )(where, order, row_tokens, *stay(col_tokens), w_kv, *stay(w_qkvg, bias_a, bias_b))
+    )(where, order, row_tokens, col_tokens, w_kv, *stay(w_qkvg, bias_a, bias_b))
 
     gathered = lax.all_to_all(partial, "kcol", 0, 0)
     return pl.pallas_call(

time: 67.9 us -> 68.1 us (level)
  Pallas kernels: 17.3 us -> 19.2 us
  waiting for transfers between devices: 13.4 us -> 12.5 us
  local copies, waits for them, and re-layouts: 0.79 us -> 0.01 us
    pallas_call x2, Pallas kernels: 8.09 us -> 9.7 us  [bias_of(): pl.pallas_call(functools.partial(bias_kernel, part * half, part), name='b...]
    ppermute x1, waiting for transfers between devices: 7.04 us -> 6.24 us  [shards(): turned = lax.ppermute(normed, ('qrow', 'kcol'), swap)]
    unnamed x8 -> x4, local copies, waits for them, and re-layouts: 0.79 us -> 0.01 us
  transfers between devices with their start and end apart: 3 -> 3, of which waited for: 3 -> 3; matrix products, arithmetic and copies ran while one was open for 0% -> 0% of each run, Pallas kernels for 13% -> 15%
where the time goes in v4:
time: 68.1 us; the launch traced here: 67.7 us
  Pallas kernels  19.2 us (28%)
  blocking collectives  18.6 us (27%)
  starting transfers between devices  17.3 us (25%)
  waiting for transfers between devices  12.5 us (18%)
    all_to_all x1, blocking collectives, shards(): gathered = lax.all_to_all(partial, 'kcol', 0, 0)  18.6 us
    pallas_call x2, Pallas kernels, bias_of(): pl.pallas_call(functools.partial(bias_kernel, part * half, part), name='b...  9.7 us
    all_to_all x1, starting transfers between devices, shards(): row_tokens = lax.all_to_all(copies, 'kcol', 0, 0)  9.5 us
    all_to_all x1, starting transfers between devices, shards(): col_tokens = lax.all_to_all(turned_copies, 'qrow', 0, 0)  6.66 us
    ppermute x1, waiting for transfers between devices, shards(): turned = lax.ppermute(normed, ('qrow', 'kcol'), swap)  6.24 us
    all_to_all x1, waiting for transfers between devices, shards(): col_tokens = lax.all_to_all(turned_copies, 'qrow', 0, 0)  5.53 us
    pallas_call x1, Pallas kernels, shards(): pl.pallas_call(attend_kernel, name='attend', out_shape=shape((n_col, rows...  5.4 us
    pallas_call x1, Pallas kernels, shards(): pl.pallas_call(norm_kernel, name='norm', out_shape=(shape((own, width), B...  1.93 us
  transfers between devices with their start and end apart: 3, of which 3 were waited for; matrix products, arithmetic and copies ran while one was open for 0% of the time, Pallas kernels for 15%

profile of v4, /device:TPU:40, one launch (start us, length us, event | category | flops | bytes accessed | tf_op | source)
XLA Modules:
  0.0 67.7 jit_solution(13513059233673109530)
XLA Ops:
  0.0 1.9 %norm.1 = (bf16[16,768]{1,0:T(8,128)(2,1)S(1)}, bf16[16,16,768]{2,1,0:T(8,128)(2,1)}) custom-call(s32[8]{0:T(128)} %restype_hbm.1, bf16[2,8,768]{2,1,0:T(8,128)(2,1)} %single_hbm.1, bf16[32,768]{1,0:T(8,128)(2,1)} %table_hbm.1, f32[768]{0:T(1024)} %gain_hbm.1), custom_call_target="tpu_custom_call" | custom-call | tf_op jit(solution)/shard_map/norm/pallas_call | solution.py:335
  1.9 9.5 %all-to-all-start = ((bf16[16,16,768]{2,1,0:T(8,128)(2,1)}), bf16[16,16,768]{2,1,0:T(8,128)(2,1)S(1)}, u32[]{:S(2)}, u32[]{:S(2)}) async-start(bf16[16,16,768]{2,1,0:T(8,128)(2,1)} %get-tuple-element.13), calls=%async_computation | async-start | bytes 786432 | tf_op jit(solution)/shard_map/all_to_all | solution.py:354
  11.4 1.1 %collective-permute-start = (bf16[16,768]{1,0:T(8,128)(2,1)S(1)}, bf16[16,768]{1,0:T(8,128)(2,1)S(1)}, u32[]{:S(2)}, u32[]{:S(2)}) collective-permute-start(bf16[16,768]{1,0:T(8,128)(2,1)S(1)} %get-tuple-element.12.normed_ref), channel_id=1, source_target_pairs={{15,0},{14,16},{12,32},{13,48},{10,64},{8,80},{11,96},{9,112},{5,1... | collective-permute-start | bytes 73736 | tf_op jit(solution)/shard_map/ppermute | solution.py:353
  12.5 0.1 pad_add_fusion.where_ref
  12.6 4.5 %bias_0.1.after_ref.bias_a_hbm = f32[16,64,128]{2,1,0:T(8,128)} custom-call(s32[2]{0:T(128)S(1)} %pad_add_fusion.where_ref, bf16[16,768]{1,0:T(8,128)(2,1)S(1)} %get-tuple-element.12.normed_ref, s32[2048]{0:T(1024)} %refs_0_.3, f32[16]{0:T(128)} %refs_1_.3, s32[16,128]{1,0:T(8,128)} %bitcast.6, s32[1,128]{1,0:T(1,128)} %bitcast.10, f32[1,128]{1,0:T(1,128)} %bitcast.12, ...), custom_call_target="tpu_custom_call" | custom-call | flops 500000000 | bytes 10000000 | tf_op jit(solution)/shard_map/bias_0/pallas_call | solution.py:376
  17.2 6.2 %collective-permute-done.one_ref = bf16[16,768]{1,0:T(8,128)(2,1)S(1)} collective-permute-done((bf16[16,768]{1,0:T(8,128)(2,1)S(1)}, bf16[16,768]{1,0:T(8,128)(2,1)S(1)}, u32[]{:S(2)}, u32[]{:S(2)}) %collective-permute-start) | collective-permute-done | bytes 24608 | tf_op jit(solution)/shard_map/ppermute | solution.py:353
  23.4 0.8 %copies.1 = bf16[16,16,768]{2,1,0:T(8,128)(2,1)} custom-call(bf16[16,768]{1,0:T(8,128)(2,1)S(1)} %collective-permute-done.one_ref, f32[16,64,128]{2,1,0:T(8,128)} %bias_0.1.after_ref.bias_a_hbm), custom_call_target="tpu_custom_call" | custom-call | tf_op jit(solution)/shard_map/copies/pallas_call | solution.py:402
  24.2 0.7 %all-to-all-done.rows_ref = bf16[16,16,768]{2,1,0:T(8,128)(2,1)S(1)} async-done(((bf16[16,16,768]{2,1,0:T(8,128)(2,1)}), bf16[16,16,768]{2,1,0:T(8,128)(2,1)S(1)}, u32[]{:S(2)}, u32[]{:S(2)}) %all-to-all-start) | async-done | bytes 393248 | tf_op jit(solution)/shard_map/all_to_all | solution.py:354
  24.9 6.7 %all-to-all-start.1 = ((bf16[16,16,768]{2,1,0:T(8,128)(2,1)}), bf16[16,16,768]{2,1,0:T(8,128)(2,1)S(1)}, u32[]{:S(2)}, u32[]{:S(2)}) async-start(bf16[16,16,768]{2,1,0:T(8,128)(2,1)} %copies.1), calls=%async_computation.1 | async-start | bytes 786432 | tf_op jit(solution)/shard_map/all_to_all | solution.py:411
  31.6 0.0 copy-start.1
  31.6 5.2 %bias_1.1 = (f32[16,64,128]{2,1,0:T(8,128)}, f32[16,768]{1,0:T(8,128)S(1)}, bf16[768,1536]{1,0:T(8,128)(2,1)S(1)}) custom-call(s32[2]{0:T(128)S(1)} %pad_add_fusion.where_ref, bf16[16,768]{1,0:T(8,128)(2,1)S(1)} %get-tuple-element.12.normed_ref, s32[2048]{0:T(1024)} %refs_0_.3, f32[16]{0:T(128)} %refs_1_.3, s32[16,128]{1,0:T(8,128)} %bitcast.7, ...), custom_call_target="tpu_custom_call" | custom-call | flops 500000000 | bytes 10000000 | tf_op jit(solution)/shard_map/bias_1/pallas_call | solution.py:376
  36.8 5.5 %all-to-all-done.1.cols_hbm = bf16[16,16,768]{2,1,0:T(8,128)(2,1)S(1)} async-done(((bf16[16,16,768]{2,1,0:T(8,128)(2,1)}), bf16[16,16,768]{2,1,0:T(8,128)(2,1)S(1)}, u32[]{:S(2)}, u32[]{:S(2)}) %all-to-all-start.1) | async-done | bytes 393248 | tf_op jit(solution)/shard_map/all_to_all | solution.py:411
  42.3 0.0 copy-done.1
  42.3 0.0 copy-start
  42.3 5.4 %attend.1 = bf16[16,104,128]{2,1,0:T(8,128)(2,1)S(1)} custom-call(s32[2]{0:T(128)S(1)} %pad_add_fusion.where_ref, s32[256]{0:T(256)S(1)} %copy-done.1, bf16[16,16,768]{2,1,0:T(8,128)(2,1)S(1)} %all-to-all-done.rows_ref, bf16[16,16,768]{2,1,0:T(8,128)(2,1)S(1)} %all-to-all-done.1.cols_hbm, bf16[768,1536]{1,0:T(8,128)(2,1)S(1)} %get-tuple-element.16.wkv_ref, ...), custom_call_target="tpu_custom_call" | custom-call | tf_op jit(solution)/shard_map/attend/pallas_call | solution.py:415
  47.7 18.6 %all_to_all.15.parts_ref = bf16[16,104,128]{2,1,0:T(8,128)(2,1)S(1)} all-to-all(bf16[16,104,128]{2,1,0:T(8,128)(2,1)S(1)} %attend.1), channel_id=1, replica_groups=mesh['qrow'=16,'kcol'=16] {'kcol'}, dimensions={0} | all-to-all | bytes 851968 | tf_op jit(solution)/shard_map/all_to_all | solution.py:430
  66.3 0.0 copy-done
  66.4 1.4 %merge.1 = bf16[2,8,768]{2,1,0:T(8,128)(2,1)} custom-call(bf16[16,104,128]{2,1,0:T(8,128)(2,1)S(1)} %all_to_all.15.parts_ref, f32[16,768]{1,0:T(8,128)S(1)} %get-tuple-element.18.gate_ref, bf16[768,768]{1,0:T(8,128)(2,1)S(1)} %copy-done), custom_call_target="tpu_custom_call" | custom-call | tf_op jit(solution)/shard_map/merge/pallas_call | solution.py:431
Async XLA Ops:
  1.9 23.0 %all-to-all-start = ((bf16[16,16,768]{2,1,0:T(8,128)(2,1)}), bf16[16,16,768]{2,1,0:T(8,128)(2,1)S(1)}, u32[]{:S(2)}, u32[]{:S(2)}) async-start(bf16[16,16,768]{2,1,0:T(8,128)(2,1)} %get-tuple-element.13), calls=%async_computation | async-start | bytes 786432 | tf_op jit(solution)/shard_map/all_to_all | solution.py:354
  11.4 12.0 %collective-permute-start = (bf16[16,768]{1,0:T(8,128)(2,1)S(1)}, bf16[16,768]{1,0:T(8,128)(2,1)S(1)}, u32[]{:S(2)}, u32[]{:S(2)}) collective-permute-start(bf16[16,768]{1,0:T(8,128)(2,1)S(1)} %get-tuple-element.12.normed_ref), channel_id=1, source_target_pairs={{15,0},{14,16},{12,32},{13,48},{10,64},{8,80},{11,96},{9,112},{5,1... | collective-permute-start | bytes 73736 | tf_op jit(solution)/shard_map/ppermute | solution.py:353
  24.9 17.4 %all-to-all-start.1 = ((bf16[16,16,768]{2,1,0:T(8,128)(2,1)}), bf16[16,16,768]{2,1,0:T(8,128)(2,1)S(1)}, u32[]{:S(2)}, u32[]{:S(2)}) async-start(bf16[16,16,768]{2,1,0:T(8,128)(2,1)} %copies.1), calls=%async_computation.1 | async-start | bytes 786432 | tf_op jit(solution)/shard_map/all_to_all | solution.py:411
  31.6 10.7 %copy-start.1 = (s32[256]{0:T(256)S(1)}, s32[256]{0:T(256)}, u32[]{:S(2)}) copy-start(s32[256]{0:T(256)} %constant.12.order_ref) | copy-start | bytes 3076
  42.3 24.0 %copy-start = (bf16[768,768]{1,0:T(8,128)(2,1)S(1)}, bf16[768,768]{1,0:T(8,128)(2,1)}, u32[]{:S(2)}) copy-start(bf16[768,768]{1,0:T(8,128)(2,1)} %wout_ref.1) | copy-start | bytes 3538948

commit v5 on v4

--- a/solution.py
+++ b/solution.py
@@ -81,15 +81,17 @@
         copies_ref[j] = one_ref[...]
 
 
-def bias_kernel(start, ahead, where_ref, normed_ref, *refs):
-    ins, refs = refs[: 7 + ahead], refs[7 + ahead :]
-    pair_hbm = ins[6]
-    out_ref, refs = refs[0], refs[1:]
-    if ahead:
-        (gate_ref, w_ref), refs = refs[:2], refs[2:]
+def bias_kernel(start, late, tokens_ref, where_ref, *refs):
+    ins, refs = refs[:8], refs[8:]
+    pair_hbm, w_hbm = ins[6:]
+    out_ref, extra_ref, refs = refs[0], refs[1], refs[2:]
+    if late:
+        w_ref, refs = refs[0], refs[1:]
     chain_ref, cbias_ref, chain_rows_ref, live_ref, gain_ref, weight_ref, pair_ref, sems, pair_sems = refs[:9]
+    mine_ref, w_sems = refs[9:]
     chunks, block, keys, channels = pair_ref.shape
     heads = weight_ref.shape[0]
+    width = mine_ref.shape[0]
     loads = [
         pltpu.make_async_copy(pair_hbm.at[pl.ds(start + i * block, block)], pair_ref.at[i], pair_sems.at[i])
         for i in range(chunks)
@@ -100,13 +102,11 @@
     small = [pltpu.make_async_copy(src, dst, sems.at[i]) for i, (src, dst) in enumerate(small)]
     for load in small + loads[2:]:
         load.start()
-    if ahead:
-        width = normed_ref.shape[1]
-        wg_ref, w_sems = refs[9:]
-        w_hbm = ins[7]
-        load_g = pltpu.make_async_copy(w_hbm.at[:, pl.ds(3 * width, width)], wg_ref, w_sems.at[0])
+    own = 0 if late else 3 * width
+    load_mine = pltpu.make_async_copy(w_hbm.at[:, pl.ds(own, width)], mine_ref, w_sems.at[0])
+    load_mine.start()
+    if late:
         load_w = pltpu.make_async_copy(w_hbm.at[:, pl.ds(width, 2 * width)], w_ref, w_sems.at[1])
-        load_g.start()
         load_w.start()
     for load in small:
         load.wait()
@@ -137,56 +137,43 @@
                 same = col_chain == chain_ref[base + at]
                 part = part + jnp.where(same, column, 0.0)
                 out_ref[:, at, :] = jnp.where(alive, part, -1e30)
-    if ahead:
-        load_g.wait()
-        pre = jnp.dot(normed_ref[...], wg_ref[...], preferred_element_type=F32)
-        gate_ref[...] = jax.nn.sigmoid(pre)
+    load_mine.wait()
+    parts, per, _ = tokens_ref.shape
+    res = jnp.dot(tokens_ref[...].reshape(parts * per, width), mine_ref[...], preferred_element_type=F32)
+    if late:
+        res = res.reshape(parts, 2, per // 2, width)
+        for s in range(2):
+            extra_ref[s] = res[:, s].reshape(parts * per // 2, width).astype(BF)
         load_w.wait()
+    else:
+        extra_ref[...] = jax.nn.sigmoid(res)
 
 
 def attend_kernel(
-    where_ref,
-    order_ref,
-    rows_ref,
-    cols_hbm,
-    wkv_ref,
-    w_hbm,
-    bias_a_hbm,
-    bias_b_hbm,
-    out_ref,
-    x_ref,
-    wq_ref,
-    bias_ref,
-    sems,
+    where_ref, order_ref, cols_ref, wkv_ref, q_ref, bias_a_hbm, bias_b_hbm, out_ref, x_ref, bias_ref, sems
 ):
-    parts, per, width = rows_ref.shape
+    parts, per, width = cols_ref.shape
     half = per // 2
     heads, queries, keys = bias_ref.shape
     few = queries // 2
     size = width // heads
     scale = 1.0 / math.sqrt(size)
     loads = [
-        pltpu.make_async_copy(w_hbm.at[:, pl.ds(0, width)], wq_ref, sems.at[0]),
-        pltpu.make_async_copy(bias_a_hbm, bias_ref.at[:, pl.ds(0, few)], sems.at[1]),
-        pltpu.make_async_copy(bias_b_hbm, bias_ref.at[:, pl.ds(few, few)], sems.at[2]),
+        pltpu.make_async_copy(bias_a_hbm, bias_ref.at[:, pl.ds(0, few)], sems.at[0]),
+        pltpu.make_async_copy(bias_b_hbm, bias_ref.at[:, pl.ds(few, few)], sems.at[1]),
     ]
-    tokens = [
-        pltpu.make_async_copy(cols_hbm.at[i], x_ref.at[order_ref[where_ref[1] * parts + i]], sems.at[3 + i])
-        for i in range(parts)
-    ]
-    for load in tokens + loads:
+    for load in loads:
         load.start()
-    for load in tokens:
-        load.wait()
-
-    def project(tokens, w):
-        x = tokens[...].reshape(parts * per, width)
+    for i in range(parts):
+        x_ref[pl.ds(order_ref[where_ref[1] * parts + i], 1)] = cols_ref[pl.ds(i, 1)]
+    x = x_ref[...].reshape(parts * per, width)
+
+    def project(w):
         return jnp.dot(x, w, preferred_element_type=F32).reshape(parts, 2, half, width)
 
-    kf, vf = project(x_ref, wkv_ref[:, :width]), project(x_ref, wkv_ref[:, width:])
+    kf, vf = project(wkv_ref[:, :width]), project(wkv_ref[:, width:])
     for load in loads:
         load.wait()
-    qf = project(rows_ref, wq_ref[...])
     span = 256
     wins = width // span
 
@@ -200,7 +187,7 @@
     lane = lax.broadcasted_iota(jnp.int32, (queries, 128), 1)
     stats = jnp.zeros((queries, 128), F32)
     for s in range(2):
-        q = qf[:, s].reshape(queries, width).astype(BF)
+        q = q_ref[s]
         k = kf[:, s].reshape(keys, width).astype(BF)
         v = vf[:, s].reshape(keys, width).astype(BF)
         raw = {}
@@ -357,34 +344,34 @@
     chunks = 4
     half = row_len // 2
 
-    def bias_of(part):
+    def bias_of(late, tokens):
         out = [pltpu.HBM((heads, half, col_len), F32)]
-        scratch = [
-            pltpu.SMEM(chain.shape, jnp.int32),
-            pltpu.SMEM((heads,), F32),
-            pltpu.VMEM((chain.shape[0] // col_len, col_len), jnp.int32),
-            pltpu.VMEM((1, col_len), jnp.int32),
-            pltpu.VMEM((1, channels), F32),
-            pltpu.VMEM((heads, channels), F32),
-            pltpu.VMEM((chunks, half // chunks, col_len, channels), BF),
-            dma((6,)),
-            dma((chunks,)),
-        ]
-        if part:
-            out += [shape((own, width), F32), shape((width, 2 * width), BF)]
-            scratch += [pltpu.VMEM((width, width), BF), dma((2,))]
+        out += [shape((samples, row_len, width), BF) if late else pltpu.HBM((own, width), F32)]
+        out += [shape((width, 2 * width), BF)] * late
         return pl.pallas_call(
-            functools.partial(bias_kernel, part * half, part),
-            name="bias_" + str(part),
+            functools.partial(bias_kernel, late * half, late),
+            name="bias_" + str(late),
             out_shape=out,
-            in_specs=[smem(), vmem()] + hbm(7 + part),
+            in_specs=[vmem(), smem()] + hbm(8),
             out_specs=[vmem()] * len(out),
-            scratch_shapes=scratch,
-            compiler_params=params(12 if part else 6),
+            scratch_shapes=[
+                pltpu.SMEM(chain.shape, jnp.int32),
+                pltpu.SMEM((heads,), F32),
+                pltpu.VMEM((chain.shape[0] // col_len, col_len), jnp.int32),
+                pltpu.VMEM((1, col_len), jnp.int32),
+                pltpu.VMEM((1, channels), F32),
+                pltpu.VMEM((heads, channels), F32),
+                pltpu.VMEM((chunks, half // chunks, col_len, channels), BF),
+                dma((6,)),
+                dma((chunks,)),
+                pltpu.VMEM((width, width), BF),
+                dma((2,)),
+            ],
+            compiler_params=params(12 if late else 8),
             cost_estimate=pl.CostEstimate(flops=5 * 10**8, bytes_accessed=10 * 10**6, transcendentals=0),
         )(
+            tokens,
             where,
-            normed,
             *stay(
                 chain,
                 chain_bias,
@@ -393,12 +380,12 @@
                 pair_gain.reshape(1, channels),
                 pair_weight.T,
                 pair,
-                *[w_qkvg][:part],
+                w_qkvg,
             ),
         )
 
-    (bias_a,) = bias_of(0)
-    bias_b, gate, w_kv = bias_of(1)
+    bias_a, gate = bias_of(0, normed[None])
+    bias_b, queries, w_kv = bias_of(1, row_tokens)
     turned_copies = pl.pallas_call(
         copies_kernel,
         name="copies",
@@ -416,16 +403,15 @@
         attend_kernel,
         name="attend",
         out_shape=shape((n_col, rows, 128), BF),
-        in_specs=[smem()] * 2 + [vmem()] + hbm(1) + [vmem()] + hbm(3),
+        in_specs=[smem()] * 2 + [vmem()] * 3 + hbm(2),
         out_specs=vmem(),
         scratch_shapes=[
             pltpu.VMEM(col_tokens.shape, BF),
-            pltpu.VMEM((width, width), BF),
             pltpu.VMEM((heads, row_len, col_len), F32),
-            dma((3 + n_row,)),
+            dma((2,)),
         ],
         compiler_params=params(16),
-    )(where, order, row_tokens, col_tokens, w_kv, *stay(w_qkvg, bias_a, bias_b))
+    )(where, order, col_tokens, w_kv, queries, *stay(bias_a, bias_b))
 
     gathered = lax.all_to_all(partial, "kcol", 0, 0)
     return pl.pallas_call(

time: 68.1 us -> 67.2 us (0.987)
    pallas_call x1, Pallas kernels: 5.4 us -> 4.53 us  [shards(): pl.pallas_call(attend_kernel, name='attend', out_shape=shape((n_col, rows...]
  transfers between devices with their start and end apart: 3 -> 3, of which waited for: 3 -> 3; matrix products, arithmetic and copies ran while one was open for 0% -> 0% of each run, Pallas kernels for 15% -> 16%
where the time goes in v5:
time: 67.2 us; the launch traced here: 66.8 us
  Pallas kernels  18.6 us (28%)
  blocking collectives  18.6 us (28%)
  starting transfers between devices  17.3 us (26%)
  waiting for transfers between devices  12.2 us (18%)
    all_to_all x1, blocking collectives, shards(): gathered = lax.all_to_all(partial, 'kcol', 0, 0)  18.6 us
    pallas_call x2, Pallas kernels, bias_of(): pl.pallas_call(functools.partial(bias_kernel, late * half, late), name='b...  10 us
    all_to_all x1, starting transfers between devices, shards(): row_tokens = lax.all_to_all(copies, 'kcol', 0, 0)  9.5 us
    all_to_all x1, starting transfers between devices, shards(): col_tokens = lax.all_to_all(turned_copies, 'qrow', 0, 0)  6.66 us
    ppermute x1, waiting for transfers between devices, shards(): turned = lax.ppermute(normed, ('qrow', 'kcol'), swap)  6.12 us
    all_to_all x1, waiting for transfers between devices, shards(): col_tokens = lax.all_to_all(turned_copies, 'qrow', 0, 0)  5.34 us
    pallas_call x1, Pallas kernels, shards(): pl.pallas_call(attend_kernel, name='attend', out_shape=shape((n_col, rows...  4.53 us
    pallas_call x1, Pallas kernels, shards(): pl.pallas_call(norm_kernel, name='norm', out_shape=(shape((own, width), B...  1.92 us
  transfers between devices with their start and end apart: 3, of which 3 were waited for; matrix products, arithmetic and copies ran while one was open for 0% of the time, Pallas kernels for 16%

profile of v5, /device:TPU:40, one launch (start us, length us, event | category | flops | bytes accessed | tf_op | source)
XLA Modules:
  0.0 66.8 jit_solution(15284265122357702782)
XLA Ops:
  0.0 1.9 %norm.1 = (bf16[16,768]{1,0:T(8,128)(2,1)S(1)}, bf16[16,16,768]{2,1,0:T(8,128)(2,1)}) custom-call(s32[8]{0:T(128)} %restype_hbm.1, bf16[2,8,768]{2,1,0:T(8,128)(2,1)} %single_hbm.1, bf16[32,768]{1,0:T(8,128)(2,1)} %table_hbm.1, f32[768]{0:T(1024)} %gain_hbm.1), custom_call_target="tpu_custom_call" | custom-call | tf_op jit(solution)/shard_map/norm/pallas_call | solution.py:322
  1.9 9.5 %all-to-all-start = ((bf16[16,16,768]{2,1,0:T(8,128)(2,1)}), bf16[16,16,768]{2,1,0:T(8,128)(2,1)S(1)}, u32[]{:S(2)}, u32[]{:S(2)}) async-start(bf16[16,16,768]{2,1,0:T(8,128)(2,1)} %get-tuple-element.15), calls=%async_computation | async-start | bytes 786432 | tf_op jit(solution)/shard_map/all_to_all | solution.py:341
  11.4 1.1 %collective-permute-start = (bf16[16,768]{1,0:T(8,128)(2,1)S(1)}, bf16[16,768]{1,0:T(8,128)(2,1)S(1)}, u32[]{:S(2)}, u32[]{:S(2)}) collective-permute-start(bf16[16,768]{1,0:T(8,128)(2,1)S(1)} %get-tuple-element.13), channel_id=1, source_target_pairs={{15,0},{14,16},{12,32},{13,48},{10,64},{8,80},{11,96},{9,112},{5,1... | collective-permute-start | bytes 73736 | tf_op jit(solution)/shard_map/ppermute | solution.py:340
  12.5 0.1 pad_add_fusion.where_ref
  12.6 4.7 %bias_0.1 = (f32[16,64,128]{2,1,0:T(8,128)}, f32[16,768]{1,0:T(8,128)}) custom-call(bf16[1,16,768]{2,1,0:T(8,128)(2,1)S(1)} %bitcast.7, s32[2]{0:T(128)S(1)} %pad_add_fusion.where_ref, s32[2048]{0:T(1024)} %refs_0_.3, f32[16]{0:T(128)} %refs_1_.3, s32[16,128]{1,0:T(8,128)} %bitcast.8, s32[1,128]{1,0:T(1,128)} %bitcast.12, f32[1,128]{1,0:T(1,128)} %bitcast.14, ...), custom_call_target="tpu_custom_call" | custom-call | flops 500000000 | bytes 10000000 | tf_op jit(solution)/shard_map/bias_0/pallas_call | solution.py:351
  17.3 6.1 %collective-permute-done.one_ref = bf16[16,768]{1,0:T(8,128)(2,1)S(1)} collective-permute-done((bf16[16,768]{1,0:T(8,128)(2,1)S(1)}, bf16[16,768]{1,0:T(8,128)(2,1)S(1)}, u32[]{:S(2)}, u32[]{:S(2)}) %collective-permute-start) | collective-permute-done | bytes 24608 | tf_op jit(solution)/shard_map/ppermute | solution.py:340
  23.4 0.8 %copies.1 = bf16[16,16,768]{2,1,0:T(8,128)(2,1)} custom-call(bf16[16,768]{1,0:T(8,128)(2,1)S(1)} %collective-permute-done.one_ref, f32[16,64,128]{2,1,0:T(8,128)} %get-tuple-element.14.after_ref.bias_a_hbm), custom_call_target="tpu_custom_call" | custom-call | tf_op jit(solution)/shard_map/copies/pallas_call | solution.py:389
  24.2 0.7 %all-to-all-done.tokens_ref = bf16[16,16,768]{2,1,0:T(8,128)(2,1)S(1)} async-done(((bf16[16,16,768]{2,1,0:T(8,128)(2,1)}), bf16[16,16,768]{2,1,0:T(8,128)(2,1)S(1)}, u32[]{:S(2)}, u32[]{:S(2)}) %all-to-all-start) | async-done | bytes 393248 | tf_op jit(solution)/shard_map/all_to_all | solution.py:341
  24.9 6.7 %all-to-all-start.1 = ((bf16[16,16,768]{2,1,0:T(8,128)(2,1)}), bf16[16,16,768]{2,1,0:T(8,128)(2,1)S(1)}, u32[]{:S(2)}, u32[]{:S(2)}) async-start(bf16[16,16,768]{2,1,0:T(8,128)(2,1)} %copies.1), calls=%async_computation.1 | async-start | bytes 786432 | tf_op jit(solution)/shard_map/all_to_all | solution.py:398
  31.6 0.0 copy-start.2
  31.6 5.3 %bias_1.1 = (f32[16,64,128]{2,1,0:T(8,128)}, bf16[2,128,768]{2,1,0:T(8,128)(2,1)S(1)}, bf16[768,1536]{1,0:T(8,128)(2,1)S(1)}) custom-call(bf16[16,16,768]{2,1,0:T(8,128)(2,1)S(1)} %all-to-all-done.tokens_ref, s32[2]{0:T(128)S(1)} %pad_add_fusion.where_ref, s32[2048]{0:T(1024)} %refs_0_.3, f32[16]{0:T(128)} %refs_1_.3, s32[16,128]{1,0:T(8,128)} %bitcast.9, ...), custom_call_target="tpu_custom_call" | custom-call | flops 500000000 | bytes 10000000 | tf_op jit(solution)/shard_map/bias_1/pallas_call | solution.py:351
  37.0 0.0 copy-start.1
  37.0 5.3 %all-to-all-done.1.cols_ref = bf16[16,16,768]{2,1,0:T(8,128)(2,1)S(1)} async-done(((bf16[16,16,768]{2,1,0:T(8,128)(2,1)}), bf16[16,16,768]{2,1,0:T(8,128)(2,1)S(1)}, u32[]{:S(2)}, u32[]{:S(2)}) %all-to-all-start.1) | async-done | bytes 393248 | tf_op jit(solution)/shard_map/all_to_all | solution.py:398
  42.3 0.0 copy-start
  42.3 0.0 copy-done.2
  42.3 4.5 %attend.1 = bf16[16,104,128]{2,1,0:T(8,128)(2,1)S(1)} custom-call(s32[2]{0:T(128)S(1)} %pad_add_fusion.where_ref, s32[256]{0:T(256)S(1)} %copy-done.2, bf16[16,16,768]{2,1,0:T(8,128)(2,1)S(1)} %all-to-all-done.1.cols_ref, bf16[768,1536]{1,0:T(8,128)(2,1)S(1)} %get-tuple-element.17.wkv_ref, bf16[2,128,768]{2,1,0:T(8,128)(2,1)S(1)} %get-tuple-element.18.q_ref, ...), custom_call_target="tpu_custom_call" | custom-call | tf_op jit(solution)/shard_map/attend/pallas_call | solution.py:402
  46.8 18.6 %all_to_all.15.parts_ref = bf16[16,104,128]{2,1,0:T(8,128)(2,1)S(1)} all-to-all(bf16[16,104,128]{2,1,0:T(8,128)(2,1)S(1)} %attend.1), channel_id=1, replica_groups=mesh['qrow'=16,'kcol'=16] {'kcol'}, dimensions={0} | all-to-all | bytes 851968 | tf_op jit(solution)/shard_map/all_to_all | solution.py:416
  65.5 0.0 copy-done.1
  65.5 0.0 copy-done
  65.5 1.4 %merge.1 = bf16[2,8,768]{2,1,0:T(8,128)(2,1)} custom-call(bf16[16,104,128]{2,1,0:T(8,128)(2,1)S(1)} %all_to_all.15.parts_ref, f32[16,768]{1,0:T(8,128)S(1)} %copy-done.1, bf16[768,768]{1,0:T(8,128)(2,1)S(1)} %copy-done), custom_call_target="tpu_custom_call" | custom-call | tf_op jit(solution)/shard_map/merge/pallas_call | solution.py:417
Async XLA Ops:
  1.9 23.0 %all-to-all-start = ((bf16[16,16,768]{2,1,0:T(8,128)(2,1)}), bf16[16,16,768]{2,1,0:T(8,128)(2,1)S(1)}, u32[]{:S(2)}, u32[]{:S(2)}) async-start(bf16[16,16,768]{2,1,0:T(8,128)(2,1)} %get-tuple-element.15), calls=%async_computation | async-start | bytes 786432 | tf_op jit(solution)/shard_map/all_to_all | solution.py:341
  11.4 12.0 %collective-permute-start = (bf16[16,768]{1,0:T(8,128)(2,1)S(1)}, bf16[16,768]{1,0:T(8,128)(2,1)S(1)}, u32[]{:S(2)}, u32[]{:S(2)}) collective-permute-start(bf16[16,768]{1,0:T(8,128)(2,1)S(1)} %get-tuple-element.13), channel_id=1, source_target_pairs={{15,0},{14,16},{12,32},{13,48},{10,64},{8,80},{11,96},{9,112},{5,1... | collective-permute-start | bytes 73736 | tf_op jit(solution)/shard_map/ppermute | solution.py:340
  24.9 17.4 %all-to-all-start.1 = ((bf16[16,16,768]{2,1,0:T(8,128)(2,1)}), bf16[16,16,768]{2,1,0:T(8,128)(2,1)S(1)}, u32[]{:S(2)}, u32[]{:S(2)}) async-start(bf16[16,16,768]{2,1,0:T(8,128)(2,1)} %copies.1), calls=%async_computation.1 | async-start | bytes 786432 | tf_op jit(solution)/shard_map/all_to_all | solution.py:398
  31.6 10.7 %copy-start.2 = (s32[256]{0:T(256)S(1)}, s32[256]{0:T(256)}, u32[]{:S(2)}) copy-start(s32[256]{0:T(256)} %constant.12.order_ref) | copy-start | bytes 3076
  37.0 28.5 %copy-start.1 = (f32[16,768]{1,0:T(8,128)S(1)}, f32[16,768]{1,0:T(8,128)}, u32[]{:S(2)}) copy-start(f32[16,768]{1,0:T(8,128)} %get-tuple-element.20.gate_ref) | copy-start | bytes 147460
  42.3 23.2 %copy-start = (bf16[768,768]{1,0:T(8,128)(2,1)S(1)}, bf16[768,768]{1,0:T(8,128)(2,1)}, u32[]{:S(2)}) copy-start(bf16[768,768]{1,0:T(8,128)(2,1)} %wout_ref.1) | copy-start | bytes 3538948

commit v6 on v5

--- a/solution.py
+++ b/solution.py
@@ -76,22 +76,22 @@
         copies_ref[j] = normed
 
 
-def copies_kernel(one_ref, after_ref, copies_ref):
-    for j in range(copies_ref.shape[0]):
-        copies_ref[j] = one_ref[...]
-
-
-def bias_kernel(start, late, tokens_ref, where_ref, *refs):
+def pack_kernel(cols_ref, own_ref, after_ref, out_ref):
+    per = own_ref.shape[0]
+    for c in range(out_ref.shape[0]):
+        out_ref[c, :per] = cols_ref[c]
+        out_ref[c, per:] = own_ref[...]
+
+
+def bias_kernel(start, late, own_ref, where_ref, *refs):
     ins, refs = refs[:8], refs[8:]
     pair_hbm, w_hbm = ins[6:]
     out_ref, extra_ref, refs = refs[0], refs[1], refs[2:]
-    if late:
-        w_ref, refs = refs[0], refs[1:]
     chain_ref, cbias_ref, chain_rows_ref, live_ref, gain_ref, weight_ref, pair_ref, sems, pair_sems = refs[:9]
-    mine_ref, w_sems = refs[9:]
+    w_ref, w_sem = refs[9:] if not late else (extra_ref, refs[9])
     chunks, block, keys, channels = pair_ref.shape
     heads = weight_ref.shape[0]
-    width = mine_ref.shape[0]
+    width = own_ref.shape[1]
     loads = [
         pltpu.make_async_copy(pair_hbm.at[pl.ds(start + i * block, block)], pair_ref.at[i], pair_sems.at[i])
         for i in range(chunks)
@@ -102,12 +102,9 @@
     small = [pltpu.make_async_copy(src, dst, sems.at[i]) for i, (src, dst) in enumerate(small)]
     for load in small + loads[2:]:
         load.start()
-    own = 0 if late else 3 * width
-    load_mine = pltpu.make_async_copy(w_hbm.at[:, pl.ds(own, width)], mine_ref, w_sems.at[0])
-    load_mine.start()
-    if late:
-        load_w = pltpu.make_async_copy(w_hbm.at[:, pl.ds(width, 2 * width)], w_ref, w_sems.at[1])
-        load_w.start()
+    place = pl.ds(width, 2 * width) if late else pl.ds(3 * width, width)
+    load_w = pltpu.make_async_copy(w_hbm.at[:, place], w_ref, w_sem.at[0])
+    load_w.start()
     for load in small:
         load.wait()
     weight = weight_ref[...] * gain_ref[...]
@@ -137,42 +134,36 @@
                 same = col_chain == chain_ref[base + at]
                 part = part + jnp.where(same, column, 0.0)
                 out_ref[:, at, :] = jnp.where(alive, part, -1e30)
-    load_mine.wait()
-    parts, per, _ = tokens_ref.shape
-    res = jnp.dot(tokens_ref[...].reshape(parts * per, width), mine_ref[...], preferred_element_type=F32)
-    if late:
-        res = res.reshape(parts, 2, per // 2, width)
-        for s in range(2):
-            extra_ref[s] = res[:, s].reshape(parts * per // 2, width).astype(BF)
-        load_w.wait()
-    else:
-        extra_ref[...] = jax.nn.sigmoid(res)
-
-
-def attend_kernel(
-    where_ref, order_ref, cols_ref, wkv_ref, q_ref, bias_a_hbm, bias_b_hbm, out_ref, x_ref, bias_ref, sems
-):
-    parts, per, width = cols_ref.shape
+    load_w.wait()
+    if not late:
+        pre = jnp.dot(own_ref[...], w_ref[...], preferred_element_type=F32)
+        extra_ref[...] = jax.nn.sigmoid(pre)
+
+
+def attend_kernel(tokens_ref, wkv_ref, w_hbm, bias_a_hbm, bias_b_hbm, out_ref, wq_ref, bias_ref, sems):
+    parts, per, width = tokens_ref.shape
+    per = per // 2
     half = per // 2
     heads, queries, keys = bias_ref.shape
     few = queries // 2
     size = width // heads
     scale = 1.0 / math.sqrt(size)
     loads = [
-        pltpu.make_async_copy(bias_a_hbm, bias_ref.at[:, pl.ds(0, few)], sems.at[0]),
-        pltpu.make_async_copy(bias_b_hbm, bias_ref.at[:, pl.ds(few, few)], sems.at[1]),
+        pltpu.make_async_copy(w_hbm.at[:, pl.ds(0, width)], wq_ref, sems.at[0]),
+        pltpu.make_async_copy(bias_a_hbm, bias_ref.at[:, pl.ds(0, few)], sems.at[1]),
+        pltpu.make_async_copy(bias_b_hbm, bias_ref.at[:, pl.ds(few, few)], sems.at[2]),
     ]
     for load in loads:
         load.start()
-    for i in range(parts):
-        x_ref[pl.ds(order_ref[where_ref[1] * parts + i], 1)] = cols_ref[pl.ds(i, 1)]
-    x = x_ref[...].reshape(parts * per, width)
-
-    def project(w):
+
+    def project(at, w):
+        x = tokens_ref[:, at : at + per].reshape(parts * per, width)
         return jnp.dot(x, w, preferred_element_type=F32).reshape(parts, 2, half, width)
 
-    kf, vf = project(wkv_ref[:, :width]), project(wkv_ref[:, width:])
-    for load in loads:
+    kf, vf = project(0, wkv_ref[:, :width]), project(0, wkv_ref[:, width:])
+    loads[0].wait()
+    qf = project(per, wq_ref[...])
+    for load in loads[1:]:
         load.wait()
     span = 256
     wins = width // span
@@ -187,7 +178,7 @@
     lane = lax.broadcasted_iota(jnp.int32, (queries, 128), 1)
     stats = jnp.zeros((queries, 128), F32)
     for s in range(2):
-        q = q_ref[s]
+        q = qf[:, s].reshape(queries, width).astype(BF)
         k = kf[:, s].reshape(keys, width).astype(BF)
         v = vf[:, s].reshape(keys, width).astype(BF)
         raw = {}
@@ -261,36 +252,6 @@
     out_ref[...] = update.reshape(out_ref.shape).astype(BF)
 
 
-def near_swap(n):
-    ring = lambda a, b, size: min((a - b) % size, (b - a) % size)
-    table = []
-    for c in range(n):
-        cx, cyh, cco = c // 4, c // 2 % 2, c % 2
-        cyl, cz = c // 8, c % 8
-
-        def cost(j, i):
-            hops = ring(cx, i // 4, 4) + ring(j % 8, cz, 8)
-            hops += ring(cyh * 2 + j // 8, (i // 2 % 2) * 2 + cyl, 4)
-            return 2 * hops + (cco != i % 2)
-
-        for most in range(100):
-            taken = {}
-
-            def place(j, seen):
-                for i in range(n):
-                    if cost(j, i) <= most and i not in seen:
-                        seen.add(i)
-                        if i not in taken or place(taken[i], seen):
-                            taken[i] = j
-                            return True
-                return False
-
-            if all(place(j, set()) for j in range(n)):
-                break
-        table.append([taken[i] for i in range(n)])
-    return table
-
-
 def params(mib):
     return pltpu.CompilerParams(vmem_limit_bytes=mib << 20)
 
@@ -322,7 +283,7 @@
     normed, copies = pl.pallas_call(
         norm_kernel,
         name="norm",
-        out_shape=(shape((own, width), BF), shape((n_col, own, width), BF)),
+        out_shape=(shape((own, width), BF), shape((n_row, own, width), BF)),
         in_specs=hbm(4),
         out_specs=(vmem(), vmem()),
         scratch_shapes=[
@@ -335,19 +296,14 @@
         compiler_params=params(4),
     )(*stay(restype, single, restype_table, single_gain))
 
-    table = near_swap(n_row)
-    swap = [(c * n_col + j, i * n_col + c) for c in range(n_row) for i, j in enumerate(table[c])]
-    turned = lax.ppermute(normed, ("qrow", "kcol"), swap)
-    row_tokens = lax.all_to_all(copies, "kcol", 0, 0)
-
+    col_tokens = lax.all_to_all(copies, "qrow", 0, 0)
     where = jnp.stack([lax.axis_index("qrow"), lax.axis_index("kcol")]).astype(jnp.int32)
     chunks = 4
     half = row_len // 2
 
-    def bias_of(late, tokens):
+    def bias_of(late):
         out = [pltpu.HBM((heads, half, col_len), F32)]
-        out += [shape((samples, row_len, width), BF) if late else pltpu.HBM((own, width), F32)]
-        out += [shape((width, 2 * width), BF)] * late
+        out += [shape((width, 2 * width), BF) if late else pltpu.HBM((own, width), F32)]
         return pl.pallas_call(
             functools.partial(bias_kernel, late * half, late),
             name="bias_" + str(late),
@@ -364,13 +320,13 @@
                 pltpu.VMEM((chunks, half // chunks, col_len, channels), BF),
                 dma((6,)),
                 dma((chunks,)),
-                pltpu.VMEM((width, width), BF),
-                dma((2,)),
-            ],
-            compiler_params=params(12 if late else 8),
+            ]
+            + ([] if late else [pltpu.VMEM((width, width), BF)])
+            + [dma((1,))],
+            compiler_params=params(8),
             cost_estimate=pl.CostEstimate(flops=5 * 10**8, bytes_accessed=10 * 10**6, transcendentals=0),
         )(
-            tokens,
+            normed,
             where,
             *stay(
                 chain,
@@ -384,34 +340,32 @@
             ),
         )
 
-    bias_a, gate = bias_of(0, normed[None])
-    bias_b, queries, w_kv = bias_of(1, row_tokens)
-    turned_copies = pl.pallas_call(
-        copies_kernel,
-        name="copies",
-        out_shape=shape((n_row, own, width), BF),
-        in_specs=[vmem()] + hbm(1),
+    bias_a, gate = bias_of(0)
+    bias_b, w_kv = bias_of(1)
+    packed = pl.pallas_call(
+        pack_kernel,
+        name="pack",
+        out_shape=shape((n_col, 2 * own, width), BF),
+        in_specs=[vmem(), vmem()] + hbm(1),
         out_specs=vmem(),
-        compiler_params=params(4),
-    )(turned, *stay(bias_a))
-    turned_copies, row_tokens = lax.optimization_barrier((turned_copies, row_tokens))
-    col_tokens = lax.all_to_all(turned_copies, "qrow", 0, 0)
-
-    order = jnp.asarray(table, jnp.int32).reshape(-1)
+        compiler_params=params(6),
+    )(col_tokens, normed, *stay(bias_a))
+    tokens = lax.all_to_all(packed, "kcol", 0, 0)
+
     rows = own * width // 128 + tok
     partial = pl.pallas_call(
         attend_kernel,
         name="attend",
         out_shape=shape((n_col, rows, 128), BF),
-        in_specs=[smem()] * 2 + [vmem()] * 3 + hbm(2),
+        in_specs=[vmem()] * 2 + hbm(3),
         out_specs=vmem(),
         scratch_shapes=[
-            pltpu.VMEM(col_tokens.shape, BF),
+            pltpu.VMEM((width, width), BF),
             pltpu.VMEM((heads, row_len, col_len), F32),
-            dma((2,)),
+            dma((3,)),
         ],
         compiler_params=params(16),
-    )(where, order, col_tokens, w_kv, queries, *stay(bias_a, bias_b))
+    )(tokens, w_kv, *stay(w_qkvg, bias_a, bias_b))
 
     gathered = lax.all_to_all(partial, "kcol", 0, 0)
     return pl.pallas_call(

time: 67.2 us -> 74.2 us (1.10)
  waiting for transfers between devices: 12.2 us -> 22 us
  starting transfers between devices: 17.3 us -> 15.6 us
  Pallas kernels: 18.6 us -> 17.7 us
    all_to_all x2, waiting for transfers between devices: 6.08 us -> 22 us  [the longest x1 16 us: shards(): tokens = lax.all_to_all(packed, 'kcol', 0, 0)]
    ppermute x1 -> x0, waiting for transfers between devices: 6.12 us -> none  [shards(): turned = lax.ppermute(normed, ('qrow', 'kcol'), swap)]
    ppermute x1 -> x0, starting transfers between devices: 1.1 us -> none  [shards(): turned = lax.ppermute(normed, ('qrow', 'kcol'), swap)]
    pallas_call x2, Pallas kernels: 10 us -> 9.18 us  [bias_of(): pl.pallas_call(functools.partial(bias_kernel, late * half, late), name='b...]
  transfers between devices with their start and end apart: 3 -> 2, of which waited for: 3 -> 2; matrix products, arithmetic and copies ran while one was open for 0% -> 0% of each run, Pallas kernels for 16% -> 12%
where the time goes in v6:
time: 74.2 us; the launch traced here: 73.8 us
  waiting for transfers between devices  22 us (30%)
  blocking collectives  18.4 us (25%)
  Pallas kernels  17.7 us (24%)
  starting transfers between devices  15.6 us (21%)
    all_to_all x1, blocking collectives, shards(): gathered = lax.all_to_all(partial, 'kcol', 0, 0)  18.4 us
    all_to_all x1, waiting for transfers between devices, shards(): tokens = lax.all_to_all(packed, 'kcol', 0, 0)  16 us
    all_to_all x1, starting transfers between devices, shards(): tokens = lax.all_to_all(packed, 'kcol', 0, 0)  9.49 us
    pallas_call x2, Pallas kernels, bias_of(): pl.pallas_call(functools.partial(bias_kernel, late * half, late), name='b...  9.18 us
    all_to_all x1, starting transfers between devices, shards(): col_tokens = lax.all_to_all(copies, 'qrow', 0, 0)  6.15 us
    all_to_all x1, waiting for transfers between devices, shards(): col_tokens = lax.all_to_all(copies, 'qrow', 0, 0)  5.94 us
    pallas_call x1, Pallas kernels, shards(): pl.pallas_call(attend_kernel, name='attend', out_shape=shape((n_col, rows...  4.26 us
    pallas_call x1, Pallas kernels, shards(): pl.pallas_call(norm_kernel, name='norm', out_shape=(shape((own, width), B...  1.92 us
  transfers between devices with their start and end apart: 2, of which 2 were waited for; matrix products, arithmetic and copies ran while one was open for 0% of the time, Pallas kernels for 12%

profile of v6, /device:TPU:40, one launch (start us, length us, event | category | flops | bytes accessed | tf_op | source)
XLA Modules:
  0.0 73.8 jit_solution(8554859621055359618)
XLA Ops:
  0.0 1.9 %norm.1 = (bf16[16,768]{1,0:T(8,128)(2,1)S(1)}, bf16[16,16,768]{2,1,0:T(8,128)(2,1)}) custom-call(s32[8]{0:T(128)} %restype_hbm.1, bf16[2,8,768]{2,1,0:T(8,128)(2,1)} %single_hbm.1, bf16[32,768]{1,0:T(8,128)(2,1)} %table_hbm.1, f32[768]{0:T(1024)} %gain_hbm.1), custom_call_target="tpu_custom_call" | custom-call | tf_op jit(solution)/shard_map/norm/pallas_call | solution.py:283
  1.9 6.1 %all-to-all-start = ((bf16[16,16,768]{2,1,0:T(8,128)(2,1)}), bf16[16,16,768]{2,1,0:T(8,128)(2,1)S(1)}, u32[]{:S(2)}, u32[]{:S(2)}) async-start(bf16[16,16,768]{2,1,0:T(8,128)(2,1)} %get-tuple-element.11), calls=%async_computation | async-start | bytes 786432 | tf_op jit(solution)/shard_map/all_to_all | solution.py:299
  8.1 0.1 pad_add_fusion.where_ref
  8.2 4.7 %bias_0.1 = (f32[16,64,128]{2,1,0:T(8,128)}, f32[16,768]{1,0:T(8,128)}) custom-call(bf16[16,768]{1,0:T(8,128)(2,1)S(1)} %get-tuple-element.12.own_ref, s32[2]{0:T(128)S(1)} %pad_add_fusion.where_ref, s32[2048]{0:T(1024)} %refs_0_.3, f32[16]{0:T(128)} %refs_1_.3, s32[16,128]{1,0:T(8,128)} %bitcast.6, s32[1,128]{1,0:T(1,128)} %bitcast.10, f32[1,128]{1,0:T(1,128)} %bitcast.12, ...), custom_call_target="tpu_custom_call" | custom-call | flops 500000000 | bytes 10000000 | tf_op jit(solution)/shard_map/bias_0/pallas_call | solution.py:307
  12.9 5.9 %all-to-all-done.cols_ref = bf16[16,16,768]{2,1,0:T(8,128)(2,1)S(1)} async-done(((bf16[16,16,768]{2,1,0:T(8,128)(2,1)}), bf16[16,16,768]{2,1,0:T(8,128)(2,1)S(1)}, u32[]{:S(2)}, u32[]{:S(2)}) %all-to-all-start) | async-done | bytes 393248 | tf_op jit(solution)/shard_map/all_to_all | solution.py:299
  18.8 0.9 %pack.1 = bf16[16,32,768]{2,1,0:T(8,128)(2,1)} custom-call(bf16[16,16,768]{2,1,0:T(8,128)(2,1)S(1)} %all-to-all-done.cols_ref, bf16[16,768]{1,0:T(8,128)(2,1)S(1)} %get-tuple-element.12.own_ref, f32[16,64,128]{2,1,0:T(8,128)} %get-tuple-element.13.after_ref.bias_a_hbm), custom_call_target="tpu_custom_call" | custom-call | tf_op jit(solution)/shard_map/pack/pallas_call | solution.py:345
  19.7 9.5 %all-to-all-start.1 = ((bf16[16,32,768]{2,1,0:T(8,128)(2,1)}), bf16[16,32,768]{2,1,0:T(8,128)(2,1)S(1)}, u32[]{:S(2)}, u32[]{:S(2)}) async-start(bf16[16,32,768]{2,1,0:T(8,128)(2,1)} %pack.1), calls=%async_computation.1 | async-start | bytes 1572864 | tf_op jit(solution)/shard_map/all_to_all | solution.py:353
  29.2 4.5 %bias_1.1 = (f32[16,64,128]{2,1,0:T(8,128)}, bf16[768,1536]{1,0:T(8,128)(2,1)S(1)}) custom-call(bf16[16,768]{1,0:T(8,128)(2,1)S(1)} %get-tuple-element.12.own_ref, s32[2]{0:T(128)S(1)} %pad_add_fusion.where_ref, s32[2048]{0:T(1024)} %refs_0_.3, f32[16]{0:T(128)} %refs_1_.3, s32[16,128]{1,0:T(8,128)} %bitcast.7, s32[1,128]{1,0:T(1,128)} %bitcast.11, ...), custom_call_target="tpu_custom_call" | custom-call | flops 500000000 | bytes 10000000 | tf_op jit(solution)/shard_map/bias_1/pallas_call | solution.py:307
  33.7 16.0 %all-to-all-done.1.tokens_ref = bf16[16,32,768]{2,1,0:T(8,128)(2,1)S(1)} async-done(((bf16[16,32,768]{2,1,0:T(8,128)(2,1)}), bf16[16,32,768]{2,1,0:T(8,128)(2,1)S(1)}, u32[]{:S(2)}, u32[]{:S(2)}) %all-to-all-start.1) | async-done | bytes 786464 | tf_op jit(solution)/shard_map/all_to_all | solution.py:353
  49.8 0.0 copy-start
  49.8 0.0 copy-start.1
  49.8 4.3 %attend.1 = bf16[16,104,128]{2,1,0:T(8,128)(2,1)S(1)} custom-call(bf16[16,32,768]{2,1,0:T(8,128)(2,1)S(1)} %all-to-all-done.1.tokens_ref, bf16[768,1536]{1,0:T(8,128)(2,1)S(1)} %get-tuple-element.14.wkv_ref, bf16[768,3072]{1,0:T(8,128)(2,1)} %w_hbm.1, f32[16,64,128]{2,1,0:T(8,128)} %get-tuple-element.13.after_ref.bias_a_hbm, ...), custom_call_target="tpu_custom_call" | custom-call | tf_op jit(solution)/shard_map/attend/pallas_call | solution.py:356
  54.0 18.4 %all_to_all.15.parts_ref = bf16[16,104,128]{2,1,0:T(8,128)(2,1)S(1)} all-to-all(bf16[16,104,128]{2,1,0:T(8,128)(2,1)S(1)} %attend.1), channel_id=1, replica_groups=mesh['qrow'=16,'kcol'=16] {'kcol'}, dimensions={0} | all-to-all | bytes 851968 | tf_op jit(solution)/shard_map/all_to_all | solution.py:370
  72.5 0.0 copy-done
  72.5 0.0 copy-done.1
  72.5 1.4 %merge.1 = bf16[2,8,768]{2,1,0:T(8,128)(2,1)} custom-call(bf16[16,104,128]{2,1,0:T(8,128)(2,1)S(1)} %all_to_all.15.parts_ref, f32[16,768]{1,0:T(8,128)S(1)} %copy-done.1, bf16[768,768]{1,0:T(8,128)(2,1)S(1)} %copy-done), custom_call_target="tpu_custom_call" | custom-call | tf_op jit(solution)/shard_map/merge/pallas_call | solution.py:371
Async XLA Ops:
  1.9 16.9 %all-to-all-start = ((bf16[16,16,768]{2,1,0:T(8,128)(2,1)}), bf16[16,16,768]{2,1,0:T(8,128)(2,1)S(1)}, u32[]{:S(2)}, u32[]{:S(2)}) async-start(bf16[16,16,768]{2,1,0:T(8,128)(2,1)} %get-tuple-element.11), calls=%async_computation | async-start | bytes 786432 | tf_op jit(solution)/shard_map/all_to_all | solution.py:299
  19.7 30.0 %all-to-all-start.1 = ((bf16[16,32,768]{2,1,0:T(8,128)(2,1)}), bf16[16,32,768]{2,1,0:T(8,128)(2,1)S(1)}, u32[]{:S(2)}, u32[]{:S(2)}) async-start(bf16[16,32,768]{2,1,0:T(8,128)(2,1)} %pack.1), calls=%async_computation.1 | async-start | bytes 1572864 | tf_op jit(solution)/shard_map/all_to_all | solution.py:353
  49.8 22.7 %copy-start = (bf16[768,768]{1,0:T(8,128)(2,1)S(1)}, bf16[768,768]{1,0:T(8,128)(2,1)}, u32[]{:S(2)}) copy-start(bf16[768,768]{1,0:T(8,128)(2,1)} %wout_ref.1) | copy-start | bytes 3538948
  49.8 22.7 %copy-start.1 = (f32[16,768]{1,0:T(8,128)S(1)}, f32[16,768]{1,0:T(8,128)}, u32[]{:S(2)}) copy-start(f32[16,768]{1,0:T(8,128)} %get-tuple-element.16.gate_ref) | copy-start | bytes 147460

commit v7 on v5

--- a/solution.py
+++ b/solution.py
@@ -76,9 +76,11 @@
         copies_ref[j] = normed
 
 
-def copies_kernel(one_ref, after_ref, copies_ref):
+def copies_kernel(one_ref, two_ref, after_ref, copies_ref):
+    per = one_ref.shape[0]
     for j in range(copies_ref.shape[0]):
-        copies_ref[j] = one_ref[...]
+        copies_ref[j, :per] = one_ref[...]
+        copies_ref[j, per:] = two_ref[...]
 
 
 def bias_kernel(start, late, tokens_ref, where_ref, *refs):
@@ -155,25 +157,24 @@
     parts, per, width = cols_ref.shape
     half = per // 2
     heads, queries, keys = bias_ref.shape
-    few = queries // 2
+    few = bias_a_hbm.shape[1]
     size = width // heads
     scale = 1.0 / math.sqrt(size)
     loads = [
         pltpu.make_async_copy(bias_a_hbm, bias_ref.at[:, pl.ds(0, few)], sems.at[0]),
-        pltpu.make_async_copy(bias_b_hbm, bias_ref.at[:, pl.ds(few, few)], sems.at[1]),
+        pltpu.make_async_copy(bias_b_hbm, bias_ref.at[:, pl.ds(few, queries - few)], sems.at[1]),
     ]
     for load in loads:
         load.start()
+    base = (where_ref[1] * 2 + lax.rem(lax.div(where_ref[0], 2), 2)) * parts
     for i in range(parts):
-        x_ref[pl.ds(order_ref[where_ref[1] * parts + i], 1)] = cols_ref[pl.ds(i, 1)]
+        x_ref[pl.ds(order_ref[base + i], 1)] = cols_ref[pl.ds(i, 1)]
     x = x_ref[...].reshape(parts * per, width)
 
     def project(w):
         return jnp.dot(x, w, preferred_element_type=F32).reshape(parts, 2, half, width)
 
     kf, vf = project(wkv_ref[:, :width]), project(wkv_ref[:, width:])
-    for load in loads:
-        load.wait()
     span = 256
     wins = width // span
 
@@ -198,6 +199,9 @@
             for i, h in enumerate(members(t)):
                 piece = res[i * queries : (i + 1) * queries]
                 raw[h] = raw[h] + piece if h in raw else piece
+        if s == 0:
+            for load in loads:
+                load.wait()
         tops = jnp.zeros((queries, 128), F32)
         tots = jnp.zeros((queries, 128), F32)
         rounded = []
@@ -261,34 +265,37 @@
     out_ref[...] = update.reshape(out_ref.shape).astype(BF)
 
 
-def near_swap(n):
+def near_swaps(n):
     ring = lambda a, b, size: min((a - b) % size, (b - a) % size)
-    table = []
+    upper = lambda i: i // 2 % 2
+    tables = ([], [])
     for c in range(n):
-        cx, cyh, cco = c // 4, c // 2 % 2, c % 2
-        cyl, cz = c // 8, c % 8
 
         def cost(j, i):
-            hops = ring(cx, i // 4, 4) + ring(j % 8, cz, 8)
-            hops += ring(cyh * 2 + j // 8, (i // 2 % 2) * 2 + cyl, 4)
-            return 2 * hops + (cco != i % 2)
-
-        for most in range(100):
-            taken = {}
-
-            def place(j, seen):
-                for i in range(n):
-                    if cost(j, i) <= most and i not in seen:
-                        seen.add(i)
-                        if i not in taken or place(taken[i], seen):
-                            taken[i] = j
-                            return True
-                return False
-
-            if all(place(j, set()) for j in range(n)):
-                break
-        table.append([taken[i] for i in range(n)])
-    return table
+            hops = ring(c // 4, i // 4, 4) + ring(j % 8, c % 8, 8)
+            hops += ring(upper(c) * 2 + j // 8, upper(i) * 2 + c // 8, 4)
+            return 2 * hops + (c % 2 != i % 2)
+
+        first = {}
+        for table in tables:
+            for most in range(100):
+                taken = {}
+
+                def place(j, seen):
+                    for i in range(n):
+                        other = j not in first or upper(first[j]) != upper(i)
+                        if other and cost(j, i) <= most and i not in seen:
+                            seen.add(i)
+                            if i not in taken or place(taken[i], seen):
+                                taken[i] = j
+                                return True
+                    return False
+
+                if all(place(j, set()) for j in range(n)):
+                    break
+            table.append([taken[i] for i in range(n)])
+            first = {j: i for i, j in taken.items()}
+    return tables
 
 
 def params(mib):
@@ -335,21 +342,23 @@
         compiler_params=params(4),
     )(*stay(restype, single, restype_table, single_gain))
 
-    table = near_swap(n_row)
-    swap = [(c * n_col + j, i * n_col + c) for c in range(n_row) for i, j in enumerate(table[c])]
-    turned = lax.ppermute(normed, ("qrow", "kcol"), swap)
+    tables = near_swaps(n_row)
+    turned = []
+    for table in tables:
+        swap = [(c * n_col + j, i * n_col + c) for c in range(n_row) for i, j in enumerate(table[c])]
+        turned.append(lax.ppermute(normed, ("qrow", "kcol"), swap))
     row_tokens = lax.all_to_all(copies, "kcol", 0, 0)
 
     where = jnp.stack([lax.axis_index("qrow"), lax.axis_index("kcol")]).astype(jnp.int32)
-    chunks = 4
-    half = row_len // 2
+    block = row_len // 8
 
     def bias_of(late, tokens):
-        out = [pltpu.HBM((heads, half, col_len), F32)]
+        chunks = 2 if late else 6
+        out = [pltpu.HBM((heads, chunks * block, col_len), F32)]
         out += [shape((samples, row_len, width), BF) if late else pltpu.HBM((own, width), F32)]
         out += [shape((width, 2 * width), BF)] * late
         return pl.pallas_call(
-            functools.partial(bias_kernel, late * half, late),
+            functools.partial(bias_kernel, late * (row_len - 2 * block), late),
             name="bias_" + str(late),
             out_shape=out,
             in_specs=[vmem(), smem()] + hbm(8),
@@ -361,13 +370,13 @@
                 pltpu.VMEM((1, col_len), jnp.int32),
                 pltpu.VMEM((1, channels), F32),
                 pltpu.VMEM((heads, channels), F32),
-                pltpu.VMEM((chunks, half // chunks, col_len, channels), BF),
+                pltpu.VMEM((chunks, block, col_len, channels), BF),
                 dma((6,)),
                 dma((chunks,)),
                 pltpu.VMEM((width, width), BF),
                 dma((2,)),
             ],
-            compiler_params=params(12 if late else 8),
+            compiler_params=params(10),
             cost_estimate=pl.CostEstimate(flops=5 * 10**8, bytes_accessed=10 * 10**6, transcendentals=0),
         )(
             tokens,
@@ -386,18 +395,21 @@
 
     bias_a, gate = bias_of(0, normed[None])
     bias_b, queries, w_kv = bias_of(1, row_tokens)
+    sides = [[i for i in range(n_row) if i // 2 % 2 == side] for side in range(2)]
     turned_copies = pl.pallas_call(
         copies_kernel,
         name="copies",
-        out_shape=shape((n_row, own, width), BF),
-        in_specs=[vmem()] + hbm(1),
+        out_shape=shape((n_row // 2, 2 * own, width), BF),
+        in_specs=[vmem()] * 2 + hbm(1),
         out_specs=vmem(),
         compiler_params=params(4),
-    )(turned, *stay(bias_a))
+    )(*turned, *stay(bias_a))
     turned_copies, row_tokens = lax.optimization_barrier((turned_copies, row_tokens))
-    col_tokens = lax.all_to_all(turned_copies, "qrow", 0, 0)
-
-    order = jnp.asarray(table, jnp.int32).reshape(-1)
+    col_tokens = lax.all_to_all(turned_copies, "qrow", 0, 0, axis_index_groups=sides)
+    col_tokens = col_tokens.reshape(n_row, own, width)
+    order = [tables[k][c][i] for c in range(n_col) for side in sides for i in side for k in range(2)]
+    order = jnp.asarray(order, jnp.int32)
+
     rows = own * width // 128 + tok
     partial = pl.pallas_call(
         attend_kernel,

time: 67.2 us -> 66.4 us (0.988)
  waiting for transfers between devices: 12.2 us -> 7.1 us
  starting transfers between devices: 17.3 us -> 19.6 us
  blocking collectives: 18.6 us -> 20.9 us
    ppermute x1 -> x2, starting transfers between devices: 1.1 us -> 5.16 us  [shards(): turned.append(lax.ppermute(normed, ('qrow', 'kcol'), swap))]
    ppermute x1 -> x2, waiting for transfers between devices: 6.12 us -> 2.38 us  [shards(): turned.append(lax.ppermute(normed, ('qrow', 'kcol'), swap))]
    all_to_all x1, blocking collectives: 18.6 us -> 20.9 us  [shards(): gathered = lax.all_to_all(partial, 'kcol', 0, 0)]
    all_to_all x1, starting transfers between devices: 6.66 us -> 4.95 us  [shards(): lax.all_to_all(turned_copies, 'qrow', 0, 0, axis_index_groups=sides)]
    all_to_all x1, waiting for transfers between devices: 0.74 us -> 0.01 us  [shards(): row_tokens = lax.all_to_all(copies, 'kcol', 0, 0)]
  transfers between devices with their start and end apart: 3 -> 4, of which waited for: 3 -> 2; matrix products, arithmetic and copies ran while one was open for 0% -> 0% of each run, Pallas kernels for 16% -> 17%
where the time goes in v7:
time: 66.4 us; the launch traced here: 66 us
  blocking collectives  20.9 us (31%)
  starting transfers between devices  19.6 us (30%)
  Pallas kernels  18.3 us (28%)
  waiting for transfers between devices  7.1 us (11%)
    all_to_all x1, blocking collectives, shards(): gathered = lax.all_to_all(partial, 'kcol', 0, 0)  20.9 us
    pallas_call x2, Pallas kernels, bias_of(): pl.pallas_call(functools.partial(bias_kernel, late * (row_len - 2 * block...  10.2 us
    all_to_all x1, starting transfers between devices, shards(): row_tokens = lax.all_to_all(copies, 'kcol', 0, 0)  9.5 us
    ppermute x2, starting transfers between devices, shards(): turned.append(lax.ppermute(normed, ('qrow', 'kcol'), swap))  5.16 us
    all_to_all x1, starting transfers between devices, shards(): lax.all_to_all(turned_copies, 'qrow', 0, 0, axis_index_groups=sides)  4.95 us
    all_to_all x1, waiting for transfers between devices, shards(): lax.all_to_all(turned_copies, 'qrow', 0, 0, axis_index_groups=sides)  4.72 us
    pallas_call x1, Pallas kernels, shards(): pl.pallas_call(attend_kernel, name='attend', out_shape=shape((n_col, rows...  4.07 us
    ppermute x2, waiting for transfers between devices, shards(): turned.append(lax.ppermute(normed, ('qrow', 'kcol'), swap))  2.38 us
  transfers between devices with their start and end apart: 4, of which 2 were waited for; matrix products, arithmetic and copies ran while one was open for 0% of the time, Pallas kernels for 17%

profile of v7, /device:TPU:40, one launch (start us, length us, event | category | flops | bytes accessed | tf_op | source)
XLA Modules:
  0.0 66.0 jit_solution(444497796427090806)
XLA Ops:
  0.0 1.9 %norm.1 = (bf16[16,768]{1,0:T(8,128)(2,1)S(1)}, bf16[16,16,768]{2,1,0:T(8,128)(2,1)}) custom-call(s32[8]{0:T(128)} %restype_hbm.1, bf16[2,8,768]{2,1,0:T(8,128)(2,1)} %single_hbm.1, bf16[32,768]{1,0:T(8,128)(2,1)} %table_hbm.1, f32[768]{0:T(1024)} %gain_hbm.1), custom_call_target="tpu_custom_call" | custom-call | tf_op jit(solution)/shard_map/norm/pallas_call | solution.py:329
  1.9 9.5 %all-to-all-start = ((bf16[16,16,768]{2,1,0:T(8,128)(2,1)}), bf16[16,16,768]{2,1,0:T(8,128)(2,1)S(1)}, u32[]{:S(2)}, u32[]{:S(2)}) async-start(bf16[16,16,768]{2,1,0:T(8,128)(2,1)} %get-tuple-element.15), calls=%async_computation | async-start | bytes 786432 | tf_op jit(solution)/shard_map/all_to_all | solution.py:350
  11.4 0.3 collective-permute-start.1
  11.7 4.9 %collective-permute-start = (bf16[16,768]{1,0:T(8,128)(2,1)S(1)}, bf16[16,768]{1,0:T(8,128)(2,1)S(1)}, u32[]{:S(2)}, u32[]{:S(2)}) collective-permute-start(bf16[16,768]{1,0:T(8,128)(2,1)S(1)} %get-tuple-element.13), channel_id=1, source_target_pairs={{15,0},{14,16},{12,32},{13,48},{10,64},{8,80},{11,96},{9,112},{5,1... | collective-permute-start | bytes 73736 | tf_op jit(solution)/shard_map/ppermute | solution.py:349
  16.6 0.1 pad_add_fusion.where_ref
  16.7 5.9 %bias_0.1 = (f32[16,96,128]{2,1,0:T(8,128)}, f32[16,768]{1,0:T(8,128)}) custom-call(bf16[1,16,768]{2,1,0:T(8,128)(2,1)S(1)} %bitcast.9, s32[2]{0:T(128)S(1)} %pad_add_fusion.where_ref, s32[2048]{0:T(1024)} %refs_0_.3, f32[16]{0:T(128)} %refs_1_.3, s32[16,128]{1,0:T(8,128)} %bitcast.10, s32[1,128]{1,0:T(1,128)} %bitcast.14, f32[1,128]{1,0:T(1,128)} %bitcast.16, ...), custom_call_target="tpu_custom_call" | custom-call | flops 500000000 | bytes 10000000 | tf_op jit(solution)/shard_map/bias_0/pallas_call | solution.py:360
  22.6 0.0 collective-permute-done.1.two_ref
  22.6 2.4 %collective-permute-done.one_ref = bf16[16,768]{1,0:T(8,128)(2,1)S(1)} collective-permute-done((bf16[16,768]{1,0:T(8,128)(2,1)S(1)}, bf16[16,768]{1,0:T(8,128)(2,1)S(1)}, u32[]{:S(2)}, u32[]{:S(2)}) %collective-permute-start) | collective-permute-done | bytes 24608 | tf_op jit(solution)/shard_map/ppermute | solution.py:349
  25.0 0.8 %copies.1 = bf16[8,32,768]{2,1,0:T(8,128)(2,1)} custom-call(bf16[16,768]{1,0:T(8,128)(2,1)S(1)} %collective-permute-done.one_ref, bf16[16,768]{1,0:T(8,128)(2,1)S(1)} %collective-permute-done.1.two_ref, f32[16,96,128]{2,1,0:T(8,128)} %get-tuple-element.14.after_ref.bias_a_hbm), custom_call_target="tpu_custom_call" | custom-call | tf_op jit(solution)/shard_map/copies/pallas_call | solution.py:399
  25.8 0.0 all-to-all-done.tokens_ref
  25.8 4.9 %all-to-all-start.1 = ((bf16[8,32,768]{2,1,0:T(8,128)(2,1)}), bf16[8,32,768]{2,1,0:T(8,128)(2,1)S(1)}, u32[]{:S(2)}, u32[]{:S(2)}) async-start(bf16[8,32,768]{2,1,0:T(8,128)(2,1)} %copies.1), calls=%async_computation.1 | async-start | bytes 786432 | tf_op jit(solution)/shard_map/all_to_all | solution.py:408
  30.8 0.0 copy-start.2
  30.8 4.2 %bias_1.1 = (f32[16,32,128]{2,1,0:T(8,128)}, bf16[2,128,768]{2,1,0:T(8,128)(2,1)S(1)}, bf16[768,1536]{1,0:T(8,128)(2,1)S(1)}) custom-call(bf16[16,16,768]{2,1,0:T(8,128)(2,1)S(1)} %all-to-all-done.tokens_ref, s32[2]{0:T(128)S(1)} %pad_add_fusion.where_ref, s32[2048]{0:T(1024)} %refs_0_.3, f32[16]{0:T(128)} %refs_1_.3, s32[16,128]{1,0:T(8,128)} %bitcast.11, ...), custom_call_target="tpu_custom_call" | custom-call | flops 500000000 | bytes 10000000 | tf_op jit(solution)/shard_map/bias_1/pallas_call | solution.py:360
  35.0 0.0 copy-start.1
  35.0 4.7 %all-to-all-done.1 = bf16[8,32,768]{2,1,0:T(8,128)(2,1)S(1)} async-done(((bf16[8,32,768]{2,1,0:T(8,128)(2,1)}), bf16[8,32,768]{2,1,0:T(8,128)(2,1)S(1)}, u32[]{:S(2)}, u32[]{:S(2)}) %all-to-all-start.1) | async-done | bytes 393248 | tf_op jit(solution)/shard_map/all_to_all | solution.py:408
  39.7 0.0 copy-start
  39.7 0.0 copy-done.2
  39.7 4.1 %attend.1 = bf16[16,104,128]{2,1,0:T(8,128)(2,1)S(1)} custom-call(s32[2]{0:T(128)S(1)} %pad_add_fusion.where_ref, s32[512]{0:T(512)S(1)} %copy-done.2, bf16[16,16,768]{2,1,0:T(8,128)(2,1)S(1)} %bitcast.8, bf16[768,1536]{1,0:T(8,128)(2,1)S(1)} %get-tuple-element.17.wkv_ref, bf16[2,128,768]{2,1,0:T(8,128)(2,1)S(1)} %get-tuple-element.18.q_ref, ...), custom_call_target="tpu_custom_call" | custom-call | tf_op jit(solution)/shard_map/attend/pallas_call | solution.py:414
  43.8 20.9 %all_to_all.15.parts_ref = bf16[16,104,128]{2,1,0:T(8,128)(2,1)S(1)} all-to-all(bf16[16,104,128]{2,1,0:T(8,128)(2,1)S(1)} %attend.1), channel_id=1, replica_groups=mesh['qrow'=16,'kcol'=16] {'kcol'}, dimensions={0} | all-to-all | bytes 851968 | tf_op jit(solution)/shard_map/all_to_all | solution.py:428
  64.7 0.0 copy-done.1
  64.7 0.0 copy-done
  64.7 1.4 %merge.1 = bf16[2,8,768]{2,1,0:T(8,128)(2,1)} custom-call(bf16[16,104,128]{2,1,0:T(8,128)(2,1)S(1)} %all_to_all.15.parts_ref, f32[16,768]{1,0:T(8,128)S(1)} %copy-done.1, bf16[768,768]{1,0:T(8,128)(2,1)S(1)} %copy-done), custom_call_target="tpu_custom_call" | custom-call | tf_op jit(solution)/shard_map/merge/pallas_call | solution.py:429
Async XLA Ops:
  1.9 23.9 %all-to-all-start = ((bf16[16,16,768]{2,1,0:T(8,128)(2,1)}), bf16[16,16,768]{2,1,0:T(8,128)(2,1)S(1)}, u32[]{:S(2)}, u32[]{:S(2)}) async-start(bf16[16,16,768]{2,1,0:T(8,128)(2,1)} %get-tuple-element.15), calls=%async_computation | async-start | bytes 786432 | tf_op jit(solution)/shard_map/all_to_all | solution.py:350
  11.4 11.2 %collective-permute-start.1 = (bf16[16,768]{1,0:T(8,128)(2,1)S(1)}, bf16[16,768]{1,0:T(8,128)(2,1)S(1)}, u32[]{:S(2)}, u32[]{:S(2)}) collective-permute-start(bf16[16,768]{1,0:T(8,128)(2,1)S(1)} %get-tuple-element.13), channel_id=1, source_target_pairs={{13,0},{12,16},{4,32},{15,48},{11,64},{9,80},{5,96},{14,112},{7,12... | collective-permute-start | bytes 73736 | tf_op jit(solution)/shard_map/ppermute | solution.py:349
  11.7 13.3 %collective-permute-start = (bf16[16,768]{1,0:T(8,128)(2,1)S(1)}, bf16[16,768]{1,0:T(8,128)(2,1)S(1)}, u32[]{:S(2)}, u32[]{:S(2)}) collective-permute-start(bf16[16,768]{1,0:T(8,128)(2,1)S(1)} %get-tuple-element.13), channel_id=1, source_target_pairs={{15,0},{14,16},{12,32},{13,48},{10,64},{8,80},{11,96},{9,112},{5,1... | collective-permute-start | bytes 73736 | tf_op jit(solution)/shard_map/ppermute | solution.py:349
  25.8 13.9 %all-to-all-start.1 = ((bf16[8,32,768]{2,1,0:T(8,128)(2,1)}), bf16[8,32,768]{2,1,0:T(8,128)(2,1)S(1)}, u32[]{:S(2)}, u32[]{:S(2)}) async-start(bf16[8,32,768]{2,1,0:T(8,128)(2,1)} %copies.1), calls=%async_computation.1 | async-start | bytes 786432 | tf_op jit(solution)/shard_map/all_to_all | solution.py:408
  30.8 8.9 %copy-start.2 = (s32[512]{0:T(512)S(1)}, s32[512]{0:T(512)}, u32[]{:S(2)}) copy-start(s32[512]{0:T(512)} %constant.9.clone.order_ref) | copy-start | bytes 6148
  35.0 29.7 %copy-start.1 = (f32[16,768]{1,0:T(8,128)S(1)}, f32[16,768]{1,0:T(8,128)}, u32[]{:S(2)}) copy-start(f32[16,768]{1,0:T(8,128)} %get-tuple-element.20.gate_ref) | copy-start | bytes 147460
  39.7 25.0 %copy-start = (bf16[768,768]{1,0:T(8,128)(2,1)S(1)}, bf16[768,768]{1,0:T(8,128)(2,1)}, u32[]{:S(2)}) copy-start(bf16[768,768]{1,0:T(8,128)(2,1)} %wout_ref.1) | copy-start | bytes 3538948

commit v8 on v7

--- a/solution.py
+++ b/solution.py
@@ -83,17 +83,17 @@
         copies_ref[j, per:] = two_ref[...]
 
 
-def bias_kernel(start, late, tokens_ref, where_ref, *refs):
+def bias_kernel(start, late, own_ref, where_ref, *refs):
     ins, refs = refs[:8], refs[8:]
     pair_hbm, w_hbm = ins[6:]
     out_ref, extra_ref, refs = refs[0], refs[1], refs[2:]
     if late:
-        w_ref, refs = refs[0], refs[1:]
+        wq_ref, refs = refs[0], refs[1:]
     chain_ref, cbias_ref, chain_rows_ref, live_ref, gain_ref, weight_ref, pair_ref, sems, pair_sems = refs[:9]
-    mine_ref, w_sems = refs[9:]
+    w_ref, w_sem = (extra_ref, refs[9]) if late else refs[9:]
     chunks, block, keys, channels = pair_ref.shape
     heads = weight_ref.shape[0]
-    width = mine_ref.shape[0]
+    width = own_ref.shape[1]
     loads = [
         pltpu.make_async_copy(pair_hbm.at[pl.ds(start + i * block, block)], pair_ref.at[i], pair_sems.at[i])
         for i in range(chunks)
@@ -104,12 +104,10 @@
     small = [pltpu.make_async_copy(src, dst, sems.at[i]) for i, (src, dst) in enumerate(small)]
     for load in small + loads[2:]:
         load.start()
-    own = 0 if late else 3 * width
-    load_mine = pltpu.make_async_copy(w_hbm.at[:, pl.ds(own, width)], mine_ref, w_sems.at[0])
-    load_mine.start()
+    place = pl.ds(width, 2 * width) if late else pl.ds(3 * width, width)
+    load_w = [pltpu.make_async_copy(w_hbm.at[:, place], w_ref, w_sem.at[0])]
     if late:
-        load_w = pltpu.make_async_copy(w_hbm.at[:, pl.ds(width, 2 * width)], w_ref, w_sems.at[1])
-        load_w.start()
+        load_w.append(pltpu.make_async_copy(w_hbm.at[:, pl.ds(0, width)], wq_ref, w_sem.at[1]))
     for load in small:
         load.wait()
     weight = weight_ref[...] * gain_ref[...]
@@ -124,6 +122,9 @@
     alive = jnp.broadcast_to(live_ref[...] == 1, (heads, keys))
     for i in range(chunks):
         loads[i].wait()
+        if i == 0:
+            for load in load_w:
+                load.start()
         for q in range(0, block, 2):
             turned = pair_ref[i, q : q + 2].reshape(2 * keys, channels).T
             x = turned.astype(F32)
@@ -139,16 +140,22 @@
                 same = col_chain == chain_ref[base + at]
                 part = part + jnp.where(same, column, 0.0)
                 out_ref[:, at, :] = jnp.where(alive, part, -1e30)
-    load_mine.wait()
-    parts, per, _ = tokens_ref.shape
-    res = jnp.dot(tokens_ref[...].reshape(parts * per, width), mine_ref[...], preferred_element_type=F32)
-    if late:
-        res = res.reshape(parts, 2, per // 2, width)
-        for s in range(2):
-            extra_ref[s] = res[:, s].reshape(parts * per // 2, width).astype(BF)
-        load_w.wait()
-    else:
-        extra_ref[...] = jax.nn.sigmoid(res)
+    for load in load_w:
+        load.wait()
+    if not late:
+        pre = jnp.dot(own_ref[...], w_ref[...], preferred_element_type=F32)
+        extra_ref[...] = jax.nn.sigmoid(pre)
+
+
+def query_kernel(where_ref, rows_ref, others_ref, w_ref, q_ref, x_ref):
+    near, per, width = rows_ref.shape
+    ours = lax.div(where_ref[1], near) * near
+    x_ref[pl.ds(ours, near)] = rows_ref[...]
+    x_ref[pl.ds(near - ours, near)] = others_ref[...]
+    x = x_ref[...].reshape(2 * near * per, width)
+    query = jnp.dot(x, w_ref[...], preferred_element_type=F32).reshape(2 * near, 2, per // 2, width)
+    for s in range(2):
+        q_ref[s] = query[:, s].reshape(near * per, width).astype(BF)
 
 
 def attend_kernel(
@@ -329,7 +336,7 @@
     normed, copies = pl.pallas_call(
         norm_kernel,
         name="norm",
-        out_shape=(shape((own, width), BF), shape((n_col, own, width), BF)),
+        out_shape=(shape((own, width), BF), shape((n_col // 2, own, width), BF)),
         in_specs=hbm(4),
         out_specs=(vmem(), vmem()),
         scratch_shapes=[
@@ -347,18 +354,19 @@
     for table in tables:
         swap = [(c * n_col + j, i * n_col + c) for c in range(n_row) for i, j in enumerate(table[c])]
         turned.append(lax.ppermute(normed, ("qrow", "kcol"), swap))
-    row_tokens = lax.all_to_all(copies, "kcol", 0, 0)
+    near = [list(range(n_col // 2)), list(range(n_col // 2, n_col))]
+    row_tokens = lax.all_to_all(copies, "kcol", 0, 0, axis_index_groups=near)
 
     where = jnp.stack([lax.axis_index("qrow"), lax.axis_index("kcol")]).astype(jnp.int32)
     block = row_len // 8
 
-    def bias_of(late, tokens):
-        chunks = 2 if late else 6
+    def bias_of(late):
+        chunks = 4
         out = [pltpu.HBM((heads, chunks * block, col_len), F32)]
-        out += [shape((samples, row_len, width), BF) if late else pltpu.HBM((own, width), F32)]
-        out += [shape((width, 2 * width), BF)] * late
+        out += [shape((width, 2 * width), BF) if late else pltpu.HBM((own, width), F32)]
+        out += [shape((width, width), BF)] * late
         return pl.pallas_call(
-            functools.partial(bias_kernel, late * (row_len - 2 * block), late),
+            functools.partial(bias_kernel, late * chunks * block, late),
             name="bias_" + str(late),
             out_shape=out,
             in_specs=[vmem(), smem()] + hbm(8),
@@ -373,13 +381,13 @@
                 pltpu.VMEM((chunks, block, col_len, channels), BF),
                 dma((6,)),
                 dma((chunks,)),
-                pltpu.VMEM((width, width), BF),
-                dma((2,)),
-            ],
+            ]
+            + ([] if late else [pltpu.VMEM((width, width), BF)])
+            + [dma((2,))],
             compiler_params=params(10),
             cost_estimate=pl.CostEstimate(flops=5 * 10**8, bytes_accessed=10 * 10**6, transcendentals=0),
         )(
-            tokens,
+            normed,
             where,
             *stay(
                 chain,
@@ -393,8 +401,8 @@
             ),
         )
 
-    bias_a, gate = bias_of(0, normed[None])
-    bias_b, queries, w_kv = bias_of(1, row_tokens)
+    bias_a, gate = bias_of(0)
+    bias_b, w_kv, w_q = bias_of(1)
     sides = [[i for i in range(n_row) if i // 2 % 2 == side] for side in range(2)]
     turned_copies = pl.pallas_call(
         copies_kernel,
@@ -406,7 +414,17 @@
     )(*turned, *stay(bias_a))
     turned_copies, row_tokens = lax.optimization_barrier((turned_copies, row_tokens))
     col_tokens = lax.all_to_all(turned_copies, "qrow", 0, 0, axis_index_groups=sides)
+    other_tokens = lax.ppermute(row_tokens, "kcol", [(i, (i + n_col // 2) % n_col) for i in range(n_col)])
     col_tokens = col_tokens.reshape(n_row, own, width)
+    queries = pl.pallas_call(
+        query_kernel,
+        name="query",
+        out_shape=shape((samples, row_len, width), BF),
+        in_specs=[smem()] + [vmem()] * 3,
+        out_specs=vmem(),
+        scratch_shapes=[pltpu.VMEM((n_col, own, width), BF)],
+        compiler_params=params(6),
+    )(where, row_tokens, other_tokens, w_q)
     order = [tables[k][c][i] for c in range(n_col) for side in sides for i in side for k in range(2)]
     order = jnp.asarray(order, jnp.int32)
 

time: 66.4 us -> 63 us (0.949); the launches traced: 66 us -> 61.9 us
  waiting for transfers between devices: 7.1 us -> 2.09 us
  starting transfers between devices: 19.6 us -> 21.5 us
  blocking collectives: 20.9 us -> 19.6 us
    all_to_all x1, waiting for transfers between devices: 4.72 us -> 0.58 us  [shards(): lax.all_to_all(turned_copies, 'qrow', 0, 0, axis_index_groups=sides)]
    ppermute x0 -> x1, starting transfers between devices: none -> 1.84 us  [shards(): lax.ppermute(row_tokens, 'kcol', [(i, (i + n_col // 2) % n_col) for i in...]
    ppermute x2, waiting for transfers between devices: 2.38 us -> 0.8 us  [shards(): turned.append(lax.ppermute(normed, ('qrow', 'kcol'), swap))]
    all_to_all x1, blocking collectives: 20.9 us -> 19.6 us  [shards(): gathered = lax.all_to_all(partial, 'kcol', 0, 0)]
    all_to_all x1, starting transfers between devices: 9.5 us -> 8.58 us  [shards(): row_tokens = lax.all_to_all(copies, 'kcol', 0, 0, axis_index_groups=near)]
    all_to_all x1, starting transfers between devices: 4.95 us -> 5.71 us  [shards(): lax.all_to_all(turned_copies, 'qrow', 0, 0, axis_index_groups=sides)]
    ppermute x0 -> x1, waiting for transfers between devices: none -> 0.71 us  [shards(): lax.ppermute(row_tokens, 'kcol', [(i, (i + n_col // 2) % n_col) for i in...]
    pallas_call x2 -> x3, Pallas kernels: 10.2 us -> 10.5 us  [the longest x2 9.43 us: bias_of(): pl.pallas_call(functools.partial(bias_kernel, late * chunks * block, late...]
  transfers between devices with their start and end apart: 4 -> 5, of which waited for: 2 -> 3; matrix products, arithmetic and copies ran while one was open for 0% -> 0% of each run, Pallas kernels for 17% -> 18%
where the time goes in v8:
time: 63 us; the launch traced here: 61.9 us
  starting transfers between devices  21.5 us (34%)
  blocking collectives  19.6 us (31%)
  Pallas kernels  18.5 us (29%)
  waiting for transfers between devices  2.09 us (3%)
    all_to_all x1, blocking collectives, shards(): gathered = lax.all_to_all(partial, 'kcol', 0, 0)  19.6 us
    pallas_call x2, Pallas kernels, bias_of(): pl.pallas_call(functools.partial(bias_kernel, late * chunks * block, late...  9.43 us
    all_to_all x1, starting transfers between devices, shards(): row_tokens = lax.all_to_all(copies, 'kcol', 0, 0, axis_index_groups=near)  8.58 us
    all_to_all x1, starting transfers between devices, shards(): lax.all_to_all(turned_copies, 'qrow', 0, 0, axis_index_groups=sides)  5.71 us
    ppermute x2, starting transfers between devices, shards(): turned.append(lax.ppermute(normed, ('qrow', 'kcol'), swap))  5.34 us
    pallas_call x1, Pallas kernels, shards(): pl.pallas_call(attend_kernel, name='attend', out_shape=shape((n_col, rows...  4.07 us
    pallas_call x1, Pallas kernels, shards(): pl.pallas_call(norm_kernel, name='norm', out_shape=(shape((own, width), B...  1.85 us
    ppermute x1, starting transfers between devices, shards(): lax.ppermute(row_tokens, 'kcol', [(i, (i + n_col // 2) % n_col) for i in...  1.84 us
  transfers between devices with their start and end apart: 5, of which 3 were waited for; matrix products, arithmetic and copies ran while one was open for 0% of the time, Pallas kernels for 18%

profile of v8, /device:TPU:40, one launch (start us, length us, event | category | flops | bytes accessed | tf_op | source)
XLA Modules:
  0.0 61.9 jit_solution(17451274266858071166)
XLA Ops:
  0.0 1.8 %norm.1 = (bf16[16,768]{1,0:T(8,128)(2,1)S(1)}, bf16[8,16,768]{2,1,0:T(8,128)(2,1)}) custom-call(s32[8]{0:T(128)} %restype_hbm.1, bf16[2,8,768]{2,1,0:T(8,128)(2,1)} %single_hbm.1, bf16[32,768]{1,0:T(8,128)(2,1)} %table_hbm.1, f32[768]{0:T(1024)} %gain_hbm.1), custom_call_target="tpu_custom_call" | custom-call | tf_op jit(solution)/shard_map/norm/pallas_call | solution.py:336
  1.9 8.6 %all-to-all-start = ((bf16[8,16,768]{2,1,0:T(8,128)(2,1)}), bf16[8,16,768]{2,1,0:T(8,128)(2,1)S(1)}, u32[]{:S(2)}, u32[]{:S(2)}) async-start(bf16[8,16,768]{2,1,0:T(8,128)(2,1)} %get-tuple-element.16), calls=%async_computation | async-start | bytes 393216 | tf_op jit(solution)/shard_map/all_to_all | solution.py:358
  10.4 0.0 collective-permute-start.1
  10.4 5.3 %collective-permute-start = (bf16[16,768]{1,0:T(8,128)(2,1)S(1)}, bf16[16,768]{1,0:T(8,128)(2,1)S(1)}, u32[]{:S(2)}, u32[]{:S(2)}) collective-permute-start(bf16[16,768]{1,0:T(8,128)(2,1)S(1)} %get-tuple-element.14.own_ref), channel_id=1, source_target_pairs={{15,0},{14,16},{12,32},{13,48},{10,64},{8,80},{11,96},{9,112},{5,1... | collective-permute-start | bytes 73736 | tf_op jit(solution)/shard_map/ppermute | solution.py:356
  15.8 0.1 pad_add_fusion.where_ref
  15.9 4.7 %bias_0.1 = (f32[16,64,128]{2,1,0:T(8,128)}, f32[16,768]{1,0:T(8,128)}) custom-call(bf16[16,768]{1,0:T(8,128)(2,1)S(1)} %get-tuple-element.14.own_ref, s32[2]{0:T(128)S(1)} %pad_add_fusion.where_ref, s32[2048]{0:T(1024)} %refs_0_.3, f32[16]{0:T(128)} %refs_1_.3, s32[16,128]{1,0:T(8,128)} %bitcast.8, s32[1,128]{1,0:T(1,128)} %bitcast.12, f32[1,128]{1,0:T(1,128)} %bitcast.14, ...), custom_call_target="tpu_custom_call" | custom-call | flops 500000000 | bytes 10000000 | tf_op jit(solution)/shard_map/bias_0/pallas_call | solution.py:368
  20.5 0.0 collective-permute-done.1.two_ref
  20.5 0.8 %collective-permute-done.one_ref = bf16[16,768]{1,0:T(8,128)(2,1)S(1)} collective-permute-done((bf16[16,768]{1,0:T(8,128)(2,1)S(1)}, bf16[16,768]{1,0:T(8,128)(2,1)S(1)}, u32[]{:S(2)}, u32[]{:S(2)}) %collective-permute-start) | collective-permute-done | bytes 24608 | tf_op jit(solution)/shard_map/ppermute | solution.py:356
  21.3 0.8 %copies.1 = bf16[8,32,768]{2,1,0:T(8,128)(2,1)} custom-call(bf16[16,768]{1,0:T(8,128)(2,1)S(1)} %collective-permute-done.one_ref, bf16[16,768]{1,0:T(8,128)(2,1)S(1)} %collective-permute-done.1.two_ref, f32[16,64,128]{2,1,0:T(8,128)} %get-tuple-element.15.after_ref.bias_a_hbm), custom_call_target="tpu_custom_call" | custom-call | tf_op jit(solution)/shard_map/copies/pallas_call | solution.py:407
  22.1 0.0 all-to-all-done.rows_ref
  22.1 5.7 %all-to-all-start.1 = ((bf16[8,32,768]{2,1,0:T(8,128)(2,1)}), bf16[8,32,768]{2,1,0:T(8,128)(2,1)S(1)}, u32[]{:S(2)}, u32[]{:S(2)}) async-start(bf16[8,32,768]{2,1,0:T(8,128)(2,1)} %copies.1), calls=%async_computation.1 | async-start | bytes 786432 | tf_op jit(solution)/shard_map/all_to_all | solution.py:416
  27.8 0.0 copy-start.2
  27.8 1.8 %collective-permute-start.2 = (bf16[8,16,768]{2,1,0:T(8,128)(2,1)S(1)}, bf16[8,16,768]{2,1,0:T(8,128)(2,1)S(1)}, u32[]{:S(2)}, u32[]{:S(2)}) collective-permute-start(bf16[8,16,768]{2,1,0:T(8,128)(2,1)S(1)} %all-to-all-done.rows_ref), channel_id=1, source_target_pairs={{0,8},{1,9},{2,10},{3,11},{4,12},{5,13},{6,14},{7,15},{8,0},{9,1},... | collective-permute-start | bytes 589832 | tf_op jit(solution)/shard_map/ppermute | solution.py:417
  29.7 4.8 %bias_1.1 = (f32[16,64,128]{2,1,0:T(8,128)}, bf16[768,1536]{1,0:T(8,128)(2,1)S(1)}, bf16[768,768]{1,0:T(8,128)(2,1)S(1)}) custom-call(bf16[16,768]{1,0:T(8,128)(2,1)S(1)} %get-tuple-element.14.own_ref, s32[2]{0:T(128)S(1)} %pad_add_fusion.where_ref, s32[2048]{0:T(1024)} %refs_0_.3, f32[16]{0:T(128)} %refs_1_.3, s32[16,128]{1,0:T(8,128)} %bitcast.9, ...), custom_call_target="tpu_custom_call" | custom-call | flops 500000000 | bytes 10000000 | tf_op jit(solution)/shard_map/bias_1/pallas_call | solution.py:368
  34.4 0.7 %collective-permute-done.2.others_ref = bf16[8,16,768]{2,1,0:T(8,128)(2,1)S(1)} collective-permute-done((bf16[8,16,768]{2,1,0:T(8,128)(2,1)S(1)}, bf16[8,16,768]{2,1,0:T(8,128)(2,1)S(1)}, u32[]{:S(2)}, u32[]{:S(2)}) %collective-permute-start.2) | collective-permute-done | bytes 196640 | tf_op jit(solution)/shard_map/ppermute | solution.py:417
  35.2 1.0 %query.1.q_ref = bf16[2,128,768]{2,1,0:T(8,128)(2,1)S(1)} custom-call(s32[2]{0:T(128)S(1)} %pad_add_fusion.where_ref, bf16[8,16,768]{2,1,0:T(8,128)(2,1)S(1)} %all-to-all-done.rows_ref, bf16[8,16,768]{2,1,0:T(8,128)(2,1)S(1)} %collective-permute-done.2.others_ref, bf16[768,768]{1,0:T(8,128)(2,1)S(1)} %get-tuple-element.20.w_ref), custom_call_target="tpu_custom_call" | custom-call | tf_op jit(solution)/shard_map/query/pallas_call | solution.py:419
  36.2 0.6 all-to-all-done.1
  36.8 0.0 copy-done.2
  36.8 0.0 copy-start
  36.8 4.1 %attend.1 = bf16[16,104,128]{2,1,0:T(8,128)(2,1)S(1)} custom-call(s32[2]{0:T(128)S(1)} %pad_add_fusion.where_ref, s32[512]{0:T(512)S(1)} %copy-done.2, bf16[16,16,768]{2,1,0:T(8,128)(2,1)S(1)} %bitcast.7, bf16[768,1536]{1,0:T(8,128)(2,1)S(1)} %get-tuple-element.18.wkv_ref, bf16[2,128,768]{2,1,0:T(8,128)(2,1)S(1)} %query.1.q_ref, ...), custom_call_target="tpu_custom_call" | custom-call | tf_op jit(solution)/shard_map/attend/pallas_call | solution.py:432
  40.9 19.6 %all_to_all.15.parts_ref = bf16[16,104,128]{2,1,0:T(8,128)(2,1)S(1)} all-to-all(bf16[16,104,128]{2,1,0:T(8,128)(2,1)S(1)} %attend.1), channel_id=1, replica_groups=mesh['qrow'=16,'kcol'=16] {'kcol'}, dimensions={0} | all-to-all | bytes 851968 | tf_op jit(solution)/shard_map/all_to_all | solution.py:446
  60.5 0.0 copy-done
  60.5 0.0 copy-done.1
  60.5 1.4 %merge.1 = bf16[2,8,768]{2,1,0:T(8,128)(2,1)} custom-call(bf16[16,104,128]{2,1,0:T(8,128)(2,1)S(1)} %all_to_all.15.parts_ref, f32[16,768]{1,0:T(8,128)S(1)} %copy-done.1, bf16[768,768]{1,0:T(8,128)(2,1)S(1)} %copy-done), custom_call_target="tpu_custom_call" | custom-call | tf_op jit(solution)/shard_map/merge/pallas_call | solution.py:447
  (1 shorter events, 0.0 us)
Async XLA Ops:
  1.9 20.3 %all-to-all-start = ((bf16[8,16,768]{2,1,0:T(8,128)(2,1)}), bf16[8,16,768]{2,1,0:T(8,128)(2,1)S(1)}, u32[]{:S(2)}, u32[]{:S(2)}) async-start(bf16[8,16,768]{2,1,0:T(8,128)(2,1)} %get-tuple-element.16), calls=%async_computation | async-start | bytes 393216 | tf_op jit(solution)/shard_map/all_to_all | solution.py:358
  10.4 10.1 %collective-permute-start.1 = (bf16[16,768]{1,0:T(8,128)(2,1)S(1)}, bf16[16,768]{1,0:T(8,128)(2,1)S(1)}, u32[]{:S(2)}, u32[]{:S(2)}) collective-permute-start(bf16[16,768]{1,0:T(8,128)(2,1)S(1)} %get-tuple-element.14.own_ref), channel_id=1, source_target_pairs={{13,0},{12,16},{4,32},{15,48},{11,64},{9,80},{5,96},{14,112},{7,12... | collective-permute-start | bytes 73736 | tf_op jit(solution)/shard_map/ppermute | solution.py:356
  10.4 10.9 %collective-permute-start = (bf16[16,768]{1,0:T(8,128)(2,1)S(1)}, bf16[16,768]{1,0:T(8,128)(2,1)S(1)}, u32[]{:S(2)}, u32[]{:S(2)}) collective-permute-start(bf16[16,768]{1,0:T(8,128)(2,1)S(1)} %get-tuple-element.14.own_ref), channel_id=1, source_target_pairs={{15,0},{14,16},{12,32},{13,48},{10,64},{8,80},{11,96},{9,112},{5,1... | collective-permute-start | bytes 73736 | tf_op jit(solution)/shard_map/ppermute | solution.py:356
  22.1 14.7 %all-to-all-start.1 = ((bf16[8,32,768]{2,1,0:T(8,128)(2,1)}), bf16[8,32,768]{2,1,0:T(8,128)(2,1)S(1)}, u32[]{:S(2)}, u32[]{:S(2)}) async-start(bf16[8,32,768]{2,1,0:T(8,128)(2,1)} %copies.1), calls=%async_computation.1 | async-start | bytes 786432 | tf_op jit(solution)/shard_map/all_to_all | solution.py:416
  27.8 8.9 %copy-start.2 = (s32[512]{0:T(512)S(1)}, s32[512]{0:T(512)}, u32[]{:S(2)}) copy-start(s32[512]{0:T(512)} %constant.9.clone.order_ref) | copy-start | bytes 6148
  27.8 7.3 %collective-permute-start.2 = (bf16[8,16,768]{2,1,0:T(8,128)(2,1)S(1)}, bf16[8,16,768]{2,1,0:T(8,128)(2,1)S(1)}, u32[]{:S(2)}, u32[]{:S(2)}) collective-permute-start(bf16[8,16,768]{2,1,0:T(8,128)(2,1)S(1)} %all-to-all-done.rows_ref), channel_id=1, source_target_pairs={{0,8},{1,9},{2,10},{3,11},{4,12},{5,13},{6,14},{7,15},{8,0},{9,1},... | collective-permute-start | bytes 589832 | tf_op jit(solution)/shard_map/ppermute | solution.py:417
  36.8 23.7 %copy-start = (bf16[768,768]{1,0:T(8,128)(2,1)S(1)}, bf16[768,768]{1,0:T(8,128)(2,1)}, u32[]{:S(2)}) copy-start(bf16[768,768]{1,0:T(8,128)(2,1)} %wout_ref.1) | copy-start | bytes 3538948
  36.8 23.7 %copy-start.1 = (f32[16,768]{1,0:T(8,128)S(1)}, f32[16,768]{1,0:T(8,128)}, u32[]{:S(2)}) copy-start(f32[16,768]{1,0:T(8,128)} %get-tuple-element.22.gate_ref) | copy-start | bytes 147460

commit v9 on v8

--- a/solution.py
+++ b/solution.py
@@ -193,7 +193,7 @@
         return jnp.where((spot >= h * size) & (spot < (h + 1) * size), 1.0, 0.0).astype(BF)
 
     lane = lax.broadcasted_iota(jnp.int32, (queries, 128), 1)
-    stats = jnp.zeros((queries, 128), F32)
+    stats = []
     for s in range(2):
         q = q_ref[s]
         k = kf[:, s].reshape(keys, width).astype(BF)
@@ -230,11 +230,12 @@
             tiles = [o[:, i * 128 : (i + 1) * 128].reshape(parts, half, 128) for i in range(2)]
             out_ref[:, at : at + per, :] = jnp.concatenate(tiles, 1).astype(BF)
         hi, mid, low = split3(tops)
+        total_hi, total_low, _ = split3(tots)
         mine = hi.astype(F32)
-        for i, p in enumerate((mid.astype(F32), low.astype(F32), tots)):
-            mine = mine + pltpu.roll(p, heads * (i + 1), 1)
-        stats = stats + (pltpu.roll(mine, 64, 1) if s else mine)
-    out_ref[:, 2 * wins * per :, :] = stats.reshape(parts, half, 128).astype(BF)
+        for i, p in enumerate((mid, low, total_hi, total_low)):
+            mine = mine + pltpu.roll(p.astype(F32), heads * (i + 1), 1)
+        stats.append(mine.reshape(parts, half, 128))
+    out_ref[:, 2 * wins * per :, :] = jnp.concatenate(stats, 1).astype(BF)
 
 
 def merge_kernel(parts_ref, gate_ref, wout_ref, out_ref):
@@ -244,11 +245,9 @@
     tiles = width // 128
     heads = 16
     size = width // heads
-    both = parts_ref[:, tiles * per :, :].astype(F32).reshape(parts, 1, half, 128)
-    other = pltpu.roll(both.reshape(parts * half, 128), 64, 1).reshape(parts, 1, half, 128)
-    st = jnp.concatenate([both, other], 1).reshape(parts * per, 128)
+    st = parts_ref[:, tiles * per :, :].astype(F32).reshape(parts * per, 128)
     top = st + pltpu.roll(st, 128 - heads, 1) + pltpu.roll(st, 128 - 2 * heads, 1)
-    tot = pltpu.roll(st, 128 - 3 * heads, 1)
+    tot = pltpu.roll(st, 128 - 3 * heads, 1) + pltpu.roll(st, 128 - 4 * heads, 1)
     lane = lax.broadcasted_iota(jnp.int32, (parts * per, 128), 1)
     top = jnp.where(lane < heads, top, 0.0).reshape(parts, per, 128)
     tot = jnp.where(lane < heads, tot, 1.0).reshape(parts, per, 128)
@@ -428,7 +427,7 @@
     order = [tables[k][c][i] for c in range(n_col) for side in sides for i in side for k in range(2)]
     order = jnp.asarray(order, jnp.int32)
 
-    rows = own * width // 128 + tok
+    rows = own * width // 128 + own
     partial = pl.pallas_call(
         attend_kernel,
         name="attend",

time: 63 us -> 63.6 us (level)
  blocking collectives: 19.6 us -> 20.4 us
    all_to_all x1, blocking collectives: 19.6 us -> 20.4 us  [shards(): gathered = lax.all_to_all(partial, 'kcol', 0, 0)]
where the time goes in v9:
time: 63.6 us; the launch traced here: 62.5 us
  starting transfers between devices  21.5 us (34%)
  blocking collectives  20.4 us (32%)
  Pallas kernels  18.4 us (29%)
  waiting for transfers between devices  2.09 us (3%)
    all_to_all x1, blocking collectives, shards(): gathered = lax.all_to_all(partial, 'kcol', 0, 0)  20.4 us
    pallas_call x2, Pallas kernels, bias_of(): pl.pallas_call(functools.partial(bias_kernel, late * chunks * block, late...  9.43 us
    all_to_all x1, starting transfers between devices, shards(): row_tokens = lax.all_to_all(copies, 'kcol', 0, 0, axis_index_groups=near)  8.58 us
    all_to_all x1, starting transfers between devices, shards(): lax.all_to_all(turned_copies, 'qrow', 0, 0, axis_index_groups=sides)  5.71 us
    ppermute x2, starting transfers between devices, shards(): turned.append(lax.ppermute(normed, ('qrow', 'kcol'), swap))  5.34 us
    pallas_call x1, Pallas kernels, shards(): pl.pallas_call(attend_kernel, name='attend', out_shape=shape((n_col, rows...  3.97 us
    pallas_call x1, Pallas kernels, shards(): pl.pallas_call(norm_kernel, name='norm', out_shape=(shape((own, width), B...  1.85 us
    ppermute x1, starting transfers between devices, shards(): lax.ppermute(row_tokens, 'kcol', [(i, (i + n_col // 2) % n_col) for i in...  1.84 us
  transfers between devices with their start and end apart: 5, of which 3 were waited for; matrix products, arithmetic and copies ran while one was open for 0% of the time, Pallas kernels for 18%

profile of v9, /device:TPU:40, one launch (start us, length us, event | category | flops | bytes accessed | tf_op | source)
XLA Modules:
  0.0 62.5 jit_solution(3045034443735325404)
XLA Ops:
  0.0 1.8 %norm.1 = (bf16[16,768]{1,0:T(8,128)(2,1)S(1)}, bf16[8,16,768]{2,1,0:T(8,128)(2,1)}) custom-call(s32[8]{0:T(128)} %restype_hbm.1, bf16[2,8,768]{2,1,0:T(8,128)(2,1)} %single_hbm.1, bf16[32,768]{1,0:T(8,128)(2,1)} %table_hbm.1, f32[768]{0:T(1024)} %gain_hbm.1), custom_call_target="tpu_custom_call" | custom-call | tf_op jit(solution)/shard_map/norm/pallas_call | solution.py:335
  1.9 8.6 %all-to-all-start = ((bf16[8,16,768]{2,1,0:T(8,128)(2,1)}), bf16[8,16,768]{2,1,0:T(8,128)(2,1)S(1)}, u32[]{:S(2)}, u32[]{:S(2)}) async-start(bf16[8,16,768]{2,1,0:T(8,128)(2,1)} %get-tuple-element.16), calls=%async_computation | async-start | bytes 393216 | tf_op jit(solution)/shard_map/all_to_all | solution.py:357
  10.4 0.0 collective-permute-start.1
  10.4 5.3 %collective-permute-start = (bf16[16,768]{1,0:T(8,128)(2,1)S(1)}, bf16[16,768]{1,0:T(8,128)(2,1)S(1)}, u32[]{:S(2)}, u32[]{:S(2)}) collective-permute-start(bf16[16,768]{1,0:T(8,128)(2,1)S(1)} %get-tuple-element.14.own_ref), channel_id=1, source_target_pairs={{15,0},{14,16},{12,32},{13,48},{10,64},{8,80},{11,96},{9,112},{5,1... | collective-permute-start | bytes 73736 | tf_op jit(solution)/shard_map/ppermute | solution.py:355
  15.8 0.1 pad_add_fusion.where_ref
  15.9 4.7 %bias_0.1 = (f32[16,64,128]{2,1,0:T(8,128)}, f32[16,768]{1,0:T(8,128)}) custom-call(bf16[16,768]{1,0:T(8,128)(2,1)S(1)} %get-tuple-element.14.own_ref, s32[2]{0:T(128)S(1)} %pad_add_fusion.where_ref, s32[2048]{0:T(1024)} %refs_0_.3, f32[16]{0:T(128)} %refs_1_.3, s32[16,128]{1,0:T(8,128)} %bitcast.8, s32[1,128]{1,0:T(1,128)} %bitcast.12, f32[1,128]{1,0:T(1,128)} %bitcast.14, ...), custom_call_target="tpu_custom_call" | custom-call | flops 500000000 | bytes 10000000 | tf_op jit(solution)/shard_map/bias_0/pallas_call | solution.py:367
  20.5 0.0 collective-permute-done.1.two_ref
  20.5 0.8 %collective-permute-done.one_ref = bf16[16,768]{1,0:T(8,128)(2,1)S(1)} collective-permute-done((bf16[16,768]{1,0:T(8,128)(2,1)S(1)}, bf16[16,768]{1,0:T(8,128)(2,1)S(1)}, u32[]{:S(2)}, u32[]{:S(2)}) %collective-permute-start) | collective-permute-done | bytes 24608 | tf_op jit(solution)/shard_map/ppermute | solution.py:355
  21.3 0.8 %copies.1 = bf16[8,32,768]{2,1,0:T(8,128)(2,1)} custom-call(bf16[16,768]{1,0:T(8,128)(2,1)S(1)} %collective-permute-done.one_ref, bf16[16,768]{1,0:T(8,128)(2,1)S(1)} %collective-permute-done.1.two_ref, f32[16,64,128]{2,1,0:T(8,128)} %get-tuple-element.15.after_ref.bias_a_hbm), custom_call_target="tpu_custom_call" | custom-call | tf_op jit(solution)/shard_map/copies/pallas_call | solution.py:406
  22.1 0.0 all-to-all-done.rows_ref
  22.1 5.7 %all-to-all-start.1 = ((bf16[8,32,768]{2,1,0:T(8,128)(2,1)}), bf16[8,32,768]{2,1,0:T(8,128)(2,1)S(1)}, u32[]{:S(2)}, u32[]{:S(2)}) async-start(bf16[8,32,768]{2,1,0:T(8,128)(2,1)} %copies.1), calls=%async_computation.1 | async-start | bytes 786432 | tf_op jit(solution)/shard_map/all_to_all | solution.py:415
  27.8 0.0 copy-start.2
  27.8 1.8 %collective-permute-start.2 = (bf16[8,16,768]{2,1,0:T(8,128)(2,1)S(1)}, bf16[8,16,768]{2,1,0:T(8,128)(2,1)S(1)}, u32[]{:S(2)}, u32[]{:S(2)}) collective-permute-start(bf16[8,16,768]{2,1,0:T(8,128)(2,1)S(1)} %all-to-all-done.rows_ref), channel_id=1, source_target_pairs={{0,8},{1,9},{2,10},{3,11},{4,12},{5,13},{6,14},{7,15},{8,0},{9,1},... | collective-permute-start | bytes 589832 | tf_op jit(solution)/shard_map/ppermute | solution.py:416
  29.7 4.8 %bias_1.1 = (f32[16,64,128]{2,1,0:T(8,128)}, bf16[768,1536]{1,0:T(8,128)(2,1)S(1)}, bf16[768,768]{1,0:T(8,128)(2,1)S(1)}) custom-call(bf16[16,768]{1,0:T(8,128)(2,1)S(1)} %get-tuple-element.14.own_ref, s32[2]{0:T(128)S(1)} %pad_add_fusion.where_ref, s32[2048]{0:T(1024)} %refs_0_.3, f32[16]{0:T(128)} %refs_1_.3, s32[16,128]{1,0:T(8,128)} %bitcast.9, ...), custom_call_target="tpu_custom_call" | custom-call | flops 500000000 | bytes 10000000 | tf_op jit(solution)/shard_map/bias_1/pallas_call | solution.py:367
  34.4 0.7 %collective-permute-done.2.others_ref = bf16[8,16,768]{2,1,0:T(8,128)(2,1)S(1)} collective-permute-done((bf16[8,16,768]{2,1,0:T(8,128)(2,1)S(1)}, bf16[8,16,768]{2,1,0:T(8,128)(2,1)S(1)}, u32[]{:S(2)}, u32[]{:S(2)}) %collective-permute-start.2) | collective-permute-done | bytes 196640 | tf_op jit(solution)/shard_map/ppermute | solution.py:416
  35.2 1.0 %query.1.q_ref = bf16[2,128,768]{2,1,0:T(8,128)(2,1)S(1)} custom-call(s32[2]{0:T(128)S(1)} %pad_add_fusion.where_ref, bf16[8,16,768]{2,1,0:T(8,128)(2,1)S(1)} %all-to-all-done.rows_ref, bf16[8,16,768]{2,1,0:T(8,128)(2,1)S(1)} %collective-permute-done.2.others_ref, bf16[768,768]{1,0:T(8,128)(2,1)S(1)} %get-tuple-element.20.w_ref), custom_call_target="tpu_custom_call" | custom-call | tf_op jit(solution)/shard_map/query/pallas_call | solution.py:418
  36.2 0.6 all-to-all-done.1
  36.8 0.0 copy-done.2
  36.8 0.0 copy-start
  36.8 4.0 %attend.1 = bf16[16,112,128]{2,1,0:T(8,128)(2,1)S(1)} custom-call(s32[2]{0:T(128)S(1)} %pad_add_fusion.where_ref, s32[512]{0:T(512)S(1)} %copy-done.2, bf16[16,16,768]{2,1,0:T(8,128)(2,1)S(1)} %bitcast.7, bf16[768,1536]{1,0:T(8,128)(2,1)S(1)} %get-tuple-element.18.wkv_ref, bf16[2,128,768]{2,1,0:T(8,128)(2,1)S(1)} %query.1.q_ref, ...), custom_call_target="tpu_custom_call" | custom-call | tf_op jit(solution)/shard_map/attend/pallas_call | solution.py:431
  40.7 20.4 %all_to_all.15.parts_ref = bf16[16,112,128]{2,1,0:T(8,128)(2,1)S(1)} all-to-all(bf16[16,112,128]{2,1,0:T(8,128)(2,1)S(1)} %attend.1), channel_id=1, replica_groups=mesh['qrow'=16,'kcol'=16] {'kcol'}, dimensions={0} | all-to-all | bytes 917504 | tf_op jit(solution)/shard_map/all_to_all | solution.py:445
  61.2 0.0 copy-done
  61.2 0.0 copy-done.1
  61.2 1.3 %merge.1 = bf16[2,8,768]{2,1,0:T(8,128)(2,1)} custom-call(bf16[16,112,128]{2,1,0:T(8,128)(2,1)S(1)} %all_to_all.15.parts_ref, f32[16,768]{1,0:T(8,128)S(1)} %copy-done.1, bf16[768,768]{1,0:T(8,128)(2,1)S(1)} %copy-done), custom_call_target="tpu_custom_call" | custom-call | tf_op jit(solution)/shard_map/merge/pallas_call | solution.py:446
  (1 shorter events, 0.0 us)
Async XLA Ops:
  1.9 20.3 %all-to-all-start = ((bf16[8,16,768]{2,1,0:T(8,128)(2,1)}), bf16[8,16,768]{2,1,0:T(8,128)(2,1)S(1)}, u32[]{:S(2)}, u32[]{:S(2)}) async-start(bf16[8,16,768]{2,1,0:T(8,128)(2,1)} %get-tuple-element.16), calls=%async_computation | async-start | bytes 393216 | tf_op jit(solution)/shard_map/all_to_all | solution.py:357
  10.4 10.1 %collective-permute-start.1 = (bf16[16,768]{1,0:T(8,128)(2,1)S(1)}, bf16[16,768]{1,0:T(8,128)(2,1)S(1)}, u32[]{:S(2)}, u32[]{:S(2)}) collective-permute-start(bf16[16,768]{1,0:T(8,128)(2,1)S(1)} %get-tuple-element.14.own_ref), channel_id=1, source_target_pairs={{13,0},{12,16},{4,32},{15,48},{11,64},{9,80},{5,96},{14,112},{7,12... | collective-permute-start | bytes 73736 | tf_op jit(solution)/shard_map/ppermute | solution.py:355
  10.4 10.9 %collective-permute-start = (bf16[16,768]{1,0:T(8,128)(2,1)S(1)}, bf16[16,768]{1,0:T(8,128)(2,1)S(1)}, u32[]{:S(2)}, u32[]{:S(2)}) collective-permute-start(bf16[16,768]{1,0:T(8,128)(2,1)S(1)} %get-tuple-element.14.own_ref), channel_id=1, source_target_pairs={{15,0},{14,16},{12,32},{13,48},{10,64},{8,80},{11,96},{9,112},{5,1... | collective-permute-start | bytes 73736 | tf_op jit(solution)/shard_map/ppermute | solution.py:355
  22.1 14.7 %all-to-all-start.1 = ((bf16[8,32,768]{2,1,0:T(8,128)(2,1)}), bf16[8,32,768]{2,1,0:T(8,128)(2,1)S(1)}, u32[]{:S(2)}, u32[]{:S(2)}) async-start(bf16[8,32,768]{2,1,0:T(8,128)(2,1)} %copies.1), calls=%async_computation.1 | async-start | bytes 786432 | tf_op jit(solution)/shard_map/all_to_all | solution.py:415
  27.8 8.9 %copy-start.2 = (s32[512]{0:T(512)S(1)}, s32[512]{0:T(512)}, u32[]{:S(2)}) copy-start(s32[512]{0:T(512)} %constant.9.clone.order_ref) | copy-start | bytes 6148
  27.8 7.3 %collective-permute-start.2 = (bf16[8,16,768]{2,1,0:T(8,128)(2,1)S(1)}, bf16[8,16,768]{2,1,0:T(8,128)(2,1)S(1)}, u32[]{:S(2)}, u32[]{:S(2)}) collective-permute-start(bf16[8,16,768]{2,1,0:T(8,128)(2,1)S(1)} %all-to-all-done.rows_ref), channel_id=1, source_target_pairs={{0,8},{1,9},{2,10},{3,11},{4,12},{5,13},{6,14},{7,15},{8,0},{9,1},... | collective-permute-start | bytes 589832 | tf_op jit(solution)/shard_map/ppermute | solution.py:416
  36.8 24.4 %copy-start = (bf16[768,768]{1,0:T(8,128)(2,1)S(1)}, bf16[768,768]{1,0:T(8,128)(2,1)}, u32[]{:S(2)}) copy-start(bf16[768,768]{1,0:T(8,128)(2,1)} %wout_ref.1) | copy-start | bytes 3538948
  36.8 24.4 %copy-start.1 = (f32[16,768]{1,0:T(8,128)S(1)}, f32[16,768]{1,0:T(8,128)}, u32[]{:S(2)}) copy-start(f32[16,768]{1,0:T(8,128)} %get-tuple-element.22.gate_ref) | copy-start | bytes 147460

commit v10 on v9

--- a/solution.py
+++ b/solution.py
@@ -59,7 +59,9 @@
         ],
         sems,
     )
-    samples, tok, width = single_ref.shape
+    rows, width = single_ref.shape
+    tok = restype_ref.shape[0]
+    samples = rows // tok
     kinds = table_ref.shape[0]
     row = lax.broadcasted_iota(jnp.int32, (tok, kinds), 0)
     col = lax.broadcasted_iota(jnp.int32, (tok, kinds), 1)
@@ -68,7 +70,7 @@
         kind = jnp.where(row == t, restype_ref[t], kind)
     one_hot = jnp.where(kind == col, 1.0, 0.0).astype(BF)
     emb = jnp.dot(one_hot, table_ref[...], preferred_element_type=F32)
-    x = single_ref[...].astype(F32) + emb[None]
+    x = single_ref[...].astype(F32).reshape(samples, tok, width) + emb[None]
     normed = layer_norm(x) * gain_ref[...].reshape(1, 1, width)
     normed = normed.reshape(samples * tok, width).astype(BF)
     normed_ref[...] = normed
@@ -340,13 +342,13 @@
         out_specs=(vmem(), vmem()),
         scratch_shapes=[
             pltpu.SMEM((tok,), jnp.int32),
-            pltpu.VMEM((samples, tok, width), BF),
+            pltpu.VMEM((own, width), BF),
             pltpu.VMEM(restype_table.shape, BF),
             pltpu.VMEM((width,), F32),
             dma((4,)),
         ],
         compiler_params=params(4),
-    )(*stay(restype, single, restype_table, single_gain))
+    )(*stay(restype, single.reshape(own, width), restype_table, single_gain))
 
     tables = near_swaps(n_row)
     turned = []

time: 63.6 us -> 63.6 us (level)
  no operation moved by 1% of the time
where the time goes in v10:
time: 63.6 us; the launch traced here: 62.5 us
  starting transfers between devices  21.5 us (34%)
  blocking collectives  20.4 us (32%)
  Pallas kernels  18.4 us (29%)
  waiting for transfers between devices  2.09 us (3%)
    all_to_all x1, blocking collectives, shards(): gathered = lax.all_to_all(partial, 'kcol', 0, 0)  20.4 us
    pallas_call x2, Pallas kernels, bias_of(): pl.pallas_call(functools.partial(bias_kernel, late * chunks * block, late...  9.43 us
    all_to_all x1, starting transfers between devices, shards(): row_tokens = lax.all_to_all(copies, 'kcol', 0, 0, axis_index_groups=near)  8.58 us
    all_to_all x1, starting transfers between devices, shards(): lax.all_to_all(turned_copies, 'qrow', 0, 0, axis_index_groups=sides)  5.71 us
    ppermute x2, starting transfers between devices, shards(): turned.append(lax.ppermute(normed, ('qrow', 'kcol'), swap))  5.34 us
    pallas_call x1, Pallas kernels, shards(): pl.pallas_call(attend_kernel, name='attend', out_shape=shape((n_col, rows...  3.97 us
    pallas_call x1, Pallas kernels, shards(): pl.pallas_call(norm_kernel, name='norm', out_shape=(shape((own, width), B...  1.85 us
    ppermute x1, starting transfers between devices, shards(): lax.ppermute(row_tokens, 'kcol', [(i, (i + n_col // 2) % n_col) for i in...  1.84 us
  transfers between devices with their start and end apart: 5, of which 3 were waited for; matrix products, arithmetic and copies ran while one was open for 0% of the time, Pallas kernels for 18%

profile of v10, /device:TPU:40, one launch (start us, length us, event | category | flops | bytes accessed | tf_op | source)
XLA Modules:
  0.0 62.5 jit_solution(3045034443735325404)
XLA Ops:
  0.0 1.8 %norm.1 = (bf16[16,768]{1,0:T(8,128)(2,1)S(1)}, bf16[8,16,768]{2,1,0:T(8,128)(2,1)}) custom-call(s32[8]{0:T(128)} %restype_hbm.1, bf16[16,768]{1,0:T(8,128)(2,1)} %bitcast.13, bf16[32,768]{1,0:T(8,128)(2,1)} %table_hbm.1, f32[768]{0:T(1024)} %gain_hbm.1), custom_call_target="tpu_custom_call" | custom-call | tf_op jit(solution)/shard_map/norm/pallas_call | solution.py:337
  1.9 8.6 %all-to-all-start = ((bf16[8,16,768]{2,1,0:T(8,128)(2,1)}), bf16[8,16,768]{2,1,0:T(8,128)(2,1)S(1)}, u32[]{:S(2)}, u32[]{:S(2)}) async-start(bf16[8,16,768]{2,1,0:T(8,128)(2,1)} %get-tuple-element.16), calls=%async_computation | async-start | bytes 393216 | tf_op jit(solution)/shard_map/all_to_all | solution.py:359
  10.4 0.0 collective-permute-start.1
  10.4 5.3 %collective-permute-start = (bf16[16,768]{1,0:T(8,128)(2,1)S(1)}, bf16[16,768]{1,0:T(8,128)(2,1)S(1)}, u32[]{:S(2)}, u32[]{:S(2)}) collective-permute-start(bf16[16,768]{1,0:T(8,128)(2,1)S(1)} %get-tuple-element.14.own_ref), channel_id=1, source_target_pairs={{15,0},{14,16},{12,32},{13,48},{10,64},{8,80},{11,96},{9,112},{5,1... | collective-permute-start | bytes 73736 | tf_op jit(solution)/shard_map/ppermute | solution.py:357
  15.8 0.1 pad_add_fusion.where_ref
  15.9 4.7 %bias_0.1 = (f32[16,64,128]{2,1,0:T(8,128)}, f32[16,768]{1,0:T(8,128)}) custom-call(bf16[16,768]{1,0:T(8,128)(2,1)S(1)} %get-tuple-element.14.own_ref, s32[2]{0:T(128)S(1)} %pad_add_fusion.where_ref, s32[2048]{0:T(1024)} %refs_0_.3, f32[16]{0:T(128)} %refs_1_.3, s32[16,128]{1,0:T(8,128)} %bitcast.9, s32[1,128]{1,0:T(1,128)} %bitcast.14, f32[1,128]{1,0:T(1,128)} %bitcast.16, ...), custom_call_target="tpu_custom_call" | custom-call | flops 500000000 | bytes 10000000 | tf_op jit(solution)/shard_map/bias_0/pallas_call | solution.py:369
  20.5 0.0 collective-permute-done.1.two_ref
  20.5 0.8 %collective-permute-done.one_ref = bf16[16,768]{1,0:T(8,128)(2,1)S(1)} collective-permute-done((bf16[16,768]{1,0:T(8,128)(2,1)S(1)}, bf16[16,768]{1,0:T(8,128)(2,1)S(1)}, u32[]{:S(2)}, u32[]{:S(2)}) %collective-permute-start) | collective-permute-done | bytes 24608 | tf_op jit(solution)/shard_map/ppermute | solution.py:357
  21.3 0.8 %copies.1 = bf16[8,32,768]{2,1,0:T(8,128)(2,1)} custom-call(bf16[16,768]{1,0:T(8,128)(2,1)S(1)} %collective-permute-done.one_ref, bf16[16,768]{1,0:T(8,128)(2,1)S(1)} %collective-permute-done.1.two_ref, f32[16,64,128]{2,1,0:T(8,128)} %get-tuple-element.15.after_ref.bias_a_hbm), custom_call_target="tpu_custom_call" | custom-call | tf_op jit(solution)/shard_map/copies/pallas_call | solution.py:408
  22.1 0.0 all-to-all-done.rows_ref
  22.1 5.7 %all-to-all-start.1 = ((bf16[8,32,768]{2,1,0:T(8,128)(2,1)}), bf16[8,32,768]{2,1,0:T(8,128)(2,1)S(1)}, u32[]{:S(2)}, u32[]{:S(2)}) async-start(bf16[8,32,768]{2,1,0:T(8,128)(2,1)} %copies.1), calls=%async_computation.1 | async-start | bytes 786432 | tf_op jit(solution)/shard_map/all_to_all | solution.py:417
  27.8 0.0 copy-start.2
  27.8 1.8 %collective-permute-start.2 = (bf16[8,16,768]{2,1,0:T(8,128)(2,1)S(1)}, bf16[8,16,768]{2,1,0:T(8,128)(2,1)S(1)}, u32[]{:S(2)}, u32[]{:S(2)}) collective-permute-start(bf16[8,16,768]{2,1,0:T(8,128)(2,1)S(1)} %all-to-all-done.rows_ref), channel_id=1, source_target_pairs={{0,8},{1,9},{2,10},{3,11},{4,12},{5,13},{6,14},{7,15},{8,0},{9,1},... | collective-permute-start | bytes 589832 | tf_op jit(solution)/shard_map/ppermute | solution.py:418
  29.7 4.8 %bias_1.1 = (f32[16,64,128]{2,1,0:T(8,128)}, bf16[768,1536]{1,0:T(8,128)(2,1)S(1)}, bf16[768,768]{1,0:T(8,128)(2,1)S(1)}) custom-call(bf16[16,768]{1,0:T(8,128)(2,1)S(1)} %get-tuple-element.14.own_ref, s32[2]{0:T(128)S(1)} %pad_add_fusion.where_ref, s32[2048]{0:T(1024)} %refs_0_.3, f32[16]{0:T(128)} %refs_1_.3, s32[16,128]{1,0:T(8,128)} %bitcast.10, ...), custom_call_target="tpu_custom_call" | custom-call | flops 500000000 | bytes 10000000 | tf_op jit(solution)/shard_map/bias_1/pallas_call | solution.py:369
  34.4 0.7 %collective-permute-done.2.others_ref = bf16[8,16,768]{2,1,0:T(8,128)(2,1)S(1)} collective-permute-done((bf16[8,16,768]{2,1,0:T(8,128)(2,1)S(1)}, bf16[8,16,768]{2,1,0:T(8,128)(2,1)S(1)}, u32[]{:S(2)}, u32[]{:S(2)}) %collective-permute-start.2) | collective-permute-done | bytes 196640 | tf_op jit(solution)/shard_map/ppermute | solution.py:418
  35.2 1.0 %query.1.q_ref = bf16[2,128,768]{2,1,0:T(8,128)(2,1)S(1)} custom-call(s32[2]{0:T(128)S(1)} %pad_add_fusion.where_ref, bf16[8,16,768]{2,1,0:T(8,128)(2,1)S(1)} %all-to-all-done.rows_ref, bf16[8,16,768]{2,1,0:T(8,128)(2,1)S(1)} %collective-permute-done.2.others_ref, bf16[768,768]{1,0:T(8,128)(2,1)S(1)} %get-tuple-element.20.w_ref), custom_call_target="tpu_custom_call" | custom-call | tf_op jit(solution)/shard_map/query/pallas_call | solution.py:420
  36.2 0.6 all-to-all-done.1
  36.8 0.0 copy-done.2
  36.8 0.0 copy-start
  36.8 4.0 %attend.1 = bf16[16,112,128]{2,1,0:T(8,128)(2,1)S(1)} custom-call(s32[2]{0:T(128)S(1)} %pad_add_fusion.where_ref, s32[512]{0:T(512)S(1)} %copy-done.2, bf16[16,16,768]{2,1,0:T(8,128)(2,1)S(1)} %bitcast.8, bf16[768,1536]{1,0:T(8,128)(2,1)S(1)} %get-tuple-element.18.wkv_ref, bf16[2,128,768]{2,1,0:T(8,128)(2,1)S(1)} %query.1.q_ref, ...), custom_call_target="tpu_custom_call" | custom-call | tf_op jit(solution)/shard_map/attend/pallas_call | solution.py:433
  40.7 20.4 %all_to_all.15.parts_ref = bf16[16,112,128]{2,1,0:T(8,128)(2,1)S(1)} all-to-all(bf16[16,112,128]{2,1,0:T(8,128)(2,1)S(1)} %attend.1), channel_id=1, replica_groups=mesh['qrow'=16,'kcol'=16] {'kcol'}, dimensions={0} | all-to-all | bytes 917504 | tf_op jit(solution)/shard_map/all_to_all | solution.py:447
  61.2 0.0 copy-done
  61.2 0.0 copy-done.1
  61.2 1.3 %merge.1 = bf16[2,8,768]{2,1,0:T(8,128)(2,1)} custom-call(bf16[16,112,128]{2,1,0:T(8,128)(2,1)S(1)} %all_to_all.15.parts_ref, f32[16,768]{1,0:T(8,128)S(1)} %copy-done.1, bf16[768,768]{1,0:T(8,128)(2,1)S(1)} %copy-done), custom_call_target="tpu_custom_call" | custom-call | tf_op jit(solution)/shard_map/merge/pallas_call | solution.py:448
  (1 shorter events, 0.0 us)
Async XLA Ops:
  1.9 20.3 %all-to-all-start = ((bf16[8,16,768]{2,1,0:T(8,128)(2,1)}), bf16[8,16,768]{2,1,0:T(8,128)(2,1)S(1)}, u32[]{:S(2)}, u32[]{:S(2)}) async-start(bf16[8,16,768]{2,1,0:T(8,128)(2,1)} %get-tuple-element.16), calls=%async_computation | async-start | bytes 393216 | tf_op jit(solution)/shard_map/all_to_all | solution.py:359
  10.4 10.1 %collective-permute-start.1 = (bf16[16,768]{1,0:T(8,128)(2,1)S(1)}, bf16[16,768]{1,0:T(8,128)(2,1)S(1)}, u32[]{:S(2)}, u32[]{:S(2)}) collective-permute-start(bf16[16,768]{1,0:T(8,128)(2,1)S(1)} %get-tuple-element.14.own_ref), channel_id=1, source_target_pairs={{13,0},{12,16},{4,32},{15,48},{11,64},{9,80},{5,96},{14,112},{7,12... | collective-permute-start | bytes 73736 | tf_op jit(solution)/shard_map/ppermute | solution.py:357
  10.4 10.9 %collective-permute-start = (bf16[16,768]{1,0:T(8,128)(2,1)S(1)}, bf16[16,768]{1,0:T(8,128)(2,1)S(1)}, u32[]{:S(2)}, u32[]{:S(2)}) collective-permute-start(bf16[16,768]{1,0:T(8,128)(2,1)S(1)} %get-tuple-element.14.own_ref), channel_id=1, source_target_pairs={{15,0},{14,16},{12,32},{13,48},{10,64},{8,80},{11,96},{9,112},{5,1... | collective-permute-start | bytes 73736 | tf_op jit(solution)/shard_map/ppermute | solution.py:357
  22.1 14.7 %all-to-all-start.1 = ((bf16[8,32,768]{2,1,0:T(8,128)(2,1)}), bf16[8,32,768]{2,1,0:T(8,128)(2,1)S(1)}, u32[]{:S(2)}, u32[]{:S(2)}) async-start(bf16[8,32,768]{2,1,0:T(8,128)(2,1)} %copies.1), calls=%async_computation.1 | async-start | bytes 786432 | tf_op jit(solution)/shard_map/all_to_all | solution.py:417
  27.8 8.9 %copy-start.2 = (s32[512]{0:T(512)S(1)}, s32[512]{0:T(512)}, u32[]{:S(2)}) copy-start(s32[512]{0:T(512)} %constant.9.clone.order_ref) | copy-start | bytes 6148
  27.8 7.3 %collective-permute-start.2 = (bf16[8,16,768]{2,1,0:T(8,128)(2,1)S(1)}, bf16[8,16,768]{2,1,0:T(8,128)(2,1)S(1)}, u32[]{:S(2)}, u32[]{:S(2)}) collective-permute-start(bf16[8,16,768]{2,1,0:T(8,128)(2,1)S(1)} %all-to-all-done.rows_ref), channel_id=1, source_target_pairs={{0,8},{1,9},{2,10},{3,11},{4,12},{5,13},{6,14},{7,15},{8,0},{9,1},... | collective-permute-start | bytes 589832 | tf_op jit(solution)/shard_map/ppermute | solution.py:418
  36.8 24.4 %copy-start = (bf16[768,768]{1,0:T(8,128)(2,1)S(1)}, bf16[768,768]{1,0:T(8,128)(2,1)}, u32[]{:S(2)}) copy-start(bf16[768,768]{1,0:T(8,128)(2,1)} %wout_ref.1) | copy-start | bytes 3538948
  36.8 24.4 %copy-start.1 = (f32[16,768]{1,0:T(8,128)S(1)}, f32[16,768]{1,0:T(8,128)}, u32[]{:S(2)}) copy-start(f32[16,768]{1,0:T(8,128)} %get-tuple-element.22.gate_ref) | copy-start | bytes 147460

commit v11 on v10

--- a/solution.py
+++ b/solution.py
@@ -362,12 +362,12 @@
     block = row_len // 8
 
     def bias_of(late):
-        chunks = 4
+        chunks = 5 if late else 3
         out = [pltpu.HBM((heads, chunks * block, col_len), F32)]
         out += [shape((width, 2 * width), BF) if late else pltpu.HBM((own, width), F32)]
         out += [shape((width, width), BF)] * late
         return pl.pallas_call(
-            functools.partial(bias_kernel, late * chunks * block, late),
+            functools.partial(bias_kernel, late * 3 * block, late),
             name="bias_" + str(late),
             out_shape=out,
             in_specs=[vmem(), smem()] + hbm(8),

time: 63.6 us -> 63.7 us (level)
  no operation moved by 1% of the time
where the time goes in v11:
time: 63.7 us; the launch traced here: 62.5 us
  starting transfers between devices  21.5 us (34%)
  blocking collectives  20.4 us (32%)
  Pallas kernels  18.1 us (28%)
  waiting for transfers between devices  2.33 us (4%)
    all_to_all x1, blocking collectives, shards(): gathered = lax.all_to_all(partial, 'kcol', 0, 0)  20.4 us
    pallas_call x2, Pallas kernels, bias_of(): pl.pallas_call(functools.partial(bias_kernel, late * 3 * block, late), na...  9.18 us
    all_to_all x1, starting transfers between devices, shards(): row_tokens = lax.all_to_all(copies, 'kcol', 0, 0, axis_index_groups=near)  8.58 us
    all_to_all x1, starting transfers between devices, shards(): lax.all_to_all(turned_copies, 'qrow', 0, 0, axis_index_groups=sides)  5.71 us
    ppermute x2, starting transfers between devices, shards(): turned.append(lax.ppermute(normed, ('qrow', 'kcol'), swap))  5.34 us
    pallas_call x1, Pallas kernels, shards(): pl.pallas_call(attend_kernel, name='attend', out_shape=shape((n_col, rows...  3.97 us
    pallas_call x1, Pallas kernels, shards(): pl.pallas_call(norm_kernel, name='norm', out_shape=(shape((own, width), B...  1.84 us
    ppermute x1, starting transfers between devices, shards(): lax.ppermute(row_tokens, 'kcol', [(i, (i + n_col // 2) % n_col) for i in...  1.84 us
  transfers between devices with their start and end apart: 5, of which 3 were waited for; matrix products, arithmetic and copies ran while one was open for 0% of the time, Pallas kernels for 18%

profile of v11, /device:TPU:40, one launch (start us, length us, event | category | flops | bytes accessed | tf_op | source)
XLA Modules:
  0.0 62.5 jit_solution(5197107594867363299)
XLA Ops:
  0.0 1.8 %norm.1 = (bf16[16,768]{1,0:T(8,128)(2,1)S(1)}, bf16[8,16,768]{2,1,0:T(8,128)(2,1)}) custom-call(s32[8]{0:T(128)} %restype_hbm.1, bf16[16,768]{1,0:T(8,128)(2,1)} %bitcast.13, bf16[32,768]{1,0:T(8,128)(2,1)} %table_hbm.1, f32[768]{0:T(1024)} %gain_hbm.1), custom_call_target="tpu_custom_call" | custom-call | tf_op jit(solution)/shard_map/norm/pallas_call | solution.py:337
  1.9 8.6 %all-to-all-start = ((bf16[8,16,768]{2,1,0:T(8,128)(2,1)}), bf16[8,16,768]{2,1,0:T(8,128)(2,1)S(1)}, u32[]{:S(2)}, u32[]{:S(2)}) async-start(bf16[8,16,768]{2,1,0:T(8,128)(2,1)} %get-tuple-element.16), calls=%async_computation | async-start | bytes 393216 | tf_op jit(solution)/shard_map/all_to_all | solution.py:359
  10.4 0.0 collective-permute-start.1
  10.4 5.3 %collective-permute-start = (bf16[16,768]{1,0:T(8,128)(2,1)S(1)}, bf16[16,768]{1,0:T(8,128)(2,1)S(1)}, u32[]{:S(2)}, u32[]{:S(2)}) collective-permute-start(bf16[16,768]{1,0:T(8,128)(2,1)S(1)} %get-tuple-element.14.own_ref), channel_id=1, source_target_pairs={{15,0},{14,16},{12,32},{13,48},{10,64},{8,80},{11,96},{9,112},{5,1... | collective-permute-start | bytes 73736 | tf_op jit(solution)/shard_map/ppermute | solution.py:357
  15.8 0.1 pad_add_fusion.where_ref
  15.8 4.0 %bias_0.1 = (f32[16,48,128]{2,1,0:T(8,128)}, f32[16,768]{1,0:T(8,128)}) custom-call(bf16[16,768]{1,0:T(8,128)(2,1)S(1)} %get-tuple-element.14.own_ref, s32[2]{0:T(128)S(1)} %pad_add_fusion.where_ref, s32[2048]{0:T(1024)} %refs_0_.3, f32[16]{0:T(128)} %refs_1_.3, s32[16,128]{1,0:T(8,128)} %bitcast.9, s32[1,128]{1,0:T(1,128)} %bitcast.14, f32[1,128]{1,0:T(1,128)} %bitcast.16, ...), custom_call_target="tpu_custom_call" | custom-call | flops 500000000 | bytes 10000000 | tf_op jit(solution)/shard_map/bias_0/pallas_call | solution.py:369
  19.9 0.0 collective-permute-done.1.two_ref
  19.9 1.4 %collective-permute-done.one_ref = bf16[16,768]{1,0:T(8,128)(2,1)S(1)} collective-permute-done((bf16[16,768]{1,0:T(8,128)(2,1)S(1)}, bf16[16,768]{1,0:T(8,128)(2,1)S(1)}, u32[]{:S(2)}, u32[]{:S(2)}) %collective-permute-start) | collective-permute-done | bytes 24608 | tf_op jit(solution)/shard_map/ppermute | solution.py:357
  21.3 0.8 %copies.1 = bf16[8,32,768]{2,1,0:T(8,128)(2,1)} custom-call(bf16[16,768]{1,0:T(8,128)(2,1)S(1)} %collective-permute-done.one_ref, bf16[16,768]{1,0:T(8,128)(2,1)S(1)} %collective-permute-done.1.two_ref, f32[16,48,128]{2,1,0:T(8,128)} %get-tuple-element.15.after_ref.bias_a_hbm), custom_call_target="tpu_custom_call" | custom-call | tf_op jit(solution)/shard_map/copies/pallas_call | solution.py:408
  22.1 0.0 all-to-all-done.rows_ref
  22.1 5.7 %all-to-all-start.1 = ((bf16[8,32,768]{2,1,0:T(8,128)(2,1)}), bf16[8,32,768]{2,1,0:T(8,128)(2,1)S(1)}, u32[]{:S(2)}, u32[]{:S(2)}) async-start(bf16[8,32,768]{2,1,0:T(8,128)(2,1)} %copies.1), calls=%async_computation.1 | async-start | bytes 786432 | tf_op jit(solution)/shard_map/all_to_all | solution.py:417
  27.8 0.0 copy-start.2
  27.8 1.8 %collective-permute-start.2 = (bf16[8,16,768]{2,1,0:T(8,128)(2,1)S(1)}, bf16[8,16,768]{2,1,0:T(8,128)(2,1)S(1)}, u32[]{:S(2)}, u32[]{:S(2)}) collective-permute-start(bf16[8,16,768]{2,1,0:T(8,128)(2,1)S(1)} %all-to-all-done.rows_ref), channel_id=1, source_target_pairs={{0,8},{1,9},{2,10},{3,11},{4,12},{5,13},{6,14},{7,15},{8,0},{9,1},... | collective-permute-start | bytes 589832 | tf_op jit(solution)/shard_map/ppermute | solution.py:418
  29.7 5.2 %bias_1.1 = (f32[16,80,128]{2,1,0:T(8,128)}, bf16[768,1536]{1,0:T(8,128)(2,1)S(1)}, bf16[768,768]{1,0:T(8,128)(2,1)S(1)}) custom-call(bf16[16,768]{1,0:T(8,128)(2,1)S(1)} %get-tuple-element.14.own_ref, s32[2]{0:T(128)S(1)} %pad_add_fusion.where_ref, s32[2048]{0:T(1024)} %refs_0_.3, f32[16]{0:T(128)} %refs_1_.3, s32[16,128]{1,0:T(8,128)} %bitcast.10, ...), custom_call_target="tpu_custom_call" | custom-call | flops 500000000 | bytes 10000000 | tf_op jit(solution)/shard_map/bias_1/pallas_call | solution.py:369
  34.8 0.3 collective-permute-done.2.others_ref
  35.1 1.0 %query.1.q_ref = bf16[2,128,768]{2,1,0:T(8,128)(2,1)S(1)} custom-call(s32[2]{0:T(128)S(1)} %pad_add_fusion.where_ref, bf16[8,16,768]{2,1,0:T(8,128)(2,1)S(1)} %all-to-all-done.rows_ref, bf16[8,16,768]{2,1,0:T(8,128)(2,1)S(1)} %collective-permute-done.2.others_ref, bf16[768,768]{1,0:T(8,128)(2,1)S(1)} %get-tuple-element.20.w_ref), custom_call_target="tpu_custom_call" | custom-call | tf_op jit(solution)/shard_map/query/pallas_call | solution.py:420
  36.2 0.6 all-to-all-done.1
  36.8 0.0 copy-done.2
  36.8 0.0 copy-start.1
  36.8 4.0 %attend.1 = bf16[16,112,128]{2,1,0:T(8,128)(2,1)S(1)} custom-call(s32[2]{0:T(128)S(1)} %pad_add_fusion.where_ref, s32[512]{0:T(512)S(1)} %copy-done.2, bf16[16,16,768]{2,1,0:T(8,128)(2,1)S(1)} %bitcast.8, bf16[768,1536]{1,0:T(8,128)(2,1)S(1)} %get-tuple-element.18.wkv_ref, bf16[2,128,768]{2,1,0:T(8,128)(2,1)S(1)} %query.1.q_ref, ...), custom_call_target="tpu_custom_call" | custom-call | tf_op jit(solution)/shard_map/attend/pallas_call | solution.py:433
  40.7 20.4 %all_to_all.15.parts_ref = bf16[16,112,128]{2,1,0:T(8,128)(2,1)S(1)} all-to-all(bf16[16,112,128]{2,1,0:T(8,128)(2,1)S(1)} %attend.1), channel_id=1, replica_groups=mesh['qrow'=16,'kcol'=16] {'kcol'}, dimensions={0} | all-to-all | bytes 917504 | tf_op jit(solution)/shard_map/all_to_all | solution.py:447
  61.2 0.0 copy-done
  61.2 0.0 copy-done.1
  61.2 1.3 %merge.1 = bf16[2,8,768]{2,1,0:T(8,128)(2,1)} custom-call(bf16[16,112,128]{2,1,0:T(8,128)(2,1)S(1)} %all_to_all.15.parts_ref, f32[16,768]{1,0:T(8,128)S(1)} %copy-done.1, bf16[768,768]{1,0:T(8,128)(2,1)S(1)} %copy-done), custom_call_target="tpu_custom_call" | custom-call | tf_op jit(solution)/shard_map/merge/pallas_call | solution.py:448
  (1 shorter events, 0.0 us)
Async XLA Ops:
  1.9 20.3 %all-to-all-start = ((bf16[8,16,768]{2,1,0:T(8,128)(2,1)}), bf16[8,16,768]{2,1,0:T(8,128)(2,1)S(1)}, u32[]{:S(2)}, u32[]{:S(2)}) async-start(bf16[8,16,768]{2,1,0:T(8,128)(2,1)} %get-tuple-element.16), calls=%async_computation | async-start | bytes 393216 | tf_op jit(solution)/shard_map/all_to_all | solution.py:359
  10.4 9.5 %collective-permute-start.1 = (bf16[16,768]{1,0:T(8,128)(2,1)S(1)}, bf16[16,768]{1,0:T(8,128)(2,1)S(1)}, u32[]{:S(2)}, u32[]{:S(2)}) collective-permute-start(bf16[16,768]{1,0:T(8,128)(2,1)S(1)} %get-tuple-element.14.own_ref), channel_id=1, source_target_pairs={{13,0},{12,16},{4,32},{15,48},{11,64},{9,80},{5,96},{14,112},{7,12... | collective-permute-start | bytes 73736 | tf_op jit(solution)/shard_map/ppermute | solution.py:357
  10.4 10.9 %collective-permute-start = (bf16[16,768]{1,0:T(8,128)(2,1)S(1)}, bf16[16,768]{1,0:T(8,128)(2,1)S(1)}, u32[]{:S(2)}, u32[]{:S(2)}) collective-permute-start(bf16[16,768]{1,0:T(8,128)(2,1)S(1)} %get-tuple-element.14.own_ref), channel_id=1, source_target_pairs={{15,0},{14,16},{12,32},{13,48},{10,64},{8,80},{11,96},{9,112},{5,1... | collective-permute-start | bytes 73736 | tf_op jit(solution)/shard_map/ppermute | solution.py:357
  22.1 14.7 %all-to-all-start.1 = ((bf16[8,32,768]{2,1,0:T(8,128)(2,1)}), bf16[8,32,768]{2,1,0:T(8,128)(2,1)S(1)}, u32[]{:S(2)}, u32[]{:S(2)}) async-start(bf16[8,32,768]{2,1,0:T(8,128)(2,1)} %copies.1), calls=%async_computation.1 | async-start | bytes 786432 | tf_op jit(solution)/shard_map/all_to_all | solution.py:417
  27.8 8.9 %copy-start.2 = (s32[512]{0:T(512)S(1)}, s32[512]{0:T(512)}, u32[]{:S(2)}) copy-start(s32[512]{0:T(512)} %constant.9.clone.order_ref) | copy-start | bytes 6148
  27.8 7.3 %collective-permute-start.2 = (bf16[8,16,768]{2,1,0:T(8,128)(2,1)S(1)}, bf16[8,16,768]{2,1,0:T(8,128)(2,1)S(1)}, u32[]{:S(2)}, u32[]{:S(2)}) collective-permute-start(bf16[8,16,768]{2,1,0:T(8,128)(2,1)S(1)} %all-to-all-done.rows_ref), channel_id=1, source_target_pairs={{0,8},{1,9},{2,10},{3,11},{4,12},{5,13},{6,14},{7,15},{8,0},{9,1},... | collective-permute-start | bytes 589832 | tf_op jit(solution)/shard_map/ppermute | solution.py:418
  36.8 24.4 %copy-start = (bf16[768,768]{1,0:T(8,128)(2,1)S(1)}, bf16[768,768]{1,0:T(8,128)(2,1)}, u32[]{:S(2)}) copy-start(bf16[768,768]{1,0:T(8,128)(2,1)} %wout_ref.1) | copy-start | bytes 3538948
  36.8 24.4 %copy-start.1 = (f32[16,768]{1,0:T(8,128)S(1)}, f32[16,768]{1,0:T(8,128)}, u32[]{:S(2)}) copy-start(f32[16,768]{1,0:T(8,128)} %get-tuple-element.22.gate_ref) | copy-start | bytes 147460

commit v12 on v10

--- a/solution.py
+++ b/solution.py
@@ -124,7 +124,7 @@
     alive = jnp.broadcast_to(live_ref[...] == 1, (heads, keys))
     for i in range(chunks):
         loads[i].wait()
-        if i == 0:
+        if i == 1:
             for load in load_w:
                 load.start()
         for q in range(0, block, 2):

time: 63.6 us -> 63.7 us (level)
  transfers between devices with their start and end apart: 5 -> 5, of which waited for: 3 -> 3; matrix products, arithmetic and copies ran while one was open for 0% -> 0% of each run, Pallas kernels for 18% -> 19%
where the time goes in v12:
time: 63.7 us; the launch traced here: 62.5 us
  starting transfers between devices  21.5 us (34%)
  blocking collectives  20.4 us (32%)
  Pallas kernels  18.8 us (30%)
  waiting for transfers between devices  1.63 us (3%)
    all_to_all x1, blocking collectives, shards(): gathered = lax.all_to_all(partial, 'kcol', 0, 0)  20.4 us
    pallas_call x2, Pallas kernels, bias_of(): pl.pallas_call(functools.partial(bias_kernel, late * chunks * block, late...  9.89 us
    all_to_all x1, starting transfers between devices, shards(): row_tokens = lax.all_to_all(copies, 'kcol', 0, 0, axis_index_groups=near)  8.58 us
    all_to_all x1, starting transfers between devices, shards(): lax.all_to_all(turned_copies, 'qrow', 0, 0, axis_index_groups=sides)  5.71 us
    ppermute x2, starting transfers between devices, shards(): turned.append(lax.ppermute(normed, ('qrow', 'kcol'), swap))  5.34 us
    pallas_call x1, Pallas kernels, shards(): pl.pallas_call(attend_kernel, name='attend', out_shape=shape((n_col, rows...  3.97 us
    pallas_call x1, Pallas kernels, shards(): pl.pallas_call(norm_kernel, name='norm', out_shape=(shape((own, width), B...  1.85 us
    ppermute x1, starting transfers between devices, shards(): lax.ppermute(row_tokens, 'kcol', [(i, (i + n_col // 2) % n_col) for i in...  1.84 us
  transfers between devices with their start and end apart: 5, of which 3 were waited for; matrix products, arithmetic and copies ran while one was open for 0% of the time, Pallas kernels for 19%

profile of v12, /device:TPU:40, one launch (start us, length us, event | category | flops | bytes accessed | tf_op | source)
XLA Modules:
  0.0 62.5 jit_solution(4286334830302347488)
XLA Ops:
  0.0 1.8 %norm.1 = (bf16[16,768]{1,0:T(8,128)(2,1)S(1)}, bf16[8,16,768]{2,1,0:T(8,128)(2,1)}) custom-call(s32[8]{0:T(128)} %restype_hbm.1, bf16[16,768]{1,0:T(8,128)(2,1)} %bitcast.13, bf16[32,768]{1,0:T(8,128)(2,1)} %table_hbm.1, f32[768]{0:T(1024)} %gain_hbm.1), custom_call_target="tpu_custom_call" | custom-call | tf_op jit(solution)/shard_map/norm/pallas_call | solution.py:337
  1.9 8.6 %all-to-all-start = ((bf16[8,16,768]{2,1,0:T(8,128)(2,1)}), bf16[8,16,768]{2,1,0:T(8,128)(2,1)S(1)}, u32[]{:S(2)}, u32[]{:S(2)}) async-start(bf16[8,16,768]{2,1,0:T(8,128)(2,1)} %get-tuple-element.16), calls=%async_computation | async-start | bytes 393216 | tf_op jit(solution)/shard_map/all_to_all | solution.py:359
  10.4 0.0 collective-permute-start.1
  10.4 5.3 %collective-permute-start = (bf16[16,768]{1,0:T(8,128)(2,1)S(1)}, bf16[16,768]{1,0:T(8,128)(2,1)S(1)}, u32[]{:S(2)}, u32[]{:S(2)}) collective-permute-start(bf16[16,768]{1,0:T(8,128)(2,1)S(1)} %get-tuple-element.14.own_ref), channel_id=1, source_target_pairs={{15,0},{14,16},{12,32},{13,48},{10,64},{8,80},{11,96},{9,112},{5,1... | collective-permute-start | bytes 73736 | tf_op jit(solution)/shard_map/ppermute | solution.py:357
  15.8 0.1 pad_add_fusion.where_ref
  15.9 4.7 %bias_0.1 = (f32[16,64,128]{2,1,0:T(8,128)}, f32[16,768]{1,0:T(8,128)}) custom-call(bf16[16,768]{1,0:T(8,128)(2,1)S(1)} %get-tuple-element.14.own_ref, s32[2]{0:T(128)S(1)} %pad_add_fusion.where_ref, s32[2048]{0:T(1024)} %refs_0_.3, f32[16]{0:T(128)} %refs_1_.3, s32[16,128]{1,0:T(8,128)} %bitcast.9, s32[1,128]{1,0:T(1,128)} %bitcast.14, f32[1,128]{1,0:T(1,128)} %bitcast.16, ...), custom_call_target="tpu_custom_call" | custom-call | flops 500000000 | bytes 10000000 | tf_op jit(solution)/shard_map/bias_0/pallas_call | solution.py:369
  20.5 0.0 collective-permute-done.1.two_ref
  20.5 0.8 %collective-permute-done.one_ref = bf16[16,768]{1,0:T(8,128)(2,1)S(1)} collective-permute-done((bf16[16,768]{1,0:T(8,128)(2,1)S(1)}, bf16[16,768]{1,0:T(8,128)(2,1)S(1)}, u32[]{:S(2)}, u32[]{:S(2)}) %collective-permute-start) | collective-permute-done | bytes 24608 | tf_op jit(solution)/shard_map/ppermute | solution.py:357
  21.3 0.8 %copies.1 = bf16[8,32,768]{2,1,0:T(8,128)(2,1)} custom-call(bf16[16,768]{1,0:T(8,128)(2,1)S(1)} %collective-permute-done.one_ref, bf16[16,768]{1,0:T(8,128)(2,1)S(1)} %collective-permute-done.1.two_ref, f32[16,64,128]{2,1,0:T(8,128)} %get-tuple-element.15.after_ref.bias_a_hbm), custom_call_target="tpu_custom_call" | custom-call | tf_op jit(solution)/shard_map/copies/pallas_call | solution.py:408
  22.1 0.0 all-to-all-done.rows_ref
  22.1 5.7 %all-to-all-start.1 = ((bf16[8,32,768]{2,1,0:T(8,128)(2,1)}), bf16[8,32,768]{2,1,0:T(8,128)(2,1)S(1)}, u32[]{:S(2)}, u32[]{:S(2)}) async-start(bf16[8,32,768]{2,1,0:T(8,128)(2,1)} %copies.1), calls=%async_computation.1 | async-start | bytes 786432 | tf_op jit(solution)/shard_map/all_to_all | solution.py:417
  27.8 0.0 copy-start.2
  27.8 1.8 %collective-permute-start.2 = (bf16[8,16,768]{2,1,0:T(8,128)(2,1)S(1)}, bf16[8,16,768]{2,1,0:T(8,128)(2,1)S(1)}, u32[]{:S(2)}, u32[]{:S(2)}) collective-permute-start(bf16[8,16,768]{2,1,0:T(8,128)(2,1)S(1)} %all-to-all-done.rows_ref), channel_id=1, source_target_pairs={{0,8},{1,9},{2,10},{3,11},{4,12},{5,13},{6,14},{7,15},{8,0},{9,1},... | collective-permute-start | bytes 589832 | tf_op jit(solution)/shard_map/ppermute | solution.py:418
  29.7 5.2 %bias_1.1 = (f32[16,64,128]{2,1,0:T(8,128)}, bf16[768,1536]{1,0:T(8,128)(2,1)S(1)}, bf16[768,768]{1,0:T(8,128)(2,1)S(1)}) custom-call(bf16[16,768]{1,0:T(8,128)(2,1)S(1)} %get-tuple-element.14.own_ref, s32[2]{0:T(128)S(1)} %pad_add_fusion.where_ref, s32[2048]{0:T(1024)} %refs_0_.3, f32[16]{0:T(128)} %refs_1_.3, s32[16,128]{1,0:T(8,128)} %bitcast.10, ...), custom_call_target="tpu_custom_call" | custom-call | flops 500000000 | bytes 10000000 | tf_op jit(solution)/shard_map/bias_1/pallas_call | solution.py:369
  34.9 0.2 collective-permute-done.2.others_ref
  35.2 1.0 %query.1.q_ref = bf16[2,128,768]{2,1,0:T(8,128)(2,1)S(1)} custom-call(s32[2]{0:T(128)S(1)} %pad_add_fusion.where_ref, bf16[8,16,768]{2,1,0:T(8,128)(2,1)S(1)} %all-to-all-done.rows_ref, bf16[8,16,768]{2,1,0:T(8,128)(2,1)S(1)} %collective-permute-done.2.others_ref, bf16[768,768]{1,0:T(8,128)(2,1)S(1)} %get-tuple-element.20.w_ref), custom_call_target="tpu_custom_call" | custom-call | tf_op jit(solution)/shard_map/query/pallas_call | solution.py:420
  36.2 0.6 all-to-all-done.1
  36.8 0.0 copy-done.2
  36.8 0.0 copy-start
  36.8 4.0 %attend.1 = bf16[16,112,128]{2,1,0:T(8,128)(2,1)S(1)} custom-call(s32[2]{0:T(128)S(1)} %pad_add_fusion.where_ref, s32[512]{0:T(512)S(1)} %copy-done.2, bf16[16,16,768]{2,1,0:T(8,128)(2,1)S(1)} %bitcast.8, bf16[768,1536]{1,0:T(8,128)(2,1)S(1)} %get-tuple-element.18.wkv_ref, bf16[2,128,768]{2,1,0:T(8,128)(2,1)S(1)} %query.1.q_ref, ...), custom_call_target="tpu_custom_call" | custom-call | tf_op jit(solution)/shard_map/attend/pallas_call | solution.py:433
  40.7 20.4 %all_to_all.15.parts_ref = bf16[16,112,128]{2,1,0:T(8,128)(2,1)S(1)} all-to-all(bf16[16,112,128]{2,1,0:T(8,128)(2,1)S(1)} %attend.1), channel_id=1, replica_groups=mesh['qrow'=16,'kcol'=16] {'kcol'}, dimensions={0} | all-to-all | bytes 917504 | tf_op jit(solution)/shard_map/all_to_all | solution.py:447
  61.2 0.0 copy-done
  61.2 0.0 copy-done.1
  61.2 1.3 %merge.1 = bf16[2,8,768]{2,1,0:T(8,128)(2,1)} custom-call(bf16[16,112,128]{2,1,0:T(8,128)(2,1)S(1)} %all_to_all.15.parts_ref, f32[16,768]{1,0:T(8,128)S(1)} %copy-done.1, bf16[768,768]{1,0:T(8,128)(2,1)S(1)} %copy-done), custom_call_target="tpu_custom_call" | custom-call | tf_op jit(solution)/shard_map/merge/pallas_call | solution.py:448
  (1 shorter events, 0.0 us)
Async XLA Ops:
  1.9 20.3 %all-to-all-start = ((bf16[8,16,768]{2,1,0:T(8,128)(2,1)}), bf16[8,16,768]{2,1,0:T(8,128)(2,1)S(1)}, u32[]{:S(2)}, u32[]{:S(2)}) async-start(bf16[8,16,768]{2,1,0:T(8,128)(2,1)} %get-tuple-element.16), calls=%async_computation | async-start | bytes 393216 | tf_op jit(solution)/shard_map/all_to_all | solution.py:359
  10.4 10.1 %collective-permute-start.1 = (bf16[16,768]{1,0:T(8,128)(2,1)S(1)}, bf16[16,768]{1,0:T(8,128)(2,1)S(1)}, u32[]{:S(2)}, u32[]{:S(2)}) collective-permute-start(bf16[16,768]{1,0:T(8,128)(2,1)S(1)} %get-tuple-element.14.own_ref), channel_id=1, source_target_pairs={{13,0},{12,16},{4,32},{15,48},{11,64},{9,80},{5,96},{14,112},{7,12... | collective-permute-start | bytes 73736 | tf_op jit(solution)/shard_map/ppermute | solution.py:357
  10.4 10.9 %collective-permute-start = (bf16[16,768]{1,0:T(8,128)(2,1)S(1)}, bf16[16,768]{1,0:T(8,128)(2,1)S(1)}, u32[]{:S(2)}, u32[]{:S(2)}) collective-permute-start(bf16[16,768]{1,0:T(8,128)(2,1)S(1)} %get-tuple-element.14.own_ref), channel_id=1, source_target_pairs={{15,0},{14,16},{12,32},{13,48},{10,64},{8,80},{11,96},{9,112},{5,1... | collective-permute-start | bytes 73736 | tf_op jit(solution)/shard_map/ppermute | solution.py:357
  22.1 14.7 %all-to-all-start.1 = ((bf16[8,32,768]{2,1,0:T(8,128)(2,1)}), bf16[8,32,768]{2,1,0:T(8,128)(2,1)S(1)}, u32[]{:S(2)}, u32[]{:S(2)}) async-start(bf16[8,32,768]{2,1,0:T(8,128)(2,1)} %copies.1), calls=%async_computation.1 | async-start | bytes 786432 | tf_op jit(solution)/shard_map/all_to_all | solution.py:417
  27.8 8.9 %copy-start.2 = (s32[512]{0:T(512)S(1)}, s32[512]{0:T(512)}, u32[]{:S(2)}) copy-start(s32[512]{0:T(512)} %constant.9.clone.order_ref) | copy-start | bytes 6148
  27.8 7.3 %collective-permute-start.2 = (bf16[8,16,768]{2,1,0:T(8,128)(2,1)S(1)}, bf16[8,16,768]{2,1,0:T(8,128)(2,1)S(1)}, u32[]{:S(2)}, u32[]{:S(2)}) collective-permute-start(bf16[8,16,768]{2,1,0:T(8,128)(2,1)S(1)} %all-to-all-done.rows_ref), channel_id=1, source_target_pairs={{0,8},{1,9},{2,10},{3,11},{4,12},{5,13},{6,14},{7,15},{8,0},{9,1},... | collective-permute-start | bytes 589832 | tf_op jit(solution)/shard_map/ppermute | solution.py:418
  36.8 24.4 %copy-start = (bf16[768,768]{1,0:T(8,128)(2,1)S(1)}, bf16[768,768]{1,0:T(8,128)(2,1)}, u32[]{:S(2)}) copy-start(bf16[768,768]{1,0:T(8,128)(2,1)} %wout_ref.1) | copy-start | bytes 3538948
  36.8 24.4 %copy-start.1 = (f32[16,768]{1,0:T(8,128)S(1)}, f32[16,768]{1,0:T(8,128)}, u32[]{:S(2)}) copy-start(f32[16,768]{1,0:T(8,128)} %get-tuple-element.22.gate_ref) | copy-start | bytes 147460
